TPU v7x, 32 devices: a whole 2x2x4 slice. The times are simulated.
32 devices in a mesh: dp: 8 (over y, x, core), mp: 4 (over z).
Axes of the slice: x: 2, y: 2, z: 4, core: 2. Of those that a mesh axis runs over, the one named last changes fastest.
Arguments:
- tokens: bfloat16 [8192, 2048], P('dp', 'mp'), may hold values from -79.19596 to 79.19596
- seq_lengths: int32 [8, 3], P('dp'), may hold values from 1 to 640, 1024 in all within a row
- gain_first: bfloat16 [2048], replicated, may hold values from 0.5 to 1.5
- lin_query: bfloat16 [2048, 256], P(None, 'mp'), may hold values from -0.125 to 0.125
- lin_key: bfloat16 [2048, 256], P(None, 'mp'), may hold values from -0.125 to 0.125
- lin_value: bfloat16 [2048, 2048], P(None, 'mp'), may hold values from -0.125 to 0.125
- lin_out: bfloat16 [2048, 2048], P('mp'), may hold values from -3 to 3
- gain_second: bfloat16 [2048], replicated, may hold values from 0.5 to 1.5
- win_query: bfloat16 [2048, 2048], P(None, 'mp'), may hold values from -0.125 to 0.125
- win_key: bfloat16 [2048, 2048], P(None, 'mp'), may hold values from -0.125 to 0.125
- win_value: bfloat16 [2048, 2048], P(None, 'mp'), may hold values from -0.125 to 0.125
- win_out: bfloat16 [2048, 2048], P('mp'), may hold values from -0.75 to 0.75
- gain_third: bfloat16 [2048], replicated, may hold values from 0.5 to 1.5
- gate_weight: bfloat16 [2048, 5632], P(None, 'mp'), may hold values from -0.125 to 0.125
- up_weight: bfloat16 [2048, 5632], P(None, 'mp'), may hold values from -0.125 to 0.125
- down_weight: bfloat16 [5632, 2048], P('mp'), may hold values from -0.078125 to 0.078125
- out_cotangent: bfloat16 [8192, 2048], P('dp', 'mp'), may hold values from -6 to 6
Outputs:
- block_out: bfloat16 [8192, 2048], P('dp', 'mp')
- tokens_grad: float32 [8192, 2048], P('dp', 'mp')
- gain_first_grad: float32 [2048], P('mp')
- lin_query_grad: float32 [2048, 256], P(None, 'mp')
- lin_key_grad: float32 [2048, 256], P(None, 'mp')
- lin_value_grad: float32 [2048, 2048], P(None, 'mp')
- lin_out_grad: float32 [2048, 2048], P('mp')
- gain_second_grad: float32 [2048], P('mp')
- win_query_grad: float32 [2048, 2048], P(None, 'mp')
- win_key_grad: float32 [2048, 2048], P(None, 'mp')
- win_value_grad: float32 [2048, 2048], P(None, 'mp')
- win_out_grad: float32 [2048, 2048], P('mp')
- gain_third_grad: float32 [2048], P('mp')
- gate_weight_grad: float32 [2048, 5632], P(None, 'mp')
- up_weight_grad: float32 [2048, 5632], P(None, 'mp')
- down_weight_grad: float32 [5632, 2048], P('mp')
- rms_values: float32 [5], replicated
Inputs may be any that keep to these rules, and one draw needn't show every extreme that they name: `seq_lengths`: for each group of 1024 slots: the length of its first sequence, of its second sequence and of its trailing padding, in that order; the three sum to 1024, and the largest of them is exactly five eighths of 1024, rounded down.
All inputs are finite; a program needn't handle non-finite values.
Results may differ from a plain program's by a relative error of at most 0.018.
Values may be sent and summed in bfloat16 or wider, within the bound.
No kernel may reach another device: no remote copies, remote signals or barrier semaphores. Data moves between devices by JAX's collectives and lax.ppermute only.
A program may use at most 320 MiB of HBM per device.

v0:
```python
import jax
import jax.numpy as jnp
from jax import lax
from jax.sharding import PartitionSpec as P

FEATURE_SIZE = 16
HEAD_DIM = 128
WINDOW = 64


EPSILON = 1e-05
NEGATIVE = -1e30


def segment_info(lengths, row_count):
    positions = jnp.arange(row_count, dtype=jnp.int32)
    first_end = lengths[0, 0]
    second_end = lengths[0, 0] + lengths[0, 1]
    segments = (positions >= first_end).astype(jnp.int32) + (positions >= second_end).astype(
        jnp.int32
    )
    validity = (positions < second_end).astype(jnp.float32)
    return (segments, validity)


def times_transposed(left_side, right_side):
    return lax.dot_general(
        left_side, right_side, (((1,), (1,)), ((), ())), preferred_element_type=jnp.float32
    )


def transposed_times(left_side, right_side):
    return lax.dot_general(
        left_side, right_side, (((0,), (0,)), ((), ())), preferred_element_type=jnp.float32
    )


def gather_stream(shard_part):
    return lax.all_gather(shard_part, "mp", axis=1, tiled=True)


def branch_total(partial_value):
    return lax.psum_scatter(partial_value, "mp", scatter_dimension=1, tiled=True)


def gather_cotangent(shard_part):
    return lax.all_gather(shard_part, "mp", axis=1, tiled=True)


def rms_forward(full_stream, gain_vector):
    inverse = lax.rsqrt(jnp.mean(full_stream * full_stream, axis=1) + EPSILON)
    normed = (full_stream * inverse[:, None] * gain_vector.astype(jnp.float32)).astype(jnp.bfloat16)
    return (normed, inverse)


def norm_backward(partial_value, resid_part, inverse, gain_part, model_width, carried):
    shard_grad = lax.psum_scatter(partial_value, "mp", scatter_dimension=1, tiled=True)
    scaled = shard_grad * gain_part
    normed_part = resid_part * inverse[:, None]
    row_dot = lax.psum(jnp.sum(scaled * normed_part, axis=1), "mp")
    input_grad = carried + inverse[:, None] * (
        scaled - normed_part * (row_dot / model_width)[:, None]
    )
    gain_grad = jnp.sum(shard_grad * normed_part, axis=0)
    return (input_grad, gain_grad)


def linear_scores(query_tile_rows, key_rows_matrix, segments, begin_row, score_scale):
    block_rows = query_tile_rows.shape[0]
    attention_logits = (
        jnp.einsum(
            "uao,sao->aus", query_tile_rows, key_rows_matrix, preferred_element_type=jnp.float32
        )
        * score_scale
    )
    query_place = begin_row + jnp.arange(block_rows, dtype=jnp.int32)
    key_place = jnp.arange(key_rows_matrix.shape[0], dtype=jnp.int32)
    query_segment = lax.dynamic_slice_in_dim(segments, begin_row, block_rows)
    allowed = (key_place[None, :] <= query_place[:, None]) & (
        segments[None, :] == query_segment[:, None]
    )
    kernel = jnp.where(
        allowed[None], 1.0 + attention_logits + 0.5 * attention_logits * attention_logits, 0.0
    )
    return (attention_logits, allowed, kernel)


def linear_forward(queries, key_rows_matrix, value_vectors, segments, block_rows, score_scale):
    row_count = queries.shape[0]

    def one_block(begin_row):
        query_tile_rows = lax.dynamic_slice_in_dim(queries, begin_row, block_rows)
        attention_logits, allowed, kernel = linear_scores(
            query_tile_rows, key_rows_matrix, segments, begin_row, score_scale
        )
        totals = jnp.sum(kernel, axis=2)
        numerator = jnp.einsum(
            "hqk,khd->qhd",
            kernel.astype(jnp.bfloat16),
            value_vectors,
            preferred_element_type=jnp.float32,
        )
        return (numerator / jnp.transpose(totals)[:, :, None]).astype(jnp.bfloat16)

    starts = jnp.arange(row_count // block_rows, dtype=jnp.int32) * block_rows
    return lax.map(one_block, starts).reshape(row_count, -1)


def linear_backward(
    queries, key_rows_matrix, value_vectors, segments, out_grad, block_rows, score_scale
):
    row_count = queries.shape[0]

    def one_block(running, begin_row):
        key_total, value_total = running
        query_tile_rows = lax.dynamic_slice_in_dim(queries, begin_row, block_rows)
        grad_block = lax.dynamic_slice_in_dim(out_grad, begin_row, block_rows)
        attention_logits, allowed, kernel = linear_scores(
            query_tile_rows, key_rows_matrix, segments, begin_row, score_scale
        )
        totals = jnp.transpose(jnp.sum(kernel, axis=2))
        kernel_low = kernel.astype(jnp.bfloat16)
        numerator = jnp.einsum(
            "hqk,khd->qhd", kernel_low, value_vectors, preferred_element_type=jnp.float32
        )
        numer_grad = (grad_block / totals[:, :, None]).astype(jnp.bfloat16)
        total_grad = -jnp.sum(grad_block * numerator, axis=2) / (totals * totals)
        kernel_grad = (
            jnp.einsum(
                "qhd,khd->hqk", numer_grad, value_vectors, preferred_element_type=jnp.float32
            )
            + jnp.transpose(total_grad)[:, :, None]
        )
        kernel_grad = jnp.where(allowed[None], kernel_grad, 0.0)
        scores_gradient = (kernel_grad * (1.0 + attention_logits)).astype(jnp.bfloat16)
        value_total = value_total + jnp.einsum(
            "hqk,qhd->khd", kernel_low, numer_grad, preferred_element_type=jnp.float32
        )
        key_total = (
            key_total
            + jnp.einsum(
                "pco,cpu->opu", scores_gradient, query_tile_rows, preferred_element_type=jnp.float32
            )
            * score_scale
        )
        query_grad = (
            jnp.einsum(
                "mwb,bmx->wmx", scores_gradient, key_rows_matrix, preferred_element_type=jnp.float32
            )
            * score_scale
        )
        return ((key_total, value_total), query_grad)

    initial = (
        jnp.zeros(key_rows_matrix.shape, jnp.float32),
        jnp.zeros(value_vectors.shape, jnp.float32),
    )
    starts = jnp.arange(row_count // block_rows, dtype=jnp.int32) * block_rows
    (key_total, value_total), query_grads = lax.scan(one_block, initial, starts)
    return (query_grads.reshape(queries.shape), key_total, value_total)


def pad_front(values, window_rows):
    return jnp.concatenate(
        [jnp.zeros((window_rows,) + values.shape[1:], values.dtype), values], axis=0
    )


def window_scores(
    query_tile_rows, key_block, padded_segments, segments, begin_row, window_rows, score_scale
):
    block_rows = query_tile_rows.shape[0]
    query_segment = lax.dynamic_slice_in_dim(segments, begin_row, block_rows)
    key_segment = lax.dynamic_slice_in_dim(padded_segments, begin_row, block_rows + window_rows)
    query_place = begin_row + jnp.arange(block_rows, dtype=jnp.int32)
    key_place = begin_row - window_rows + jnp.arange(block_rows + window_rows, dtype=jnp.int32)
    allowed = (
        (key_place[None, :] <= query_place[:, None])
        & (key_place[None, :] > query_place[:, None] - window_rows)
        & (key_segment[None, :] == query_segment[:, None])
    )
    attention_logits = (
        jnp.einsum("qhd,khd->hqk", query_tile_rows, key_block, preferred_element_type=jnp.float32)
        * score_scale
    )
    return jnp.where(allowed[None], attention_logits, NEGATIVE)


def window_forward(
    queries, key_rows_matrix, value_vectors, segments, block_rows, window_rows, score_scale
):
    row_count = queries.shape[0]
    padded_keys = pad_front(key_rows_matrix, window_rows)
    padded_values = pad_front(value_vectors, window_rows)
    padded_segments = jnp.concatenate([jnp.full((window_rows,), -1, jnp.int32), segments])

    def one_block(begin_row):
        query_tile_rows = lax.dynamic_slice_in_dim(queries, begin_row, block_rows)
        key_block = lax.dynamic_slice_in_dim(padded_keys, begin_row, block_rows + window_rows)
        value_block = lax.dynamic_slice_in_dim(padded_values, begin_row, block_rows + window_rows)
        masked = window_scores(
            query_tile_rows,
            key_block,
            padded_segments,
            segments,
            begin_row,
            window_rows,
            score_scale,
        )
        row_max = jnp.max(masked, axis=2)
        exponent = jnp.exp(masked - row_max[:, :, None])
        totals = jnp.sum(exponent, axis=2)
        weights = exponent / totals[:, :, None]
        mixed = jnp.einsum(
            "hqk,khd->qhd",
            weights.astype(jnp.bfloat16),
            value_block,
            preferred_element_type=jnp.float32,
        )
        return (mixed.astype(jnp.bfloat16), row_max + jnp.log(totals))

    starts = jnp.arange(row_count // block_rows, dtype=jnp.int32) * block_rows
    mixed, log_totals = lax.map(one_block, starts)
    return (mixed.reshape(row_count, -1), log_totals)


def window_backward(
    queries,
    key_rows_matrix,
    value_vectors,
    segments,
    log_totals,
    out_grad,
    block_rows,
    window_rows,
    score_scale,
):
    row_count = queries.shape[0]
    padded_keys = pad_front(key_rows_matrix, window_rows)
    padded_values = pad_front(value_vectors, window_rows)
    padded_segments = jnp.concatenate([jnp.full((window_rows,), -1, jnp.int32), segments])

    def one_block(running, inputs):
        key_total, value_total = running
        begin_row, log_block = inputs
        query_tile_rows = lax.dynamic_slice_in_dim(queries, begin_row, block_rows)
        grad_block = lax.dynamic_slice_in_dim(out_grad, begin_row, block_rows)
        key_block = lax.dynamic_slice_in_dim(padded_keys, begin_row, block_rows + window_rows)
        value_block = lax.dynamic_slice_in_dim(padded_values, begin_row, block_rows + window_rows)
        masked = window_scores(
            query_tile_rows,
            key_block,
            padded_segments,
            segments,
            begin_row,
            window_rows,
            score_scale,
        )
        weights = jnp.exp(masked - log_block[:, :, None])
        weight_grad = jnp.einsum(
            "qhd,khd->hqk", grad_block, value_block, preferred_element_type=jnp.float32
        )
        row_delta = jnp.sum(weights * weight_grad, axis=2)
        scores_gradient = (weights * (weight_grad - row_delta[:, :, None])).astype(jnp.bfloat16)
        query_grad = (
            jnp.einsum(
                "hqk,khd->qhd", scores_gradient, key_block, preferred_element_type=jnp.float32
            )
            * score_scale
        )
        key_part = (
            jnp.einsum(
                "hqk,qhd->khd", scores_gradient, query_tile_rows, preferred_element_type=jnp.float32
            )
            * score_scale
        )
        value_part = jnp.einsum(
            "hqk,qhd->khd",
            weights.astype(jnp.bfloat16),
            grad_block,
            preferred_element_type=jnp.float32,
        )
        span = block_rows + window_rows
        key_total = lax.dynamic_update_slice_in_dim(
            key_total, lax.dynamic_slice_in_dim(key_total, begin_row, span) + key_part, begin_row, 0
        )
        value_total = lax.dynamic_update_slice_in_dim(
            value_total,
            lax.dynamic_slice_in_dim(value_total, begin_row, span) + value_part,
            begin_row,
            0,
        )
        return ((key_total, value_total), query_grad)

    padded_shape = (row_count + window_rows,) + key_rows_matrix.shape[1:]
    initial = (jnp.zeros(padded_shape, jnp.float32), jnp.zeros(padded_shape, jnp.float32))
    starts = jnp.arange(row_count // block_rows, dtype=jnp.int32) * block_rows
    (key_total, value_total), query_grads = lax.scan(one_block, initial, (starts, log_totals))
    return (query_grads.reshape(queries.shape), key_total[window_rows:], value_total[window_rows:])


def per_device(
    tokens,
    seq_lengths,
    gain_first,
    lin_query,
    lin_key,
    lin_value,
    lin_out,
    gain_second,
    win_query,
    win_key,
    win_value,
    win_out,
    gain_third,
    gate_weight,
    up_weight,
    down_weight,
    out_cotangent,
):
    row_count, shard_width = tokens.shape
    model_width = shard_width * lax.axis_size("mp")
    block_rows = min(512, row_count)
    heads_here = lin_query.shape[1] // FEATURE_SIZE
    offset = lax.axis_index("mp") * shard_width
    segments, validity = segment_info(seq_lengths, row_count)
    lin_scale = FEATURE_SIZE ** (-0.5)
    win_scale = HEAD_DIM ** (-0.5)
    resid_zero = tokens.astype(jnp.float32)
    stream_zero = gather_stream(resid_zero)
    normed_first, inverse_first = rms_forward(stream_zero, gain_first)
    lin_q = (
        jnp.dot(normed_first, lin_query, preferred_element_type=jnp.float32)
        .astype(jnp.bfloat16)
        .reshape(row_count, heads_here, FEATURE_SIZE)
    )
    lin_k = (
        jnp.dot(normed_first, lin_key, preferred_element_type=jnp.float32)
        .astype(jnp.bfloat16)
        .reshape(row_count, heads_here, FEATURE_SIZE)
    )
    lin_v = (
        jnp.dot(normed_first, lin_value, preferred_element_type=jnp.float32)
        .astype(jnp.bfloat16)
        .reshape(row_count, heads_here, HEAD_DIM)
    )
    lin_mixed = linear_forward(lin_q, lin_k, lin_v, segments, block_rows, lin_scale)
    branch_first = branch_total(jnp.dot(lin_mixed, lin_out, preferred_element_type=jnp.float32))
    resid_one = resid_zero + branch_first
    stream_one = gather_stream(resid_one)
    normed_second, inverse_second = rms_forward(stream_one, gain_second)
    win_q = (
        jnp.dot(normed_second, win_query, preferred_element_type=jnp.float32)
        .astype(jnp.bfloat16)
        .reshape(row_count, heads_here, HEAD_DIM)
    )
    win_k = (
        jnp.dot(normed_second, win_key, preferred_element_type=jnp.float32)
        .astype(jnp.bfloat16)
        .reshape(row_count, heads_here, HEAD_DIM)
    )
    win_v = (
        jnp.dot(normed_second, win_value, preferred_element_type=jnp.float32)
        .astype(jnp.bfloat16)
        .reshape(row_count, heads_here, HEAD_DIM)
    )
    win_mixed, log_totals = window_forward(
        win_q, win_k, win_v, segments, block_rows, WINDOW, win_scale
    )
    branch_second = branch_total(jnp.dot(win_mixed, win_out, preferred_element_type=jnp.float32))
    resid_two = resid_one + branch_second
    stream_two = gather_stream(resid_two)
    normed_third, inverse_third = rms_forward(stream_two, gain_third)
    gate_values = jnp.dot(normed_third, gate_weight, preferred_element_type=jnp.float32)
    upper_values = jnp.dot(normed_third, up_weight, preferred_element_type=jnp.float32)
    sigma = jax.nn.sigmoid(gate_values)
    hidden = (gate_values * sigma * upper_values).astype(jnp.bfloat16)
    branch_third = branch_total(jnp.dot(hidden, down_weight, preferred_element_type=jnp.float32))
    output_resid = resid_two + branch_third
    cot_shard = out_cotangent.astype(jnp.float32) * validity[:, None]
    cot_third = gather_cotangent(cot_shard.astype(jnp.bfloat16))
    grad_down = transposed_times(hidden, cot_third)
    hidden_grad = times_transposed(cot_third, down_weight)
    gate_grad = (hidden_grad * upper_values * sigma * (1.0 + gate_values * (1.0 - sigma))).astype(
        jnp.bfloat16
    )
    upper_grad = (hidden_grad * gate_values * sigma).astype(jnp.bfloat16)
    grad_gate = transposed_times(normed_third, gate_grad)
    grad_upper = transposed_times(normed_third, upper_grad)
    normed_third_grad = times_transposed(gate_grad, gate_weight) + times_transposed(
        upper_grad, up_weight
    )
    gain_third_part = lax.dynamic_slice_in_dim(gain_third, offset, shard_width).astype(jnp.float32)
    resid_two_grad, gain_third_grad = norm_backward(
        normed_third_grad, resid_two, inverse_third, gain_third_part, model_width, cot_shard
    )
    ffn_totals = (grad_gate, grad_upper, grad_down, gain_third_grad)
    cot_second = gather_cotangent(resid_two_grad.astype(jnp.bfloat16))
    grad_win_out = transposed_times(win_mixed, cot_second)
    win_mixed_grad = (
        times_transposed(cot_second, win_out)
        .astype(jnp.bfloat16)
        .reshape(row_count, heads_here, HEAD_DIM)
    )
    win_q_grad, win_k_grad, win_v_grad = window_backward(
        win_q, win_k, win_v, segments, log_totals, win_mixed_grad, block_rows, WINDOW, win_scale
    )
    win_q_low = win_q_grad.astype(jnp.bfloat16).reshape(row_count, heads_here * HEAD_DIM)
    win_k_low = win_k_grad.astype(jnp.bfloat16).reshape(row_count, heads_here * HEAD_DIM)
    win_v_low = win_v_grad.astype(jnp.bfloat16).reshape(row_count, heads_here * HEAD_DIM)
    grad_win_query = transposed_times(normed_second, win_q_low)
    grad_win_key = transposed_times(normed_second, win_k_low)
    grad_win_value = transposed_times(normed_second, win_v_low)
    normed_second_grad = (
        times_transposed(win_q_low, win_query)
        + times_transposed(win_k_low, win_key)
        + times_transposed(win_v_low, win_value)
    )
    gain_second_part = lax.dynamic_slice_in_dim(gain_second, offset, shard_width).astype(
        jnp.float32
    )
    resid_one_grad, gain_second_grad = norm_backward(
        normed_second_grad, resid_one, inverse_second, gain_second_part, model_width, resid_two_grad
    )
    window_totals = (grad_win_query, grad_win_key, grad_win_value, grad_win_out, gain_second_grad)
    cot_first = gather_cotangent(resid_one_grad.astype(jnp.bfloat16))
    grad_lin_out = transposed_times(lin_mixed, cot_first)
    lin_mixed_grad = times_transposed(cot_first, lin_out).reshape(row_count, heads_here, HEAD_DIM)
    lin_q_grad, lin_k_grad, lin_v_grad = linear_backward(
        lin_q, lin_k, lin_v, segments, lin_mixed_grad, block_rows, lin_scale
    )
    lin_q_low = lin_q_grad.astype(jnp.bfloat16).reshape(row_count, heads_here * FEATURE_SIZE)
    lin_k_low = lin_k_grad.astype(jnp.bfloat16).reshape(row_count, heads_here * FEATURE_SIZE)
    lin_v_low = lin_v_grad.astype(jnp.bfloat16).reshape(row_count, heads_here * HEAD_DIM)
    grad_lin_query = transposed_times(normed_first, lin_q_low)
    grad_lin_key = transposed_times(normed_first, lin_k_low)
    grad_lin_value = transposed_times(normed_first, lin_v_low)
    normed_first_grad = (
        times_transposed(lin_q_low, lin_query)
        + times_transposed(lin_k_low, lin_key)
        + times_transposed(lin_v_low, lin_value)
    )
    gain_first_part = lax.dynamic_slice_in_dim(gain_first, offset, shard_width).astype(jnp.float32)
    input_grad, gain_first_grad = norm_backward(
        normed_first_grad, resid_zero, inverse_first, gain_first_part, model_width, resid_one_grad
    )
    linear_totals = (grad_lin_query, grad_lin_key, grad_lin_value, grad_lin_out, gain_first_grad)
    every_total = lax.psum(
        (
            linear_totals[0],
            linear_totals[1],
            linear_totals[2],
            linear_totals[3],
            linear_totals[4],
            window_totals[0],
            window_totals[1],
            window_totals[2],
            window_totals[3],
            window_totals[4],
            ffn_totals[0],
            ffn_totals[1],
            ffn_totals[2],
            ffn_totals[3],
        ),
        "dp",
    )

    def masked_squares(values):
        return jnp.sum(validity * jnp.sum(values * values, axis=1))

    totals = lax.psum(
        (
            masked_squares(resid_zero),
            masked_squares(branch_first),
            masked_squares(branch_second),
            masked_squares(branch_third),
            masked_squares(output_resid),
            jnp.sum(validity),
        ),
        ("dp", "mp"),
    )
    count = totals[5] / lax.axis_size("mp")
    rms_values = jnp.sqrt(
        jnp.stack([totals[0], totals[1], totals[2], totals[3], totals[4]]) / (count * model_width)
    )
    return (
        output_resid.astype(jnp.bfloat16),
        input_grad,
        every_total[4],
        every_total[0],
        every_total[1],
        every_total[2],
        every_total[3],
        every_total[9],
        every_total[5],
        every_total[6],
        every_total[7],
        every_total[8],
        every_total[13],
        every_total[10],
        every_total[11],
        every_total[12],
        rms_values,
    )


def solution(mesh):
    in_specs = (
        P("dp", "mp"),
        P("dp", None),
        P(),
        P(None, "mp"),
        P(None, "mp"),
        P(None, "mp"),
        P("mp", None),
        P(),
        P(None, "mp"),
        P(None, "mp"),
        P(None, "mp"),
        P("mp", None),
        P(),
        P(None, "mp"),
        P(None, "mp"),
        P("mp", None),
        P("dp", "mp"),
    )
    out_specs = (
        P("dp", "mp"),
        P("dp", "mp"),
        P("mp"),
        P(None, "mp"),
        P(None, "mp"),
        P(None, "mp"),
        P("mp", None),
        P("mp"),
        P(None, "mp"),
        P(None, "mp"),
        P(None, "mp"),
        P("mp", None),
        P("mp"),
        P(None, "mp"),
        P(None, "mp"),
        P("mp", None),
        P(),
    )
    return jax.shard_map(
        per_device, mesh=mesh, in_specs=in_specs, out_specs=out_specs, check_vma=False
    )
```

profile of v0, /device:TPU:0, one launch (start us, length us, event | category | flops | bytes accessed | tf_op | source)
XLA Modules:
  0.0 2675.5 jit_solution(17794289890238666283)
XLA Ops:
  12.9 149.9 %all-gather.7.cloned.1.call-done = f32[1024,2048]{1,0:T(8,128)} async-done(((f32[1024,512]{1,0:T(8,128)}), f32[1024,2048]{1,0:T(8,128)}) %all-gather.7.cloned.1.call-update) | async-done | bytes 8388624 | tf_op jit(solution)/shard_map/all_gather | solution.py:39
  176.8 19.7 while.61
  204.4 142.7 %reduce-scatter.7.cloned.1.call-done = f32[1024,512]{1,0:T(8,128)} async-done(((f32[1024,2048]{1,0:T(8,128)}), f32[1024,512]{1,0:T(8,128)}) %reduce-scatter.7.cloned.1.call-update) | async-done | bytes 2097168 | tf_op jit(solution)/shard_map/reduce_scatter | solution.py:43
  351.1 150.4 %all-gather.9.cloned.1.call-done = f32[1024,2048]{1,0:T(8,128)} async-done(((f32[1024,512]{1,0:T(8,128)}), f32[1024,2048]{1,0:T(8,128)}) %all-gather.9.cloned.1.call-update) | async-done | bytes 8388624 | tf_op jit(solution)/shard_map/all_gather | solution.py:39
  531.1 31.2 %while.62 = (s32[]{:T(128)}, bf16[2,512,4,128]{3,2,1,0:T(4,128)(2,1)}, f32[2,4,512]{2,1,0:T(4,128)S(1)}, s32[2]{0:T(128)S(1)}, bf16[1088,4,128]{2,0,1:T(8,128)(2...) while((s32[]{:T(128)}, ...), condition=%wide.region_9.10_spmd, body=%wide.region_6.9_spmd.sunk | while | flops 619871808 | bytes 24208928 | solution.py:223
  569.3 142.8 %reduce-scatter.9.cloned.1.call-done = f32[1024,512]{1,0:T(8,128)} async-done(((f32[1024,2048]{1,0:T(8,128)}), f32[1024,512]{1,0:T(8,128)}) %reduce-scatter.9.cloned.1.call-update) | async-done | bytes 2097168 | tf_op jit(solution)/shard_map/reduce_scatter | solution.py:43
  719.1 147.9 %all-gather.11.cloned.1.call-done = f32[1024,2048]{1,0:T(8,128)} async-done(((f32[1024,512]{1,0:T(8,128)}), f32[1024,2048]{1,0:T(8,128)}) %all-gather.11.cloned.1.call-update) | async-done | bytes 8388624 | tf_op jit(solution)/shard_map/all_gather | solution.py:39
  873.6 13.0 fusion.108
  895.0 52.9 %all-gather.13.cloned.1.call-done = bf16[1024,2048]{1,0:T(8,128)(2,1)} async-done(((bf16[1024,512]{1,0:T(8,128)(2,1)}), bf16[1024,2048]{1,0:T(8,128)(2,1)}) %all-gather.13.cloned.1.call-update) | async-done | bytes 4194320 | tf_op jit(solution)/shard_map/all_gather | solution.py:47
  948.0 16.3 multiply_convert_fusion.5
  997.5 122.2 %reduce-scatter.11.cloned.1.call-done = f32[1024,512]{1,0:T(8,128)} async-done(((f32[1024,2048]{1,0:T(8,128)}), f32[1024,512]{1,0:T(8,128)}) %reduce-scatter.11.cloned.1.call-update) | async-done | bytes 2097168 | tf_op jit(solution)/shard_map/reduce_scatter | solution.py:43
  1119.7 148.2 %reduce-scatter.13.cloned.1.call-done = f32[1024,512]{1,0:T(8,128)} async-done(((f32[1024,2048]{1,0:T(8,128)}), f32[1024,512]{1,0:T(8,128)}) %reduce-scatter.13.cloned.1.call-update) | async-done | bytes 2097168 | tf_op jit(solution)/shard_map/reduce_scatter | solution.py:57
  1273.0 11.1 psum.161
  1288.3 79.2 %all-gather.15.cloned.1.call-done = bf16[1024,2048]{1,0:T(8,128)(2,1)} async-done(((bf16[1024,512]{1,0:T(8,128)(2,1)}), bf16[1024,2048]{1,0:T(8,128)(2,1)}) %all-gather.15.cloned.1.call-update) | async-done | bytes 4194320 | tf_op jit(solution)/shard_map/all_gather | solution.py:47
  1376.1 67.6 %while.63 = (s32[]{:T(128)}, f32[1088,4,128]{2,0,1:T(8,128)}, f32[1088,4,128]{2,0,1:T(8,128)}, bf16[2,512,4,128]{1,3,2,0:T(8,128)(2,1)}, s32[2]{0:T(128)S(1)}, /...) while((s32[]{:T(128)}, f32[1088,4,128]{2,0,1:T(8,128)}, ...), condition=%wide.region_18.19_spmd, body=%wide.region_16.18_spmd.sunk | while | flops 1530265088 | bytes 114968328 | solution.py:298
  1465.0 142.2 %reduce-scatter.15.cloned.1.call-done = f32[1024,512]{1,0:T(8,128)} async-done(((f32[1024,2048]{1,0:T(8,128)}), f32[1024,512]{1,0:T(8,128)}) %reduce-scatter.15.cloned.1.call-update) | async-done | bytes 2097168 | tf_op jit(solution)/shard_map/reduce_scatter | solution.py:57
  1610.0 11.1 psum.162
  1625.7 79.2 %all-gather.17.cloned.1.call-done = bf16[1024,2048]{1,0:T(8,128)(2,1)} async-done(((bf16[1024,512]{1,0:T(8,128)(2,1)}), bf16[1024,2048]{1,0:T(8,128)(2,1)}) %all-gather.17.cloned.1.call-update) | async-done | bytes 4194320 | tf_op jit(solution)/shard_map/all_gather | solution.py:47
  1711.5 33.9 %while.64 = (s32[]{:T(128)}, f32[1024,4,16]{0,2,1:T(8,128)S(1)}, f32[1024,4,128]{0,2,1:T(8,128)}, bf16[2,512,4,16]{1,3,2,0:T(8,128)(2,1)S(1)}, s32[2]{0:T(128)S(...) while((s32[]{:T(128)}, f32[1024,4,16]{0,2,1:T(8,128)S(1)}, ...), condition=%wide.region_25.26_spmd.clone, body=%wide.region_22.25_spmd.clone.sunk | while | flops 1872988672 | bytes 84490544 | solution.py:159
  1757.4 11.5 fusion.120
  1822.2 78.2 %reduce-scatter.17.cloned.1.call-done = f32[1024,512]{1,0:T(8,128)} async-done(((f32[1024,2048]{1,0:T(8,128)}), f32[1024,512]{1,0:T(8,128)}) %reduce-scatter.17.cloned.1.call-update) | async-done | bytes 2097168 | tf_op jit(solution)/shard_map/reduce_scatter | solution.py:57
  1903.5 42.2 %all-reduce.3 = (f32[1]{0:T(128)}, f32[1]{0:T(128)}, f32[1]{0:T(128)}, f32[1]{0:T(128)}, f32[1]{0:T(128)}, /*index=5*/f32[]{:T(128)}) all-reduce(f32[1]{0:T(128)} %bitcast.28, f32[1]{0:T(128)} %bitcast.29, f32[1]{0:T(128)} %bitcast.30, f32[1]{0:T(128)} %bitcast.31, f32[1]{0:T(128)} %bitcast.32, ...), channel_id=1, replica_groups=mesh['dp'=8,'mp'=4] {'dp','mp'}, use_global_device_ids=true, to_apply=%region_48.49 | all-reduce | flops 6 | bytes 48 | tf_op jit(solution)/shard_map/psum | solution.py:471
  1949.7 14.7 all-reduce.4
  1980.0 633.7 %all-reduce.8.cloned.1.call-done = (f32[2048,64]{0,1:T(8,128)}, f32[2048,64]{0,1:T(8,128)}, f32[2048,512]{1,0:T(8,128)}, f32[512,2048]{1,0:T(8,128)}, f32[2048,5...) async-done(((f32[2048,64]{0,1:T(8,128)}, ...) | async-done | bytes 60817424 | tf_op jit(solution)/shard_map/psum | solution.py:448
  (405 shorter events, 444.2 us)
Async XLA Ops:
  7.2 555.1 %copy-start = (bf16[512,2048]{1,0:T(8,128)(2,1)S(1)}, bf16[512,2048]{1,0:T(8,128)(2,1)}, u32[]{:S(2)}) copy-start(bf16[512,2048]{1,0:T(8,128)(2,1)} %param.36) | copy-start | bytes 6291460
  7.2 155.5 %all-gather.7.cloned.1.call-start = ((), (), s32[]{:S(2)}) async-start(), calls=%async_computation.6 | async-start | bytes 10485760 | tf_op jit(solution)/shard_map/all_gather | solution.py:39
  10.3 336.9 %reduce-scatter.7.cloned.1.call-start = ((), (), s32[]{:S(2)}) async-start(), calls=%async_computation.7 | async-start | bytes 10485760 | tf_op jit(solution)/shard_map/reduce_scatter | solution.py:43
  204.3 142.8 %copy-start.12 = (bf16[1024,512]{1,0:T(8,128)(2,1)S(1)}, bf16[1024,512]{1,0:T(8,128)(2,1)}, u32[]{:S(2)}) copy-start(bf16[1024,512]{1,0:T(8,128)(2,1)} %param.25) | copy-start | bytes 3145732
  204.4 146.7 %copy-start.62 = (bf16[2048]{0:T(1024)(128)(2,1)S(1)}, bf16[2048]{0:T(1024)(128)(2,1)}, u32[]{:S(2)}) copy-start(bf16[2048]{0:T(1024)(128)(2,1)} %param.32) | copy-start | bytes 12292
  204.4 297.1 %all-gather.9.cloned.1.call-start = ((), (), s32[]{:S(2)}) async-start(), calls=%async_computation.8 | async-start | bytes 10485760 | tf_op jit(solution)/shard_map/all_gather | solution.py:39
  351.0 361.1 %reduce-scatter.9.cloned.1.call-start = ((), (), s32[]{:S(2)}) async-start(), calls=%async_computation.9 | async-start | bytes 10485760 | tf_op jit(solution)/shard_map/reduce_scatter | solution.py:43
  569.3 297.7 %all-gather.11.cloned.1.call-start = ((), (), s32[]{:S(2)}) async-start(), calls=%async_computation.10 | async-start | bytes 10485760 | tf_op jit(solution)/shard_map/all_gather | solution.py:39
  716.5 231.5 %all-gather.13.cloned.1.call-start = ((), (), s32[]{:S(2)}) async-start(), calls=%async_computation.12 | async-start | bytes 5242880 | tf_op jit(solution)/shard_map/all_gather | solution.py:47
  719.0 400.7 %reduce-scatter.11.cloned.1.call-start = ((), (), s32[]{:S(2)}) async-start(), calls=%async_computation.11 | async-start | bytes 10485760 | tf_op jit(solution)/shard_map/reduce_scatter | solution.py:43
  976.6 291.3 %reduce-scatter.13.cloned.1.call-start = ((), (), s32[]{:S(2)}) async-start(), calls=%async_computation.13 | async-start | bytes 10485760 | tf_op jit(solution)/shard_map/reduce_scatter | solution.py:57
  997.4 370.2 %all-gather.15.cloned.1.call-start = ((), (), s32[]{:S(2)}) async-start(), calls=%async_computation.14 | async-start | bytes 5242880 | tf_op jit(solution)/shard_map/all_gather | solution.py:47
  1288.3 319.0 %reduce-scatter.15.cloned.1.call-start = ((), (), s32[]{:S(2)}) async-start(), calls=%async_computation.15 | async-start | bytes 10485760 | tf_op jit(solution)/shard_map/reduce_scatter | solution.py:57
  1464.1 143.2 %copy-start.7 = (f32[1024,512]{1,0:T(8,128)S(1)}, f32[1024,512]{1,0:T(8,128)}, u32[]{:S(2)}) copy-start(f32[1024,512]{1,0:T(8,128)} %get-tuple-element.808) | copy-start | bytes 6291460
  1464.1 143.2 %copy-start.54 = (f32[1024]{0:T(1024)S(1)}, f32[1024]{0:T(1024)}, u32[]{:S(2)}) copy-start(f32[1024]{0:T(1024)} %copy-done.53) | copy-start | bytes 12292
  1464.1 240.8 %all-gather.17.cloned.1.call-start = ((), (), s32[]{:S(2)}) async-start(), calls=%async_computation.16 | async-start | bytes 5242880 | tf_op jit(solution)/shard_map/all_gather | solution.py:47
  1625.6 274.8 %reduce-scatter.17.cloned.1.call-start = ((), (), s32[]{:S(2)}) async-start(), calls=%async_computation.17 | async-start | bytes 10485760 | tf_op jit(solution)/shard_map/reduce_scatter | solution.py:57
  1625.7 85.8 %copy-start.22 = (bf16[1024,4,16]{0,2,1:T(8,128)(2,1)S(1)}, bf16[1024,4,16]{0,2,1:T(8,128)(2,1)}, u32[]{:S(2)}) copy-start(bf16[1024,4,16]{0,2,1:T(8,128)(2,1)} %copy-done.21) | copy-start | bytes 393220
  1625.7 85.8 %copy-start.39 = (bf16[1024,4,16]{0,2,1:T(8,128)(2,1)S(1)}, bf16[1024,4,16]{0,2,1:T(8,128)(2,1)}, u32[]{:S(2)}) copy-start(bf16[1024,4,16]{0,2,1:T(8,128)(2,1)} %copy-done.38) | copy-start | bytes 393220
  1625.7 85.8 %copy-start.45 = (bf16[1024,512]{0,1:T(8,128)(2,1)S(1)}, bf16[1024,512]{0,1:T(8,128)(2,1)}, u32[]{:S(2)}) copy-start(bf16[1024,512]{0,1:T(8,128)(2,1)} %copy-done.44) | copy-start | bytes 3145732
  1757.3 856.4 %all-reduce.8.cloned.1.call-start = ((), (), s32[]{:S(2)}) async-start(), calls=%async_computation.18 | async-start | bytes 121634816 | tf_op jit(solution)/shard_map/psum | solution.py:448
  1818.9 81.6 %copy-start.13 = (bf16[1024,512]{1,0:T(8,128)(2,1)S(1)}, bf16[1024,512]{1,0:T(8,128)(2,1)}, u32[]{:S(2)}) copy-start(bf16[1024,512]{1,0:T(8,128)(2,1)} %param.25) | copy-start | bytes 3145732
  1818.9 130.7 %copy-start.59 = (f32[512]{0:T(512)S(1)}, f32[512]{0:T(512)}, u32[]{:S(2)}) copy-start(f32[512]{0:T(512)} %get-tuple-element.680) | copy-start | bytes 6148
  1818.9 130.7 %copy-start.60 = (f32[512]{0:T(512)S(1)}, f32[512]{0:T(512)}, u32[]{:S(2)}) copy-start(f32[512]{0:T(512)} %get-tuple-element.687) | copy-start | bytes 6148
  (79 other events, 471.1 us)
Sparse Core Ops, SparseCore 0:
  10.4 152.3 all-gather.6
  204.5 142.6 reduce-scatter.6
  351.1 150.3 all-gather.8
  569.4 142.6 reduce-scatter.8
  716.6 150.3 all-gather.10
  869.0 78.9 all-gather.12
  976.7 142.9 reduce-scatter.10
  1122.6 145.2 reduce-scatter.12
  1288.4 79.1 all-gather.14
  1464.2 142.9 reduce-scatter.14
  1625.7 79.1 all-gather.16
  1757.4 142.9 reduce-scatter.16
  1907.6 706.1 all-reduce.7
where the time goes:
time: 2680 us
  waiting for transfers between devices  2070 us (77%)
  matrix products  269 us (10%)
  local copies, waits for them, and re-layouts  131 us (5%)
  blocking collectives  89.8 us (3%)
  other arithmetic  73.2 us (3%)
    psum x1, waiting for transfers between devices, per_device(): lax.psum((linear_totals[0], linear_totals[1], linear_totals[2], linear_to...  634 us
    all_gather x3, waiting for transfers between devices, gather_stream(): return lax.all_gather(shard_part, 'mp', axis=1, tiled=True)  448 us
    reduce_scatter x3, waiting for transfers between devices, branch_total(): lax.psum_scatter(partial_value, 'mp', scatter_dimension=1, tiled=True)  408 us
    reduce_scatter x3, waiting for transfers between devices, norm_backward(): lax.psum_scatter(partial_value, 'mp', scatter_dimension=1, tiled=True)  369 us
    all_gather x3, waiting for transfers between devices, gather_cotangent(): return lax.all_gather(shard_part, 'mp', axis=1, tiled=True)  211 us
    dot_general x11, matrix products, times_transposed(): lax.dot_general(left_side, right_side, (((1,), (1,)), ((), ())), preferre...  71.6 us
    unnamed x140, local copies, waits for them, and re-layouts  63 us
    dot_general x11, matrix products, transposed_times(): lax.dot_general(left_side, right_side, (((0,), (0,)), ((), ())), preferre...  61.4 us
  transfers between devices with their start and end apart: 13, of which 13 were waited for; matrix products, arithmetic and copies ran while one was open for 5% of the time, Pallas kernels for 0%

commit v1 on v0

--- a/solution.py
+++ b/solution.py
@@ -36,15 +36,24 @@
 
 
 def gather_stream(shard_part):
-    return lax.all_gather(shard_part, "mp", axis=1, tiled=True)
+    return lax.all_gather(shard_part.astype(jnp.bfloat16), "mp", axis=1, tiled=True).astype(
+        jnp.float32
+    )
 
 
 def branch_total(partial_value):
-    return lax.psum_scatter(partial_value, "mp", scatter_dimension=1, tiled=True)
+    return lax.psum_scatter(
+        partial_value.astype(jnp.bfloat16), "mp", scatter_dimension=1, tiled=True
+    ).astype(jnp.float32)
 
 
 def gather_cotangent(shard_part):
     return lax.all_gather(shard_part, "mp", axis=1, tiled=True)
+
+
+def sum_groups(values):
+    narrow = tuple(v.astype(jnp.bfloat16) if v.ndim == 2 else v for v in values)
+    return tuple(v.astype(jnp.float32) for v in lax.psum(narrow, "dp"))
 
 
 def rms_forward(full_stream, gain_vector):
@@ -54,7 +63,7 @@
 
 
 def norm_backward(partial_value, resid_part, inverse, gain_part, model_width, carried):
-    shard_grad = lax.psum_scatter(partial_value, "mp", scatter_dimension=1, tiled=True)
+    shard_grad = branch_total(partial_value)
     scaled = shard_grad * gain_part
     normed_part = resid_part * inverse[:, None]
     row_dot = lax.psum(jnp.sum(scaled * normed_part, axis=1), "mp")
@@ -445,7 +454,7 @@
         normed_first_grad, resid_zero, inverse_first, gain_first_part, model_width, resid_one_grad
     )
     linear_totals = (grad_lin_query, grad_lin_key, grad_lin_value, grad_lin_out, gain_first_grad)
-    every_total = lax.psum(
+    every_total = sum_groups(
         (
             linear_totals[0],
             linear_totals[1],
@@ -461,8 +470,7 @@
             ffn_totals[1],
             ffn_totals[2],
             ffn_totals[3],
-        ),
-        "dp",
+        )
     )
 
     def masked_squares(values):

time: 2680 us -> 1710 us (0.64)
  waiting for transfers between devices: 2070 us -> 1130 us
  local copies, waits for them, and re-layouts: 131 us -> 77.2 us
  other arithmetic: 73.2 us -> 101 us
    reduce_scatter x6, waiting for transfers between devices: 776 us -> 360 us  [branch_total(): lax.psum_scatter(partial_value.astype(jnp.bfloat16), 'mp', scatter_dimens...]
    psum x1, waiting for transfers between devices: 634 us -> 327 us  [sum_groups(): return tuple((v.astype(jnp.float32) for v in lax.psum(narrow, 'dp')))]
    all_gather x3, waiting for transfers between devices: 448 us -> 241 us  [gather_stream(): lax.all_gather(shard_part.astype(jnp.bfloat16), 'mp', axis=1, tiled=True)]
    unnamed x140 -> x145, local copies, waits for them, and re-layouts: 63 us -> 4.47 us
    convert_element_type x1 -> x13, other arithmetic: 2.97 us -> 43.8 us  [the longest x11 38.1 us: sum_groups(): return tuple((v.astype(jnp.float32) for v in lax.psum(narrow, 'dp')))]
  transfers between devices with their start and end apart: 13 -> 13, of which waited for: 13 -> 12; matrix products, arithmetic and copies ran while one was open for 5% -> 7% of each run, Pallas kernels for 0% -> 0%
where the time goes in v1:
time: 1710 us
  waiting for transfers between devices  1130 us (66%)
  matrix products  264 us (15%)
  other arithmetic  101 us (6%)
  blocking collectives  90 us (5%)
  local copies, waits for them, and re-layouts  77.2 us (5%)
  loops' own time  24.7 us (1%)
  between operations  17.1 us (1%)
    reduce_scatter x6, waiting for transfers between devices, branch_total(): lax.psum_scatter(partial_value.astype(jnp.bfloat16), 'mp', scatter_dimens...  360 us
    psum x1, waiting for transfers between devices, sum_groups(): return tuple((v.astype(jnp.float32) for v in lax.psum(narrow, 'dp')))  327 us
    all_gather x3, waiting for transfers between devices, gather_stream(): lax.all_gather(shard_part.astype(jnp.bfloat16), 'mp', axis=1, tiled=True)  241 us
    all_gather x3, waiting for transfers between devices, gather_cotangent(): return lax.all_gather(shard_part, 'mp', axis=1, tiled=True)  205 us
    dot_general x11, matrix products, times_transposed(): lax.dot_general(left_side, right_side, (((1,), (1,)), ((), ())), preferre...  70.9 us
    dot_general x11, matrix products, transposed_times(): lax.dot_general(left_side, right_side, (((0,), (0,)), ((), ())), preferre...  58.3 us
    psum x1, blocking collectives, per_device(): lax.psum((masked_squares(resid_zero), masked_squares(branch_first), maske...  42.4 us
    convert_element_type x11, other arithmetic, sum_groups(): return tuple((v.astype(jnp.float32) for v in lax.psum(narrow, 'dp')))  38.1 us
  transfers between devices with their start and end apart: 13, of which 12 were waited for; matrix products, arithmetic and copies ran while one was open for 7% of the time, Pallas kernels for 0%

profile of v1, /device:TPU:0, one launch (start us, length us, event | category | flops | bytes accessed | tf_op | source)
XLA Modules:
  0.0 1707.6 jit_solution(12650474813000453455)
XLA Ops:
  12.0 81.1 %all-gather.7.cloned.1.call-done = bf16[1024,2048]{1,0:T(8,128)(2,1)} async-done(((bf16[1024,512]{1,0:T(8,128)(2,1)}), bf16[1024,2048]{1,0:T(8,128)(2,1)}) %all-gather.7.cloned.1.call-update) | async-done | bytes 4194320 | tf_op jit(solution)/shard_map/all_gather | solution.py:39
  108.1 21.5 %while.61 = (s32[]{:T(128)}, bf16[2,512,4,128]{3,2,1,0:T(4,128)(2,1)}, s32[2]{0:T(128)S(1)}, s32[1024]{0:T(1024)S(1)}, bf16[1024,4,16]{0,2,1:T(8,128)(2,1)S(1)},...) while((s32[]{:T(128)}, ...), condition=%wide.region_3.4_spmd, body=%wide.region_1.3_spmd.sunk | while | flops 635435520 | bytes 33782016 | solution.py:115
  136.6 75.4 %reduce-scatter.7.cloned.1.call-done = bf16[1024,512]{1,0:T(8,128)(2,1)} async-done(((bf16[1024,2048]{1,0:T(8,128)(2,1)}), bf16[1024,512]{1,0:T(8,128)(2,1)}) %reduce-scatter.7.cloned.1.call-update) | async-done | bytes 1048592 | tf_op jit(solution)/shard_map/reduce_scatter | solution.py:45
  214.7 81.3 %all-gather.9.cloned.1.call-done = bf16[1024,2048]{1,0:T(8,128)(2,1)} async-done(((bf16[1024,512]{1,0:T(8,128)(2,1)}), bf16[1024,2048]{1,0:T(8,128)(2,1)}) %all-gather.9.cloned.1.call-update) | async-done | bytes 4194320 | tf_op jit(solution)/shard_map/all_gather | solution.py:39
  323.3 31.3 %while.62 = (s32[]{:T(128)}, bf16[2,512,4,128]{3,2,1,0:T(4,128)(2,1)}, f32[2,4,512]{2,1,0:T(4,128)S(1)}, s32[2]{0:T(128)S(1)}, bf16[1088,4,128]{2,0,1:T(8,128)(2...) while((s32[]{:T(128)}, ...), condition=%wide.region_9.10_spmd, body=%wide.region_6.9_spmd.sunk | while | flops 619871808 | bytes 24208928 | solution.py:232
  360.2 75.4 %reduce-scatter.9.cloned.1.call-done = bf16[1024,512]{1,0:T(8,128)(2,1)} async-done(((bf16[1024,2048]{1,0:T(8,128)(2,1)}), bf16[1024,512]{1,0:T(8,128)(2,1)}) %reduce-scatter.9.cloned.1.call-update) | async-done | bytes 1048592 | tf_op jit(solution)/shard_map/reduce_scatter | solution.py:45
  441.5 78.8 %all-gather.11.cloned.1.call-done = bf16[1024,2048]{1,0:T(8,128)(2,1)} async-done(((bf16[1024,512]{1,0:T(8,128)(2,1)}), bf16[1024,2048]{1,0:T(8,128)(2,1)}) %all-gather.11.cloned.1.call-update) | async-done | bytes 4194320 | tf_op jit(solution)/shard_map/all_gather | solution.py:39
  523.7 11.0 fusion.139
  543.5 58.1 %all-gather.13.cloned.1.call-done = bf16[1024,2048]{1,0:T(8,128)(2,1)} async-done(((bf16[1024,512]{1,0:T(8,128)(2,1)}), bf16[1024,2048]{1,0:T(8,128)(2,1)}) %all-gather.13.cloned.1.call-update) | async-done | bytes 4194320 | tf_op jit(solution)/shard_map/all_gather | solution.py:51
  601.6 16.1 multiply_convert_fusion.2
  619.3 11.0 convolution_convert_fusion.3
  640.6 11.0 add_convert_fusion.2
  651.7 54.0 %reduce-scatter.11.cloned.1.call-done = bf16[1024,512]{1,0:T(8,128)(2,1)} async-done(((bf16[1024,2048]{1,0:T(8,128)(2,1)}), bf16[1024,512]{1,0:T(8,128)(2,1)}) %reduce-scatter.11.cloned.1.call-update) | async-done | bytes 1048592 | tf_op jit(solution)/shard_map/reduce_scatter | solution.py:45
  705.7 80.3 %reduce-scatter.13.cloned.1.call-done = bf16[1024,512]{1,0:T(8,128)(2,1)} async-done(((bf16[1024,2048]{1,0:T(8,128)(2,1)}), bf16[1024,512]{1,0:T(8,128)(2,1)}) %reduce-scatter.13.cloned.1.call-update) | async-done | bytes 1048592 | tf_op jit(solution)/shard_map/reduce_scatter | solution.py:45
  806.2 79.2 %all-gather.15.cloned.1.call-done = bf16[1024,2048]{1,0:T(8,128)(2,1)} async-done(((bf16[1024,512]{1,0:T(8,128)(2,1)}), bf16[1024,2048]{1,0:T(8,128)(2,1)}) %all-gather.15.cloned.1.call-update) | async-done | bytes 4194320 | tf_op jit(solution)/shard_map/all_gather | solution.py:51
  894.0 67.4 %while.63 = (s32[]{:T(128)}, f32[1088,4,128]{2,0,1:T(8,128)}, f32[1088,4,128]{2,0,1:T(8,128)}, bf16[2,512,4,128]{1,3,2,0:T(8,128)(2,1)}, s32[2]{0:T(128)S(1)}, /...) while((s32[]{:T(128)}, f32[1088,4,128]{2,0,1:T(8,128)}, ...), condition=%wide.region_18.19_spmd, body=%wide.region_16.18_spmd.sunk | while | flops 1530265088 | bytes 114968328 | solution.py:307
  983.0 74.5 %reduce-scatter.15.cloned.1.call-done = bf16[1024,512]{1,0:T(8,128)(2,1)} async-done(((bf16[1024,2048]{1,0:T(8,128)(2,1)}), bf16[1024,512]{1,0:T(8,128)(2,1)}) %reduce-scatter.15.cloned.1.call-update) | async-done | bytes 1048592 | tf_op jit(solution)/shard_map/reduce_scatter | solution.py:45
  1060.2 10.9 psum.162
  1075.5 11.4 convolution_convert_fusion.1
  1086.9 67.8 %all-gather.17.cloned.1.call-done = bf16[1024,2048]{1,0:T(8,128)(2,1)} async-done(((bf16[1024,512]{1,0:T(8,128)(2,1)}), bf16[1024,2048]{1,0:T(8,128)(2,1)}) %all-gather.17.cloned.1.call-update) | async-done | bytes 4194320 | tf_op jit(solution)/shard_map/all_gather | solution.py:51
  1161.3 33.8 %while.64 = (s32[]{:T(128)}, f32[1024,4,16]{0,2,1:T(8,128)S(1)}, f32[1024,4,128]{0,2,1:T(8,128)}, bf16[2,512,4,16]{1,3,2,0:T(8,128)(2,1)S(1)}, s32[2]{0:T(128)S(...) while((s32[]{:T(128)}, f32[1024,4,16]{0,2,1:T(8,128)S(1)}, ...), condition=%wide.region_25.26_spmd.clone, body=%wide.region_22.25_spmd.clone.sunk | while | flops 1872988672 | bytes 84490544 | solution.py:168
  1256.3 42.4 %all-reduce.3 = (f32[1]{0:T(128)}, f32[1]{0:T(128)}, f32[1]{0:T(128)}, f32[1]{0:T(128)}, f32[1]{0:T(128)}, /*index=5*/f32[]{:T(128)}) all-reduce(f32[1]{0:T(128)} %bitcast.28, f32[1]{0:T(128)} %bitcast.29, f32[1]{0:T(128)} %bitcast.30, f32[1]{0:T(128)} %bitcast.31, f32[1]{0:T(128)} %bitcast.32, ...), channel_id=1, replica_groups=mesh['dp'=8,'mp'=4] {'dp','mp'}, use_global_device_ids=true, to_apply=%region_48.49 | all-reduce | flops 6 | bytes 48 | tf_op jit(solution)/shard_map/psum | solution.py:479
  1305.1 15.1 all-reduce.4
  1334.8 326.7 %all-reduce.8.cloned.1.call-done = (bf16[2048,64]{0,1:T(8,128)(2,1)}, bf16[2048,64]{0,1:T(8,128)(2,1)}, bf16[2048,512]{1,0:T(8,128)(2,1)}, bf16[512,2048]{1,0:T(...) async-done(((bf16[2048,64]{0,1:T(8,128)(2,1)}, ...) | async-done | bytes 30408720 | tf_op jit(solution)/shard_map/psum | solution.py:56
  (428 shorter events, 404.4 us)
Async XLA Ops:
  7.2 347.4 %copy-start = (bf16[512,2048]{1,0:T(8,128)(2,1)S(1)}, bf16[512,2048]{1,0:T(8,128)(2,1)}, u32[]{:S(2)}) copy-start(bf16[512,2048]{1,0:T(8,128)(2,1)} %param.36) | copy-start | bytes 6291460
  7.2 85.9 %all-gather.7.cloned.1.call-start = ((), (), s32[]{:S(2)}) async-start(), calls=%async_computation.6 | async-start | bytes 5242880 | tf_op jit(solution)/shard_map/all_gather | solution.py:39
  7.9 204.1 %reduce-scatter.7.cloned.1.call-start = ((), (), s32[]{:S(2)}) async-start(), calls=%async_computation.7 | async-start | bytes 5242880 | tf_op jit(solution)/shard_map/reduce_scatter | solution.py:45
  136.5 75.5 %copy-start.7 = (bf16[1024,512]{1,0:T(8,128)(2,1)S(1)}, bf16[1024,512]{1,0:T(8,128)(2,1)}, u32[]{:S(2)}) copy-start(bf16[1024,512]{1,0:T(8,128)(2,1)} %param.25) | copy-start | bytes 3145732
  136.5 78.0 %copy-start.68 = (bf16[2048]{0:T(1024)(128)(2,1)S(1)}, bf16[2048]{0:T(1024)(128)(2,1)}, u32[]{:S(2)}) copy-start(bf16[2048]{0:T(1024)(128)(2,1)} %param.32) | copy-start | bytes 12292
  136.6 159.4 %all-gather.9.cloned.1.call-start = ((), (), s32[]{:S(2)}) async-start(), calls=%async_computation.8 | async-start | bytes 5242880 | tf_op jit(solution)/shard_map/all_gather | solution.py:39
  214.5 221.1 %reduce-scatter.9.cloned.1.call-start = ((), (), s32[]{:S(2)}) async-start(), calls=%async_computation.9 | async-start | bytes 5242880 | tf_op jit(solution)/shard_map/reduce_scatter | solution.py:45
  214.6 97.1 %copy-start.62 = (f32[2048]{0:T(1024)}, f32[2048]{0:T(1024)S(1)}, u32[]{:S(2)}) copy-start(f32[2048]{0:T(1024)S(1)} %convert_element_type.302) | copy-start | bytes 24580
  360.1 81.3 %copy-start.67 = (bf16[2048]{0:T(1024)(128)(2,1)S(1)}, bf16[2048]{0:T(1024)(128)(2,1)}, u32[]{:S(2)}) copy-start(bf16[2048]{0:T(1024)(128)(2,1)} %param.37) | copy-start | bytes 12292
  360.2 160.1 %all-gather.11.cloned.1.call-start = ((), (), s32[]{:S(2)}) async-start(), calls=%async_computation.10 | async-start | bytes 5242880 | tf_op jit(solution)/shard_map/all_gather | solution.py:39
  438.9 162.7 %all-gather.13.cloned.1.call-start = ((), (), s32[]{:S(2)}) async-start(), calls=%async_computation.12 | async-start | bytes 5242880 | tf_op jit(solution)/shard_map/all_gather | solution.py:51
  441.4 264.3 %reduce-scatter.11.cloned.1.call-start = ((), (), s32[]{:S(2)}) async-start(), calls=%async_computation.11 | async-start | bytes 5242880 | tf_op jit(solution)/shard_map/reduce_scatter | solution.py:45
  441.5 93.2 %copy-start.64 = (f32[2048]{0:T(1024)}, f32[2048]{0:T(1024)S(1)}, u32[]{:S(2)}) copy-start(f32[2048]{0:T(1024)S(1)} %convert_element_type.311) | copy-start | bytes 24580
  523.7 551.7 %copy-start.48 = (f32[1024]{0:T(1024)}, f32[1024]{0:T(1024)S(1)}, u32[]{:S(2)}) copy-start(f32[1024]{0:T(1024)S(1)} %add_rsqrt_fusion) | copy-start | bytes 12292
  630.3 155.7 %reduce-scatter.13.cloned.1.call-start = ((), (), s32[]{:S(2)}) async-start(), calls=%async_computation.13 | async-start | bytes 5242880 | tf_op jit(solution)/shard_map/reduce_scatter | solution.py:45
  651.6 233.9 %all-gather.15.cloned.1.call-start = ((), (), s32[]{:S(2)}) async-start(), calls=%async_computation.14 | async-start | bytes 5242880 | tf_op jit(solution)/shard_map/all_gather | solution.py:51
  806.2 251.3 %reduce-scatter.15.cloned.1.call-start = ((), (), s32[]{:S(2)}) async-start(), calls=%async_computation.15 | async-start | bytes 5242880 | tf_op jit(solution)/shard_map/reduce_scatter | solution.py:45
  982.0 75.5 %copy-start.8 = (bf16[1024,512]{1,0:T(8,128)(2,1)S(1)}, bf16[1024,512]{1,0:T(8,128)(2,1)}, u32[]{:S(2)}) copy-start(bf16[1024,512]{1,0:T(8,128)(2,1)} %param.25) | copy-start | bytes 3145732
  982.0 75.5 %copy-start.11 = (bf16[1024,512]{1,0:T(8,128)(2,1)S(1)}, bf16[1024,512]{1,0:T(8,128)(2,1)}, u32[]{:S(2)}) copy-start(bf16[1024,512]{1,0:T(8,128)(2,1)} %reduce-scatter.7.cloned.1.call-done) | copy-start | bytes 3145732
  982.0 75.5 %copy-start.53 = (f32[1024]{0:T(1024)S(1)}, f32[1024]{0:T(1024)}, u32[]{:S(2)}) copy-start(f32[1024]{0:T(1024)} %copy-done.52) | copy-start | bytes 12292
  982.0 89.1 %copy-start.13 = (bf16[1024,512]{1,0:T(8,128)(2,1)S(1)}, bf16[1024,512]{1,0:T(8,128)(2,1)}, u32[]{:S(2)}) copy-start(bf16[1024,512]{1,0:T(8,128)(2,1)} %reduce-scatter.9.cloned.1.call-done) | copy-start | bytes 3145732
  982.0 172.7 %all-gather.17.cloned.1.call-start = ((), (), s32[]{:S(2)}) async-start(), calls=%async_computation.16 | async-start | bytes 5242880 | tf_op jit(solution)/shard_map/all_gather | solution.py:51
  1075.4 227.7 %reduce-scatter.17.cloned.1.call-start = ((), (), s32[]{:S(2)}) async-start(), calls=%async_computation.17 | async-start | bytes 5242880 | tf_op jit(solution)/shard_map/reduce_scatter | solution.py:45
  1205.7 455.8 %all-reduce.8.cloned.1.call-start = ((), (), s32[]{:S(2)}) async-start(), calls=%async_computation.18 | async-start | bytes 60817408 | tf_op jit(solution)/shard_map/psum | solution.py:56
  (91 other events, 836.6 us)
Sparse Core Ops, SparseCore 0:
  9.6 83.4 all-gather.6
  136.7 75.2 reduce-scatter.6
  214.6 81.2 all-gather.8
  360.3 75.2 reduce-scatter.8
  439.0 81.2 all-gather.10
  522.3 79.2 all-gather.12
  630.4 75.2 reduce-scatter.10
  708.7 77.2 reduce-scatter.12
  806.3 79.1 all-gather.14
  982.2 75.2 reduce-scatter.14
  1075.5 79.1 all-gather.16
  1205.8 75.9 reduce-scatter.16
  1289.1 372.3 all-reduce.7

commit v2 on v0

v2 whole, which is shorter than its diff:
```python
import functools

import jax
import jax.numpy as jnp
from jax import lax
from jax.experimental import pallas as pl
from jax.experimental.pallas import tpu as pltpu
from jax.sharding import PartitionSpec as P

FEATURE_SIZE = 16
HEAD_DIM = 128
WINDOW = 64
EPSILON = 1e-05
NEGATIVE = -1e30
CHUNKS = 2
LIN_SCALE = FEATURE_SIZE ** (-0.5)
WIN_SCALE = HEAD_DIM ** (-0.5)
F32 = jnp.float32
BF16 = jnp.bfloat16
PAD_ROWS = 16
VMEM_LIMIT = 40 * 1024 * 1024


def nn(left, right):
    return lax.dot_general(left, right, (((1,), (0,)), ((), ())), preferred_element_type=F32)


def nt(left, right):
    return lax.dot_general(left, right, (((1,), (1,)), ((), ())), preferred_element_type=F32)


def tn(left, right):
    return lax.dot_general(left, right, (((0,), (0,)), ((), ())), preferred_element_type=F32)


def segment_start(lens_ref, place):
    first_end = lens_ref[0, 0]
    second_end = first_end + lens_ref[0, 1]
    return jnp.where(place < first_end, 0, jnp.where(place < second_end, first_end, second_end))


def causal_allowed(lens_ref, row_begin, key_begin, rows, keys, window):
    place = row_begin + lax.broadcasted_iota(jnp.int32, (rows, 1), 0)
    key_place = key_begin + lax.broadcasted_iota(jnp.int32, (rows, keys), 1)
    lowest = segment_start(lens_ref, place)
    if window:
        lowest = jnp.maximum(lowest, place - (window - 1))
    allowed = key_place >= lowest
    if key_begin + keys > row_begin:
        allowed = allowed & (key_place <= place)
    return allowed


def head_lanes(values, head):
    lane = lax.broadcasted_iota(jnp.int32, values.shape, 1) // FEATURE_SIZE
    return jnp.where(lane == head, values, jnp.zeros_like(values))


def linear_tile(lens_ref, query, key, row_begin, key_begin):
    logits = nt(query, key) * LIN_SCALE
    allowed = causal_allowed(lens_ref, row_begin, key_begin, query.shape[0], key.shape[0], 0)
    kernel = jnp.where(allowed, 1.0 + logits + 0.5 * logits * logits, 0.0)
    return logits, allowed, kernel


def linear_forward_kernel(chunk, rows, tile, lens_ref, q_ref, *refs):
    count = chunk + 1
    k_refs, v_refs = refs[:count], refs[count : 2 * count]
    low_ref, mixed_ref, total_ref = refs[2 * count :]
    head = pl.program_id(0)
    per = rows // tile
    for i in range(per):
        row_begin = chunk * rows + i * tile
        query = q_ref[pl.ds(i * tile, tile), :]
        total = jnp.zeros((tile, 1), F32)
        number = jnp.zeros((tile, HEAD_DIM), F32)
        for j in range(chunk * per + i + 1):
            span = pl.ds((j % per) * tile, tile)
            key = head_lanes(k_refs[j // per][span, :], head)
            _, _, kernel = linear_tile(lens_ref, query, key, row_begin, j * tile)
            total += jnp.sum(kernel, axis=1, keepdims=True)
            number += nn(kernel.astype(BF16), v_refs[j // per][span, :])
        mixed = number / total
        low_ref[pl.ds(i * tile, tile), :] = mixed.astype(BF16)
        mixed_ref[pl.ds(i * tile, tile), :] = mixed
        total_ref[0, pl.ds(i * tile, tile), :] = total


def linear_backward_kernel(chunk, rows, tile, carried, lens_ref, q_ref, *refs):
    count = chunk + 1
    k_refs, v_refs = refs[:count], refs[count : 2 * count]
    do_ref, mixed_ref, total_ref = refs[2 * count : 2 * count + 3]
    refs = refs[2 * count + 3 :]
    if carried:
        dk_in, dv_in = refs[:2]
        refs = refs[2:]
    dq_out, dk_out, dv_out = refs[:3]
    dk_prev, dv_prev = refs[3 : 3 + chunk], refs[3 + chunk : 3 + 2 * chunk]
    dq_acc, dk_acc, dv_acc = refs[3 + 2 * chunk :]
    head = pl.program_id(0)
    last = pl.num_programs(0) - 1
    per = rows // tile

    @pl.when(head == 0)
    def _():
        dq_acc[...] = jnp.zeros_like(dq_acc)
        dk_acc[...] = jnp.zeros_like(dk_acc)
        if carried:
            dk_acc[pl.ds(chunk * rows, rows), :] = dk_in[...]

    dv_acc[...] = jnp.zeros_like(dv_acc)
    if carried:
        dv_acc[pl.ds(chunk * rows, rows), :] = dv_in[...]
    for i in range(per):
        row_begin = chunk * rows + i * tile
        own = pl.ds(i * tile, tile)
        query = head_lanes(q_ref[own, :], head)
        grad = do_ref[own, :]
        inverse = 1.0 / total_ref[0, own, :]
        number_grad = (grad * inverse).astype(BF16)
        total_grad = -jnp.sum(grad * mixed_ref[own, :], axis=1, keepdims=True) * inverse
        dq = jnp.zeros((tile, q_ref.shape[1]), F32)
        for j in range(chunk * per + i + 1):
            span = pl.ds((j % per) * tile, tile)
            key = head_lanes(k_refs[j // per][span, :], head)
            logits, allowed, kernel = linear_tile(lens_ref, query, key, row_begin, j * tile)
            kernel_grad = nt(number_grad, v_refs[j // per][span, :]) + total_grad
            scores_grad = jnp.where(allowed, kernel_grad * (1.0 + logits), 0.0).astype(BF16)
            dq += nn(scores_grad, key)
            keys = pl.ds(j * tile, tile)
            dk_acc[keys, :] += tn(scores_grad, query) * LIN_SCALE
            dv_acc[keys, :] += tn(kernel.astype(BF16), number_grad)
        dq_acc[own, :] += dq * LIN_SCALE
    dv_out[...] = dv_acc[pl.ds(chunk * rows, rows), :].astype(BF16)
    for c in range(chunk):
        dv_prev[c][...] = dv_acc[pl.ds(c * rows, rows), :]

    @pl.when(head == last)
    def _():
        dq_out[...] = dq_acc[...].astype(BF16)
        dk_out[...] = dk_acc[pl.ds(chunk * rows, rows), :].astype(BF16)
        for c in range(chunk):
            dk_prev[c][...] = dk_acc[pl.ds(c * rows, rows), :]


def window_tile(lens_ref, query, key, row_begin, key_begin):
    logits = nt(query, key) * WIN_SCALE
    allowed = causal_allowed(lens_ref, row_begin, key_begin, query.shape[0], key.shape[0], WINDOW)
    logits = jnp.where(allowed, logits, NEGATIVE)
    exponent = jnp.exp(logits - jnp.max(logits, axis=1, keepdims=True))
    return exponent / jnp.sum(exponent, axis=1, keepdims=True)


def window_keys(current_ref, prev_ref, i, tile):
    if i > 0:
        return current_ref[pl.ds(i * tile - WINDOW, tile + WINDOW), :], i * tile - WINDOW
    if prev_ref is not None:
        return jnp.concatenate([prev_ref[...], current_ref[pl.ds(0, tile), :]], axis=0), -WINDOW
    return current_ref[pl.ds(0, tile), :], 0


def window_forward_kernel(chunk, rows, tile, lens_ref, q_ref, k_ref, v_ref, *refs):
    k_prev, v_prev = refs[:2] if chunk else (None, None)
    out_ref = refs[-1]
    for i in range(rows // tile):
        own = pl.ds(i * tile, tile)
        key, key_begin = window_keys(k_ref, k_prev, i, tile)
        value, _ = window_keys(v_ref, v_prev, i, tile)
        base = chunk * rows
        weights = window_tile(lens_ref, q_ref[own, :], key, base + i * tile, base + key_begin)
        out_ref[own, :] = nn(weights.astype(BF16), value).astype(BF16)


def window_backward_kernel(chunk, rows, tile, carried, lens_ref, q_ref, k_ref, v_ref, *refs):
    k_prev, v_prev = refs[:2] if chunk else (None, None)
    refs = refs[2:] if chunk else refs
    do_ref, refs = refs[0], refs[1:]
    if carried:
        dk_in, dv_in = refs[:2]
        refs = refs[2:]
    dq_out, dk_out, dv_out = refs[:3]
    dk_back, dv_back = refs[3:5] if chunk else (None, None)
    dk_acc, dv_acc = refs[-2:]
    dk_acc[...] = jnp.zeros_like(dk_acc)
    dv_acc[...] = jnp.zeros_like(dv_acc)
    if carried:
        dk_acc[pl.ds(rows, WINDOW), :] = dk_in[...]
        dv_acc[pl.ds(rows, WINDOW), :] = dv_in[...]
    for i in range(rows // tile):
        own = pl.ds(i * tile, tile)
        key, key_begin = window_keys(k_ref, k_prev, i, tile)
        value, _ = window_keys(v_ref, v_prev, i, tile)
        base = chunk * rows
        query = q_ref[own, :]
        grad = do_ref[own, :]
        weights = window_tile(lens_ref, query, key, base + i * tile, base + key_begin)
        weight_grad = nt(grad, value)
        delta = jnp.sum(weights * weight_grad, axis=1, keepdims=True)
        scores_grad = (weights * (weight_grad - delta)).astype(BF16)
        dq_out[own, :] = (nn(scores_grad, key) * WIN_SCALE).astype(BF16)
        keys = pl.ds(WINDOW + key_begin, key.shape[0])
        dk_acc[keys, :] += tn(scores_grad, query) * WIN_SCALE
        dv_acc[keys, :] += tn(weights.astype(BF16), grad)
    dk_out[...] = dk_acc[pl.ds(WINDOW, rows), :].astype(BF16)
    dv_out[...] = dv_acc[pl.ds(WINDOW, rows), :].astype(BF16)
    if chunk:
        dk_back[...] = dk_acc[pl.ds(0, WINDOW), :]
        dv_back[...] = dv_acc[pl.ds(0, WINDOW), :]


SMEM_SPEC = pl.BlockSpec(memory_space=pltpu.SMEM)
PARAMS = pltpu.CompilerParams(
    dimension_semantics=("arbitrary",), vmem_limit_bytes=VMEM_LIMIT
)


def cost(flops, moved):
    return pl.CostEstimate(flops=flops, bytes_accessed=moved, transcendentals=0)


def narrow_spec(rows, width):
    return pl.BlockSpec((rows, width), lambda h: (0, 0))


def head_spec(rows):
    return pl.BlockSpec((rows, HEAD_DIM), lambda h: (0, h))


def total_spec(rows):
    return pl.BlockSpec((1, rows, 1), lambda h: (h, 0, 0))


def linear_forward(chunk, lengths, query, keys, values):
    rows, width = query.shape
    heads = width // FEATURE_SIZE
    tile = min(256, rows)
    count = chunk + 1
    wide = heads * HEAD_DIM
    return pl.pallas_call(
        functools.partial(linear_forward_kernel, chunk, rows, tile),
        grid=(heads,),
        in_specs=[SMEM_SPEC, narrow_spec(rows, width)]
        + [narrow_spec(rows, width)] * count
        + [head_spec(rows)] * count,
        out_specs=[head_spec(rows), head_spec(rows), total_spec(rows)],
        out_shape=[
            jax.ShapeDtypeStruct((rows, wide), BF16),
            jax.ShapeDtypeStruct((rows, wide), F32),
            jax.ShapeDtypeStruct((heads, rows, 1), F32),
        ],
        compiler_params=PARAMS,
        cost_estimate=cost(4 * heads * rows * rows * count * HEAD_DIM, 8 * rows * wide),
        name="linear_forward",
    )(lengths, query, *keys, *values)


def linear_backward(chunk, lengths, query, keys, values, grad, mixed, total, carry):
    rows, width = query.shape
    heads = width // FEATURE_SIZE
    tile = min(256, rows)
    count = chunk + 1
    wide = heads * HEAD_DIM
    carry = list(carry)
    outs = pl.pallas_call(
        functools.partial(linear_backward_kernel, chunk, rows, tile, bool(carry)),
        grid=(heads,),
        in_specs=[SMEM_SPEC, narrow_spec(rows, width)]
        + [narrow_spec(rows, width)] * count
        + [head_spec(rows)] * count
        + [head_spec(rows), head_spec(rows), total_spec(rows)]
        + ([narrow_spec(rows, width), head_spec(rows)] if carry else []),
        out_specs=[narrow_spec(rows, width), narrow_spec(rows, width), head_spec(rows)]
        + [narrow_spec(rows, width)] * chunk
        + [head_spec(rows)] * chunk,
        out_shape=[
            jax.ShapeDtypeStruct((rows, width), BF16),
            jax.ShapeDtypeStruct((rows, width), BF16),
            jax.ShapeDtypeStruct((rows, wide), BF16),
        ]
        + [jax.ShapeDtypeStruct((rows, width), F32)] * chunk
        + [jax.ShapeDtypeStruct((rows, wide), F32)] * chunk,
        scratch_shapes=[
            pltpu.VMEM((rows, width), F32),
            pltpu.VMEM((count * rows, width), F32),
            pltpu.VMEM((count * rows, HEAD_DIM), F32),
        ],
        compiler_params=PARAMS,
        cost_estimate=cost(10 * heads * rows * rows * count * HEAD_DIM, 16 * rows * wide),
        name="linear_backward",
    )(lengths, query, *keys, *values, grad, mixed, total, *carry)
    return outs[:3], list(zip(outs[3 : 3 + chunk], outs[3 + chunk :]))


def prev_spec(rows):
    return pl.BlockSpec((WINDOW, HEAD_DIM), lambda h: (rows // WINDOW - 1, h))


def edge_spec():
    return pl.BlockSpec((WINDOW, HEAD_DIM), lambda h: (0, h))


def window_forward(chunk, lengths, query, key, value, before):
    rows, wide = query.shape
    heads = wide // HEAD_DIM
    tile = min(128, rows)
    return pl.pallas_call(
        functools.partial(window_forward_kernel, chunk, rows, tile),
        grid=(heads,),
        in_specs=[SMEM_SPEC] + [head_spec(rows)] * 3 + [prev_spec(rows)] * len(before),
        out_specs=head_spec(rows),
        out_shape=jax.ShapeDtypeStruct((rows, wide), BF16),
        compiler_params=PARAMS,
        cost_estimate=cost(4 * rows * 4 * HEAD_DIM * wide, 8 * rows * wide),
        name="window_forward",
    )(lengths, query, key, value, *before)


def window_backward(chunk, lengths, query, key, value, before, grad, carry):
    rows, wide = query.shape
    heads = wide // HEAD_DIM
    tile = min(128, rows)
    carry = list(carry)
    edges = 2 if chunk else 0
    outs = pl.pallas_call(
        functools.partial(window_backward_kernel, chunk, rows, tile, bool(carry)),
        grid=(heads,),
        in_specs=[SMEM_SPEC]
        + [head_spec(rows)] * 3
        + [prev_spec(rows)] * len(before)
        + [head_spec(rows)]
        + [edge_spec()] * len(carry),
        out_specs=[head_spec(rows)] * 3 + [edge_spec()] * edges,
        out_shape=[jax.ShapeDtypeStruct((rows, wide), BF16)] * 3
        + [jax.ShapeDtypeStruct((WINDOW, wide), F32)] * edges,
        scratch_shapes=[pltpu.VMEM((WINDOW + rows, HEAD_DIM), F32)] * 2,
        compiler_params=PARAMS,
        cost_estimate=cost(10 * rows * 4 * HEAD_DIM * wide, 16 * rows * wide),
        name="window_backward",
    )(lengths, query, key, value, *before, grad, *carry)
    return outs[:3], outs[3:]


def gather_norm_kernel(count, width, place_ref, own_ref, *refs):
    right, left = refs[: count - 1], refs[count - 1 : 2 * count - 2]
    gain_ref, normed_ref, inverse_ref, held = refs[2 * count - 2 :]
    place = place_ref[0]
    squares = jnp.zeros((own_ref.shape[0], 1), F32)
    for k in range(count):
        if k == 0:
            piece = own_ref[...].astype(F32)
        else:
            piece = jnp.where(place >= k, right[k - 1][...], left[count - k - 1][...]).astype(F32)
        held[k] = piece
        squares += jnp.sum(piece * piece, axis=1, keepdims=True)
    inverse = lax.rsqrt(squares * (1.0 / (count * width)) + EPSILON)
    inverse_ref[...] = inverse
    for k in range(count):
        block = lax.rem(place - k + count, count)
        columns = pl.ds(pl.multiple_of(block * width, width), width)
        gain = gain_ref[:, columns].astype(F32)
        normed_ref[:, columns] = (held[k] * inverse * gain).astype(BF16)


def gather_norm(pieces, gain_vector):
    own, right, left = pieces
    rows, width = own.shape
    count = len(right) + 1
    tile = min(128, rows)
    place = lax.axis_index("mp").astype(jnp.int32).reshape(1)
    piece_spec = pl.BlockSpec((tile, width), lambda t: (t, 0))
    return pl.pallas_call(
        functools.partial(gather_norm_kernel, count, width),
        grid=(rows // tile,),
        in_specs=[SMEM_SPEC]
        + [piece_spec] * (2 * count - 1)
        + [pl.BlockSpec((1, count * width), lambda t: (0, 0))],
        out_specs=[
            pl.BlockSpec((tile, count * width), lambda t: (t, 0)),
            pl.BlockSpec((tile, 1), lambda t: (t, 0)),
        ],
        out_shape=[
            jax.ShapeDtypeStruct((rows, count * width), BF16),
            jax.ShapeDtypeStruct((rows, 1), F32),
        ],
        scratch_shapes=[pltpu.VMEM((count, tile, width), F32)],
        compiler_params=PARAMS,
        cost_estimate=cost(8 * rows * width * count, 6 * rows * width * count),
        name="gather_norm",
    )(place, own, *right, *left, gain_vector.reshape(1, -1))


def gather_join_kernel(count, width, place_ref, own_ref, *refs):
    right, left = refs[: count - 1], refs[count - 1 : 2 * count - 2]
    out_ref = refs[-1]
    place = place_ref[0]
    for k in range(count):
        if k == 0:
            piece = own_ref[...]
        else:
            piece = jnp.where(place >= k, right[k - 1][...], left[count - k - 1][...])
        block = lax.rem(place - k + count, count)
        out_ref[:, pl.ds(pl.multiple_of(block * width, width), width)] = piece


def gather_join(pieces):
    own, right, left = pieces
    rows, width = own.shape
    count = len(right) + 1
    tile = min(128, rows)
    place = lax.axis_index("mp").astype(jnp.int32).reshape(1)
    piece_spec = pl.BlockSpec((tile, width), lambda t: (t, 0))
    return pl.pallas_call(
        functools.partial(gather_join_kernel, count, width),
        grid=(rows // tile,),
        in_specs=[SMEM_SPEC] + [piece_spec] * (2 * count - 1),
        out_specs=pl.BlockSpec((tile, count * width), lambda t: (t, 0)),
        out_shape=jax.ShapeDtypeStruct((rows, count * width), BF16),
        compiler_params=PARAMS,
        cost_estimate=cost(rows * width * count, 6 * rows * width * count),
        name="gather_join",
    )(place, own, *right, *left)


def hidden_kernel(gate_ref, upper_ref, after_ref, hidden_ref):
    gate = gate_ref[...]
    hidden_ref[...] = (gate * jax.nn.sigmoid(gate) * upper_ref[...]).astype(BF16)


def hidden_backward_kernel(gate_ref, upper_ref, grad_ref, dg_ref, du_ref, row_ref):
    gate, upper, grad = gate_ref[...], upper_ref[...], grad_ref[...]
    sigma = jax.nn.sigmoid(gate)
    gate_grad = (grad * upper * sigma * (1.0 + gate * (1.0 - sigma))).astype(BF16)
    upper_grad = (grad * gate * sigma).astype(BF16)
    dg_ref[...] = gate_grad
    du_ref[...] = upper_grad
    row_ref[...] = jnp.sum(
        gate_grad.astype(F32) * gate + upper_grad.astype(F32) * upper, axis=1, keepdims=True
    )


def row_tiles(rows, most):
    return max(t for t in range(16, most + 1, 16) if rows % t == 0)


def hidden_forward(gate, upper, after):
    rows, width = gate.shape
    tile = row_tiles(rows, 128)
    spec = pl.BlockSpec((tile, width), lambda t: (t, 0))
    return pl.pallas_call(
        hidden_kernel,
        grid=(rows // tile,),
        in_specs=[spec, spec, pl.BlockSpec(memory_space=pl.ANY)],
        out_specs=spec,
        out_shape=jax.ShapeDtypeStruct((rows, width), BF16),
        compiler_params=PARAMS,
        cost_estimate=cost(8 * rows * width, 10 * rows * width),
        name="hidden_forward",
    )(gate, upper, after)


def hidden_backward(gate, upper, grad):
    rows, width = gate.shape
    tile = row_tiles(rows, 128)
    spec = pl.BlockSpec((tile, width), lambda t: (t, 0))
    return pl.pallas_call(
        hidden_backward_kernel,
        grid=(rows // tile,),
        in_specs=[spec] * 3,
        out_specs=[spec, spec, pl.BlockSpec((tile, 1), lambda t: (t, 0))],
        out_shape=[jax.ShapeDtypeStruct((rows, width), BF16)] * 2
        + [jax.ShapeDtypeStruct((rows, 1), F32)],
        compiler_params=PARAMS,
        cost_estimate=cost(20 * rows * width, 16 * rows * width),
        name="hidden_backward",
    )(gate, upper, grad)


def pack_kernel(count, tile, grad_ref, normed_ref, extra_ref, out_ref, sum_ref):
    step = pl.program_id(0)
    rows = out_ref.shape[1] - PAD_ROWS
    width = out_ref.shape[2]
    grad = grad_ref[...]

    @pl.when(step == 0)
    def _():
        sum_ref[...] = jnp.zeros_like(sum_ref)

    sum_ref[...] += jnp.sum(grad * normed_ref[...].astype(F32), axis=0, keepdims=True)
    own = pl.ds(pl.multiple_of(step * tile, tile), tile)
    for j in range(count):
        out_ref[j, own, :] = grad[:, j * width : (j + 1) * width].astype(BF16)

    @pl.when(step == pl.num_programs(0) - 1)
    def _():
        line = lax.broadcasted_iota(jnp.int32, extra_ref.shape, 0)
        last = jnp.where(line == PAD_ROWS - 1, sum_ref[...], extra_ref[...]).astype(BF16)
        for j in range(count):
            out_ref[j, pl.ds(rows, PAD_ROWS), :] = last[:, j * width : (j + 1) * width]


def pack_rows(grad, normed, extra, count):
    rows, width = grad.shape
    tile = row_tiles(rows, 128)
    shape = (count, rows + PAD_ROWS, width // count)
    return pl.pallas_call(
        functools.partial(pack_kernel, count, tile),
        grid=(rows // tile,),
        in_specs=[
            pl.BlockSpec((tile, width), lambda t: (t, 0)),
            pl.BlockSpec((tile, width), lambda t: (t, 0)),
            pl.BlockSpec((PAD_ROWS, width), lambda t: (0, 0)),
        ],
        out_specs=pl.BlockSpec(shape, lambda t: (0, 0, 0)),
        out_shape=jax.ShapeDtypeStruct(shape, BF16),
        scratch_shapes=[pltpu.VMEM((1, width), F32)],
        compiler_params=PARAMS,
        cost_estimate=cost(4 * rows * width, 8 * rows * width),
        name="pack_rows",
    )(grad, normed, extra)


def block_product_kernel(left_ref, right_ref, out_ref):
    out_ref[0] = nn(left_ref[...], right_ref[...]).astype(BF16)


def block_product(left, right, count):
    rows, depth = left.shape
    width = right.shape[1] // count
    return pl.pallas_call(
        block_product_kernel,
        grid=(count,),
        in_specs=[
            pl.BlockSpec((rows, depth), lambda j: (0, 0)),
            pl.BlockSpec((depth, width), lambda j: (0, j)),
        ],
        out_specs=pl.BlockSpec((1, rows, width), lambda j: (j, 0, 0)),
        out_shape=jax.ShapeDtypeStruct((count, rows, width), BF16),
        compiler_params=PARAMS,
        cost_estimate=cost(2 * rows * depth * width * count, 2 * depth * width * count),
        name="block_product",
    )(left, right)


def line_gather(part):
    count = lax.axis_size("mp")
    right, left = [part], [part]
    for k in range(1, count):
        right.append(
            lax.ppermute(right[-1], "mp", [(j, j + 1) for j in range(k - 1, count - 1)])
        )
        left.append(lax.ppermute(left[-1], "mp", [(j, j - 1) for j in range(1, count - k + 1)]))
    return part, right[1:], left[1:]


def tie(value, *others):
    if not others:
        return value
    zero = sum(other[(0,) * other.ndim].astype(F32) * 0.0 for other in others)
    return value + zero.astype(value.dtype)


def block_at(blocks, index):
    count = blocks.shape[0]
    return lax.dynamic_index_in_dim(blocks, lax.rem(index + count, count), 0, keepdims=False)


def scatter_sum(blocks):
    count = lax.axis_size("mp")
    place = lax.axis_index("mp")
    right = left = None
    for k in range(1, count):
        to_right, to_left = block_at(blocks, place - k), block_at(blocks, place + k)
        if right is not None:
            to_right, to_left = to_right + right, to_left + left
        right = lax.ppermute(to_right, "mp", [(j, j + 1) for j in range(k)])
        left = lax.ppermute(to_left, "mp", [(j, j - 1) for j in range(count - k, count)])
    return block_at(blocks, place).astype(F32) + right.astype(F32) + left.astype(F32)


def scatter_sum_rows(partial_value, normed, row_values, *lines):
    rows, model_width = partial_value.shape
    count = lax.axis_size("mp")
    width = model_width // count
    places = rows // width
    extra = jnp.tile(row_values.reshape(places, width), (1, count))
    extra = jnp.concatenate([extra] + [line[None] for line in lines], axis=0)
    extra = jnp.pad(extra, ((0, PAD_ROWS - extra.shape[0]), (0, 0)))
    total = scatter_sum(pack_rows(partial_value, normed, extra, count))
    sums = [total[-1]] + [total[rows + places + j] for j in range(len(lines))]
    return total[:rows], total[rows : rows + places].reshape(rows), sums


def sum_groups(values, turn):
    count = lax.axis_size("dp")
    listed = [(j + turn) % count for j in range(count)]
    return [v.astype(F32) for v in lax.psum(tuple(values), "dp", axis_index_groups=[listed])]


def norm_backward(
    normed_grad, normed, row_values, lines, resid, inverse, gain_part, model_width, carried
):
    shard_grad, row_dot, sums = scatter_sum_rows(normed_grad, normed, row_values, *lines)
    normed_part = resid * inverse
    input_grad = carried + inverse * (
        shard_grad * gain_part - normed_part * (row_dot / model_width)[:, None]
    )
    return input_grad, sums


def row_product(*pairs):
    total = 0.0
    for left, right in pairs:
        total = total + jnp.sum(left.astype(F32) * right.astype(F32), axis=1)
    return total


def per_device(
    tokens,
    seq_lengths,
    gain_first,
    lin_query,
    lin_key,
    lin_value,
    lin_out,
    gain_second,
    win_query,
    win_key,
    win_value,
    win_out,
    gain_third,
    gate_weight,
    up_weight,
    down_weight,
    out_cotangent,
):
    row_count, width = tokens.shape
    count = lax.axis_size("mp")
    model_width = width * count
    rows = row_count // CHUNKS
    order = list(range(CHUNKS))
    offset = lax.axis_index("mp") * width
    places = jnp.arange(row_count, dtype=jnp.int32)
    validity = (places < seq_lengths[0, 0] + seq_lengths[0, 1]).astype(F32)
    valid = [validity[c * rows : (c + 1) * rows, None] for c in order]

    def cut(values):
        return [values[c * rows : (c + 1) * rows] for c in order]

    def join(values):
        return jnp.concatenate(values, axis=0) if len(values) > 1 else values[0]

    def part_of(gain):
        return lax.dynamic_slice_in_dim(gain, offset, width).astype(F32)

    blank = [None] * CHUNKS
    token_parts = cut(tokens)
    resid_zero = [t.astype(F32) for t in token_parts]
    cot_shard = [c.astype(F32) * v for c, v in zip(cut(out_cotangent), valid)]

    n1, r1, lq, lk, lv, lo, lo32, lden, b1, resid_one = [list(blank) for _ in range(10)]
    for c in order:
        n1[c], r1[c] = gather_norm(line_gather(token_parts[c]), gain_first)
        lq[c] = nn(n1[c], lin_query).astype(BF16)
        lk[c] = nn(n1[c], lin_key).astype(BF16)
        lv[c] = nn(n1[c], lin_value).astype(BF16)
        lo[c], lo32[c], lden[c] = linear_forward(
            c, seq_lengths, lq[c], lk[: c + 1], lv[: c + 1]
        )
        b1[c] = scatter_sum(block_product(lo[c], lin_out, count))
        resid_one[c] = resid_zero[c] + b1[c]
    cot_joined = lax.all_gather(
        join([c.astype(BF16) for c in cot_shard]), "mp", axis=1, tiled=True
    )
    cot_full = cut(cot_joined)
    n2, r2, wq, wk, wv, wo, b2, resid_two = [list(blank) for _ in range(8)]
    for c in order:
        n2[c], r2[c] = gather_norm(line_gather(resid_one[c].astype(BF16)), gain_second)
        wq[c] = nn(n2[c], win_query).astype(BF16)
        wk[c] = nn(n2[c], win_key).astype(BF16)
        wv[c] = nn(n2[c], win_value).astype(BF16)
        before = [wk[c - 1], wv[c - 1]] if c else []
        wo[c] = window_forward(c, seq_lengths, wq[c], wk[c], wv[c], before)
        b2[c] = scatter_sum(block_product(wo[c], win_out, count))
        resid_two[c] = resid_one[c] + b2[c]
    n3, r3, hid, dg, du, b3, resid_three, dn3, resid_two_grad = [list(blank) for _ in range(9)]
    gates, uppers = list(blank), list(blank)
    for c in order:
        n3[c], r3[c] = gather_norm(line_gather(resid_two[c].astype(BF16)), gain_third)
        gates[c] = nn(n3[c], gate_weight)
        uppers[c] = nn(n3[c], up_weight)
    def masked_squares(values):
        return sum(jnp.sum(v * jnp.sum(p * p, axis=1, keepdims=True)) for v, p in zip(valid, values))

    def stat_line(*values):
        block = jnp.pad(jnp.stack(values), (0, width - len(values)))
        return jnp.tile(block, count)

    stats = stat_line(masked_squares(resid_zero), masked_squares(b1), masked_squares(b2))
    sums_three, sums_two, sums_one = list(blank), list(blank), list(blank)
    for c in order:
        hid[c] = hidden_forward(gates[c], uppers[c], cot_joined)
    for c in reversed(order):
        hid_grad = nt(cot_full[c], down_weight)
        dg[c], du[c], row_values = hidden_backward(gates[c], uppers[c], hid_grad)
        dn3[c] = nt(dg[c], gate_weight) + nt(du[c], up_weight)
        resid_two_grad[c], sums_three[c] = norm_backward(
            dn3[c],
            n3[c],
            row_values[:, 0],
            (stats,),
            resid_two[c],
            r3[c],
            part_of(gain_third),
            model_width,
            cot_shard[c],
        )
    for c in order:
        b3[c] = scatter_sum(block_product(hid[c], down_weight, count))
        resid_three[c] = resid_two[c] + b3[c]
    ffn_normed, ffn_hid = join(n3), join(hid)
    ffn_grads = [
        tn(ffn_normed, join(dg)).astype(BF16),
        tn(ffn_normed, join(du)).astype(BF16),
        tn(ffn_hid, join(cot_full)).astype(BF16),
    ]
    ffn_sums = sum_groups(ffn_grads, 0)
    cot_two, wdq, wdk, wdv, dn2, resid_one_grad = [list(blank) for _ in range(6)]
    carry = []
    for c in reversed(order):
        shard = resid_two_grad[c] if c else tie(resid_two_grad[c], *ffn_grads)
        cot_two[c] = gather_join(line_gather(shard.astype(BF16)))
        mixed_grad = nt(cot_two[c], win_out).astype(BF16)
        before = [wk[c - 1], wv[c - 1]] if c else []
        (wdq[c], wdk[c], wdv[c]), carry = window_backward(
            c, seq_lengths, wq[c], wk[c], wv[c], before, mixed_grad, carry
        )
        dn2[c] = nt(wdq[c], win_query) + nt(wdk[c], win_key) + nt(wdv[c], win_value)
        resid_one_grad[c], sums_two[c] = norm_backward(
            dn2[c],
            n2[c],
            row_product((wdq[c], wq[c]), (wdk[c], wk[c]), (wdv[c], wv[c])),
            (),
            resid_one[c],
            r2[c],
            part_of(gain_second),
            model_width,
            resid_two_grad[c],
        )
    win_normed = join(n2)
    win_grads = [
        tn(win_normed, join(wdq)).astype(BF16),
        tn(win_normed, join(wdk)).astype(BF16),
        tn(win_normed, join(wdv)).astype(BF16),
        tn(join(wo), join(cot_two)).astype(BF16),
    ]
    win_sums = sum_groups(win_grads[:3] + [tie(win_grads[3], *ffn_sums)], 1)
    cot_one, ldq, ldk, ldv, dn1, tokens_grad = [list(blank) for _ in range(6)]
    pending = [[] for _ in order]
    for c in reversed(order):
        shard = resid_one_grad[c] if c else tie(resid_one_grad[c], *win_grads[:3])
        cot_one[c] = gather_join(line_gather(shard.astype(BF16)))
        mixed_grad = nt(cot_one[c], lin_out)
        carry = []
        if pending[c]:
            carry = [functools.reduce(jnp.add, [p[s] for p in pending[c]]) for s in (0, 1)]
        (ldq[c], ldk[c], ldv[c]), back = linear_backward(
            c,
            seq_lengths,
            lq[c],
            lk[: c + 1],
            lv[: c + 1],
            mixed_grad,
            lo32[c],
            lden[c],
            carry,
        )
        for earlier, pair in enumerate(back):
            pending[earlier].append(pair)
        dn1[c] = nt(ldq[c], lin_query) + nt(ldk[c], lin_key) + nt(ldv[c], lin_value)
        stats = stat_line(masked_squares(b3), masked_squares(resid_three))
        tokens_grad[c], sums_one[c] = norm_backward(
            dn1[c],
            n1[c],
            row_product((ldq[c], lq[c]), (ldk[c], lk[c]), (ldv[c], lv[c])),
            () if c else (stats,),
            resid_zero[c],
            r1[c],
            part_of(gain_first),
            model_width,
            resid_one_grad[c],
        )
    lin_normed = join(n1)
    lin_grads = [
        tn(lin_normed, join(ldq)).astype(BF16),
        tn(lin_normed, join(ldk)).astype(BF16),
        tn(lin_normed, join(ldv)).astype(BF16),
        tn(join(lo), join(cot_one)).astype(BF16),
    ]
    lin_sums = sum_groups(lin_grads[:3] + [tie(lin_grads[3], *win_sums)], 2)
    small = lax.psum(
        jnp.concatenate(
            [sum(part[0] for part in sums) for sums in (sums_one, sums_two, sums_three)]
            + [sums_three[0][1][:3], sums_one[0][1][:2], jnp.sum(validity)[None]]
        ),
        "dp",
    )
    gain_grads = [
        small[s * width : (s + 1) * width] / part_of(gain)
        for s, gain in enumerate((gain_first, gain_second, gain_third))
    ]
    rms_values = jnp.sqrt(small[3 * width : -1] / (small[-1] * model_width))
    return (
        join([v.astype(BF16) for v in resid_three]),
        join(tokens_grad),
        gain_grads[0],
        lin_sums[0],
        lin_sums[1],
        lin_sums[2],
        lin_sums[3],
        gain_grads[1],
        win_sums[0],
        win_sums[1],
        win_sums[2],
        win_sums[3],
        gain_grads[2],
        ffn_sums[0],
        ffn_sums[1],
        ffn_sums[2],
        rms_values,
    )


def solution(mesh):
    in_specs = (
        P("dp", "mp"),
        P("dp", None),
        P(),
        P(None, "mp"),
        P(None, "mp"),
        P(None, "mp"),
        P("mp", None),
        P(),
        P(None, "mp"),
        P(None, "mp"),
        P(None, "mp"),
        P("mp", None),
        P(),
        P(None, "mp"),
        P(None, "mp"),
        P("mp", None),
        P("dp", "mp"),
    )
    out_specs = (
        P("dp", "mp"),
        P("dp", "mp"),
        P("mp"),
        P(None, "mp"),
        P(None, "mp"),
        P(None, "mp"),
        P("mp", None),
        P("mp"),
        P(None, "mp"),
        P(None, "mp"),
        P(None, "mp"),
        P("mp", None),
        P("mp"),
        P(None, "mp"),
        P(None, "mp"),
        P("mp", None),
        P(),
    )
    return jax.shard_map(
        per_device, mesh=mesh, in_specs=in_specs, out_specs=out_specs, check_vma=False
    )
```

time: 2680 us -> 1260 us (0.47)
  waiting for transfers between devices: 2070 us -> 396 us
  starting transfers between devices: 0.54 us -> 327 us
  Pallas kernels: 0 us -> 118 us
  matrix products: 269 us -> 156 us
  blocking collectives: 89.8 us -> 12.6 us
  local copies, waits for them, and re-layouts: 131 us -> 77 us
  other arithmetic: 73.2 us -> 123 us
    reduce_scatter x6 -> x0, waiting for transfers between devices: 776 us -> none  [the longest x3 408 us: branch_total(): lax.psum_scatter(partial_value, 'mp', scatter_dimension=1, tiled=True)]
    all_gather x6 -> x1, waiting for transfers between devices: 660 us -> 0.02 us  [per_device(): lax.all_gather(join([c.astype(BF16) for c in cot_shard]), 'mp', axis=1, t...]
    psum x1 -> x3, waiting for transfers between devices: 634 us -> 110 us  [sum_groups(): lax.psum(tuple(values), 'dp', axis_index_groups=[listed])]
    ppermute x0 -> x132, starting transfers between devices: none -> 327 us  [the longest x36 144 us: scatter_sum(): right = lax.ppermute(to_right, 'mp', [(j, j + 1) for j in range(k)])]
    ppermute x0 -> x132, waiting for transfers between devices: none -> 287 us  [the longest x30 165 us: line_gather(): lax.ppermute(left[-1], 'mp', [(j, j - 1) for j in range(1, count - k + 1)])]
    pallas_call x0 -> x34, Pallas kernels: none -> 118 us  [the longest x6 18.7 us: gather_norm(): pl.pallas_call(functools.partial(gather_norm_kernel, count, width), grid=...]
    dot_general x63 -> x49, matrix products: 269 us -> 156 us  [the longest x22 62 us: nt(): lax.dot_general(left, right, (((1,), (1,)), ((), ())), preferred_element_...]
    psum x5 -> x1, blocking collectives: 89.8 us -> 12.6 us  [per_device(): lax.psum(jnp.concatenate([sum((part[0] for part in sums)) for sums in (su...]
  transfers between devices with their start and end apart: 13 -> 136, of which waited for: 13 -> 50; matrix products, arithmetic and copies ran while one was open for 5% -> 21% of each run, Pallas kernels for 0% -> 8%
where the time goes in v2:
time: 1260 us; the launch traced here: 1240 us
  waiting for transfers between devices  396 us (31%)
  starting transfers between devices  327 us (26%)
  matrix products  156 us (12%)
  other arithmetic  123 us (10%)
  Pallas kernels  118 us (9%)
  local copies, waits for them, and re-layouts  77 us (6%)
  between operations  35 us (3%)
  blocking collectives  12.6 us (1%)
    ppermute x30, waiting for transfers between devices, line_gather(): lax.ppermute(left[-1], 'mp', [(j, j - 1) for j in range(1, count - k + 1)])  165 us
    ppermute x36, starting transfers between devices, scatter_sum(): right = lax.ppermute(to_right, 'mp', [(j, j + 1) for j in range(k)])  144 us
    psum x3, waiting for transfers between devices, sum_groups(): lax.psum(tuple(values), 'dp', axis_index_groups=[listed])  110 us
    ppermute x30, starting transfers between devices, line_gather(): lax.ppermute(right[-1], 'mp', [(j, j + 1) for j in range(k - 1, count - 1)])  105 us
    ppermute x36, waiting for transfers between devices, scatter_sum(): right = lax.ppermute(to_right, 'mp', [(j, j + 1) for j in range(k)])  87.3 us
    dot_general x22, matrix products, nt(): lax.dot_general(left, right, (((1,), (1,)), ((), ())), preferred_element_...  62 us
    dot_general x11, matrix products, tn(): lax.dot_general(left, right, (((0,), (0,)), ((), ())), preferred_element_...  53.5 us
    unnamed x389, local copies, waits for them, and re-layouts  49.5 us
  transfers between devices with their start and end apart: 136, of which 50 were waited for; matrix products, arithmetic and copies ran while one was open for 21% of the time, Pallas kernels for 8%

profile of v2, /device:TPU:0, one launch (start us, length us, event | category | flops | bytes accessed | tf_op | source)
XLA Modules:
  0.0 1244.5 jit_solution(2123099078749328818)
XLA Ops:
  40.5 8.5 collective-permute-done.4.refs_4_
  51.7 8.5 collective-permute-done.40.refs_4_
  62.2 9.2 collective-permute-done.5.refs_5_
  166.6 9.1 collective-permute-done.8
  221.5 8.5 collective-permute-done.16.refs_4_
  243.2 19.1 %collective-permute-done.17.refs_5_ = bf16[512,512]{1,0:T(8,128)(2,1)} collective-permute-done((bf16[512,512]{1,0:T(8,128)(2,1)}, bf16[512,512]{1,0:T(8,128)(2,1)}, u32[]{:S(2)}, u32[]{:S(2)}) %collective-permute-start.17) | collective-permute-done | bytes 524320 | tf_op jit(solution)/shard_map/ppermute | solution.py:551
  283.0 24.1 %collective-permute-done.53.refs_5_ = bf16[512,512]{1,0:T(8,128)(2,1)S(1)} collective-permute-done((bf16[512,512]{1,0:T(8,128)(2,1)}, bf16[512,512]{1,0:T(8,128)(2,1)S(1)}, u32[]{:S(2)}, u32[]{:S(2)}) %collective-permute-start.53) | collective-permute-done | bytes 524320 | tf_op jit(solution)/shard_map/ppermute | solution.py:551
  328.0 16.7 %collective-permute-done.54 = bf16[512,512]{1,0:T(8,128)(2,1)S(1)} collective-permute-done((bf16[512,512]{1,0:T(8,128)(2,1)S(1)}, bf16[512,512]{1,0:T(8,128)(2,1)S(1)}, u32[]{:S(2)}, u32[]{:S(2)}) %collective-permute-start.54) | collective-permute-done | bytes 524320 | tf_op jit(solution)/shard_map/ppermute | solution.py:575
  386.5 14.9 %collective-permute-start.24 = (bf16[512,512]{1,0:T(8,128)(2,1)S(1)}, bf16[512,512]{1,0:T(8,128)(2,1)}, u32[]{:S(2)}, u32[]{:S(2)}) collective-permute-start(bf16[512,512]{1,0:T(8,128)(2,1)S(1)} %get-tuple-element.131.own_ref), channel_id=1, source_target_pairs={{0,1},{1,2},{2,3},{4,5},{5,6},{6,7},{8,9},{9,10},{10,11},{12,13},{... | collective-permute-start | bytes 1572872 | tf_op jit(solution)/shard_map/ppermute | solution.py:549
  405.7 8.6 collective-permute-start.60
  415.7 12.4 collective-permute-start.25
  448.3 11.6 collective-permute-done.64.refs_4_
  655.9 8.6 convolution_convert_fusion.1
  680.1 8.6 convolution_convert_fusion.2
  768.4 8.6 window_backward.2
  777.1 9.4 window_backward.3
  846.0 12.5 %collective-permute-start.110 = (bf16[528,512]{1,0:T(8,128)(2,1)}, bf16[528,512]{1,0:T(8,128)(2,1)}, u32[]{:S(2)}, u32[]{:S(2)}) collective-permute-start(bf16[528,512]{1,0:T(8,128)(2,1)} %get-tuple-element.161), channel_id=1, source_target_pairs={{0,1},{1,2},{2,3},{4,5},{5,6},{6,7},{8,9},{9,10},{10,11},{12,13},{... | collective-permute-start | bytes 1622024 | tf_op jit(solution)/shard_map/ppermute | solution.py:575
  872.5 9.4 collective-permute-done.113
  929.1 52.3 %all-reduce.15.cloned.1.call-done = (bf16[2048,1408]{1,0:T(8,128)(2,1)}, bf16[2048,1408]{1,0:T(8,128)(2,1)}, bf16[1408,2048]{1,0:T(8,128)(2,1)}) async-done(((bf16[2048,1408]{1,0:T(8,128)(2,1)}, bf16[2048,1408]{1,0:T(8,128)(2,1)}, bf16[1408,2048]{1,0:T(8,128)(2,1)}), (bf16[2048,1408]{1,0:T(8,128)(2,1)}, bf16[2048,1408]{1,0:T(8,128)(2,1)}, bf16[1408,2048]{1,0:T(8,128)(2,1)})) %all-reduce.15.cloned.1.call-update) | async-done | bytes 17301520 | tf_op jit(solution)/shard_map/psum | solution.py:596
  1008.7 12.1 linear_backward.2
  1094.6 30.9 %all-reduce.17.cloned.1.call-done = (bf16[2048,512]{1,0:T(8,128)(2,1)}, bf16[2048,512]{1,0:T(8,128)(2,1)}, bf16[2048,512]{1,0:T(8,128)(2,1)}, bf16[512,2048]{1,0:T(8,128)(2,1)}) async-done(((bf16[2048,512]{1,0:T(8,128)(2,1)}, bf16[2048,512]{1,0:T(8,128)(2,1)}, bf16[2048,512]{1,0:T(8,128)(2,1)}, bf16[512,2048]{1,0:T(8,128)(2,1)}), (bf16[2048,512]{1,0:T(8,128)(2,1)}, bf16[2048,512]{1,0:T(8,128)(2,1)}, ...) | async-done | bytes 8388624 | tf_op jit(solution)/shard_map/psum | solution.py:596
  1142.4 8.5 convert_element_type.562
  1170.2 12.6 %psum.84 = f32[1542]{0:T(1024)S(1)} all-reduce(f32[1542]{0:T(1024)S(1)} %concatenate.84), channel_id=1, replica_groups=mesh['dp'=8,'mp'=4] {'dp'}, use_global_device_ids=true, to_apply=%region_33.34 | all-reduce | flops 1542 | bytes 12336 | tf_op jit(solution)/shard_map/psum | solution.py:800
  1200.6 26.4 %all-reduce.19.cloned.1.call-done = (bf16[2048,64]{0,1:T(8,128)(2,1)}, bf16[2048,64]{0,1:T(8,128)(2,1)}, bf16[2048,512]{1,0:T(8,128)(2,1)}, bf16[512,2048]{1,0:T(8,128)(2,1)}) async-done(((bf16[2048,64]{0,1:T(8,128)(2,1)}, bf16[2048,64]{0,1:T(8,128)(2,1)}, bf16[2048,512]{1,0:T(8,128)(2,1)}, bf16[512,2048]{1,0:T(8,128)(2,1)}), (bf16[2048,64]{0,1:T(8,128)(2,1)}, bf16[2048,64]{0,1:T(8,128)(2,1)}, ...) | async-done | bytes 4718608 | tf_op jit(solution)/shard_map/psum | solution.py:596
  (871 shorter events, 858.6 us)
Async XLA Ops:
  7.2 420.9 %all-gather.2.cloned.1.call-start = ((), (), s32[]{:S(2)}) async-start(), calls=%async_computation | async-start | bytes 5242880 | tf_op jit(solution)/shard_map/all_gather | solution.py:671
  229.9 32.3 %collective-permute-start.17 = (bf16[512,512]{1,0:T(8,128)(2,1)}, bf16[512,512]{1,0:T(8,128)(2,1)}, u32[]{:S(2)}, u32[]{:S(2)}) collective-permute-start(bf16[512,512]{1,0:T(8,128)(2,1)} %collective-permute-done.16.refs_4_), channel_id=1, source_target_pairs={{1,0},{5,4},{9,8},{13,12},{17,16},{21,20},{25,24},{29,28}} | collective-permute-start | bytes 1572872 | tf_op jit(solution)/shard_map/ppermute | solution.py:551
  231.2 31.0 %collective-permute-start.14 = (bf16[512,512]{1,0:T(8,128)(2,1)}, bf16[512,512]{1,0:T(8,128)(2,1)}, u32[]{:S(2)}, u32[]{:S(2)}) collective-permute-start(bf16[512,512]{1,0:T(8,128)(2,1)} %collective-permute-done.13.refs_1_), channel_id=1, source_target_pairs={{2,3},{6,7},{10,11},{14,15},{18,19},{22,23},{26,27},{30,31}} | collective-permute-start | bytes 1572872 | tf_op jit(solution)/shard_map/ppermute | solution.py:549
  241.2 65.8 %collective-permute-start.53 = (bf16[512,512]{1,0:T(8,128)(2,1)}, bf16[512,512]{1,0:T(8,128)(2,1)S(1)}, u32[]{:S(2)}, u32[]{:S(2)}) collective-permute-start(bf16[512,512]{1,0:T(8,128)(2,1)} %collective-permute-done.52.refs_4_), channel_id=1, source_target_pairs={{1,0},{5,4},{9,8},{13,12},{17,16},{21,20},{25,24},{29,28}} | collective-permute-start | bytes 1572872 | tf_op jit(solution)/shard_map/ppermute | solution.py:551
  242.5 64.6 %collective-permute-start.50 = (bf16[512,512]{1,0:T(8,128)(2,1)}, bf16[512,512]{1,0:T(8,128)(2,1)S(1)}, u32[]{:S(2)}, u32[]{:S(2)}) collective-permute-start(bf16[512,512]{1,0:T(8,128)(2,1)} %collective-permute-done.49.refs_1_), channel_id=1, source_target_pairs={{2,3},{6,7},{10,11},{14,15},{18,19},{22,23},{26,27},{30,31}} | collective-permute-start | bytes 1572872 | tf_op jit(solution)/shard_map/ppermute | solution.py:549
  281.6 44.2 %collective-permute-start.18 = (bf16[512,512]{1,0:T(8,128)(2,1)S(1)}, bf16[512,512]{1,0:T(8,128)(2,1)S(1)}, u32[]{:S(2)}, u32[]{:S(2)}) collective-permute-start(bf16[512,512]{1,0:T(8,128)(2,1)S(1)} %get-tuple-element.175), channel_id=1, source_target_pairs={{0,1},{4,5},{8,9},{12,13},{16,17},{20,21},{24,25},{28,29}} | collective-permute-start | bytes 1572872 | tf_op jit(solution)/shard_map/ppermute | solution.py:575
  370.7 30.8 %collective-permute-start.56 = (bf16[512,512]{1,0:T(8,128)(2,1)}, bf16[512,512]{1,0:T(8,128)(2,1)}, u32[]{:S(2)}, u32[]{:S(2)}) collective-permute-start(bf16[512,512]{1,0:T(8,128)(2,1)} %get-tuple-element.181), channel_id=1, source_target_pairs={{0,1},{1,2},{2,3},{4,5},{5,6},{6,7},{8,9},{9,10},{10,11},{12,13},{... | collective-permute-start | bytes 1572872 | tf_op jit(solution)/shard_map/ppermute | solution.py:575
  404.5 32.1 %collective-permute-start.63 = (bf16[512,512]{1,0:T(8,128)(2,1)S(1)}, bf16[512,512]{1,0:T(8,128)(2,1)}, u32[]{:S(2)}, u32[]{:S(2)}) collective-permute-start(bf16[512,512]{1,0:T(8,128)(2,1)S(1)} %get-tuple-element.133.own_ref), channel_id=1, source_target_pairs={{1,0},{2,1},{3,2},{5,4},{6,5},{7,6},{9,8},{10,9},{11,10},{13,12},{... | collective-permute-start | bytes 1572872 | tf_op jit(solution)/shard_map/ppermute | solution.py:551
  405.7 32.1 %collective-permute-start.60 = (bf16[512,512]{1,0:T(8,128)(2,1)S(1)}, bf16[512,512]{1,0:T(8,128)(2,1)}, u32[]{:S(2)}, u32[]{:S(2)}) collective-permute-start(bf16[512,512]{1,0:T(8,128)(2,1)S(1)} %get-tuple-element.133.own_ref), channel_id=1, source_target_pairs={{0,1},{1,2},{2,3},{4,5},{5,6},{6,7},{8,9},{9,10},{10,11},{12,13},{... | collective-permute-start | bytes 1572872 | tf_op jit(solution)/shard_map/ppermute | solution.py:549
  510.1 37.9 %collective-permute-start.30 = (bf16[512,512]{1,0:T(8,128)(2,1)}, bf16[512,512]{1,0:T(8,128)(2,1)S(1)}, u32[]{:S(2)}, u32[]{:S(2)}) collective-permute-start(bf16[512,512]{1,0:T(8,128)(2,1)} %get-tuple-element.171), channel_id=1, source_target_pairs={{0,1},{4,5},{8,9},{12,13},{16,17},{20,21},{24,25},{28,29}} | collective-permute-start | bytes 1572872 | tf_op jit(solution)/shard_map/ppermute | solution.py:575
  511.7 48.6 %collective-permute-start.33 = (bf16[512,512]{1,0:T(8,128)(2,1)}, bf16[512,512]{1,0:T(8,128)(2,1)}, u32[]{:S(2)}, u32[]{:S(2)}) collective-permute-start(bf16[512,512]{1,0:T(8,128)(2,1)} %get-tuple-element.172), channel_id=1, source_target_pairs={{3,2},{7,6},{11,10},{15,14},{19,18},{23,22},{27,26},{31,30}} | collective-permute-start | bytes 1572872 | tf_op jit(solution)/shard_map/ppermute | solution.py:576
  524.1 39.9 %collective-permute-start.69 = (bf16[512,512]{1,0:T(8,128)(2,1)S(1)}, bf16[512,512]{1,0:T(8,128)(2,1)S(1)}, u32[]{:S(2)}, u32[]{:S(2)}) collective-permute-start(bf16[512,512]{1,0:T(8,128)(2,1)S(1)} %get-tuple-element.180), channel_id=1, source_target_pairs={{3,2},{7,6},{11,10},{15,14},{19,18},{23,22},{27,26},{31,30}} | collective-permute-start | bytes 1572872 | tf_op jit(solution)/shard_map/ppermute | solution.py:576
  692.5 288.8 %all-reduce.15.cloned.1.call-start = ((), (), s32[]{:S(2)}) async-start(), calls=%async_computation.1 | async-start | bytes 34603008 | tf_op jit(solution)/shard_map/psum | solution.py:596
  867.3 258.2 %all-reduce.17.cloned.1.call-start = ((), (), s32[]{:S(2)}) async-start(), calls=%async_computation.2 | async-start | bytes 16777216 | tf_op jit(solution)/shard_map/psum | solution.py:596
  914.9 72.0 %collective-permute-start.118 = (bf16[512,512]{1,0:T(8,128)(2,1)}, bf16[512,512]{1,0:T(8,128)(2,1)}, u32[]{:S(2)}, u32[]{:S(2)}) collective-permute-start(bf16[512,512]{1,0:T(8,128)(2,1)} %collective-permute-done.117.refs_3_), channel_id=1, source_target_pairs={{1,0},{2,1},{5,4},{6,5},{9,8},{10,9},{13,12},{14,13},{17,16},{18,1... | collective-permute-start | bytes 1572872 | tf_op jit(solution)/shard_map/ppermute | solution.py:551
  916.2 72.0 %collective-permute-start.115 = (bf16[512,512]{1,0:T(8,128)(2,1)}, bf16[512,512]{1,0:T(8,128)(2,1)}, u32[]{:S(2)}, u32[]{:S(2)}) collective-permute-start(bf16[512,512]{1,0:T(8,128)(2,1)} %collective-permute-done.114.refs_0_), channel_id=1, source_target_pairs={{1,2},{2,3},{5,6},{6,7},{9,10},{10,11},{13,14},{14,15},{17,18},{18... | collective-permute-start | bytes 1572872 | tf_op jit(solution)/shard_map/ppermute | solution.py:549
  924.0 72.1 %collective-permute-start.107 = (bf16[512,512]{1,0:T(8,128)(2,1)}, bf16[512,512]{1,0:T(8,128)(2,1)}, u32[]{:S(2)}, u32[]{:S(2)}) collective-permute-start(bf16[512,512]{1,0:T(8,128)(2,1)} %collective-permute-done.106.refs_4_), channel_id=1, source_target_pairs={{1,0},{5,4},{9,8},{13,12},{17,16},{21,20},{25,24},{29,28}} | collective-permute-start | bytes 1572872 | tf_op jit(solution)/shard_map/ppermute | solution.py:551
  925.3 70.8 %collective-permute-start.104 = (bf16[512,512]{1,0:T(8,128)(2,1)}, bf16[512,512]{1,0:T(8,128)(2,1)}, u32[]{:S(2)}, u32[]{:S(2)}) collective-permute-start(bf16[512,512]{1,0:T(8,128)(2,1)} %collective-permute-done.103.refs_1_), channel_id=1, source_target_pairs={{2,3},{6,7},{10,11},{14,15},{18,19},{22,23},{26,27},{30,31}} | collective-permute-start | bytes 1572872 | tf_op jit(solution)/shard_map/ppermute | solution.py:549
  995.8 231.2 %all-reduce.19.cloned.1.call-start = ((), (), s32[]{:S(2)}) async-start(), calls=%async_computation.3 | async-start | bytes 9437184 | tf_op jit(solution)/shard_map/psum | solution.py:596
  1043.9 38.3 %collective-permute-start.129 = (bf16[528,512]{1,0:T(8,128)(2,1)S(1)}, bf16[528,512]{1,0:T(8,128)(2,1)S(1)}, u32[]{:S(2)}, u32[]{:S(2)}) collective-permute-start(bf16[528,512]{1,0:T(8,128)(2,1)S(1)} %get-tuple-element.160), channel_id=1, source_target_pairs={{3,2},{7,6},{11,10},{15,14},{19,18},{23,22},{27,26},{31,30}} | collective-permute-start | bytes 1622024 | tf_op jit(solution)/shard_map/ppermute | solution.py:576
  1076.3 88.7 %collective-permute-start.122 = (bf16[528,512]{1,0:T(8,128)(2,1)}, bf16[528,512]{1,0:T(8,128)(2,1)}, u32[]{:S(2)}, u32[]{:S(2)}) collective-permute-start(bf16[528,512]{1,0:T(8,128)(2,1)} %get-tuple-element.145), channel_id=1, source_target_pairs={{0,1},{1,2},{2,3},{4,5},{5,6},{6,7},{8,9},{9,10},{10,11},{12,13},{... | collective-permute-start | bytes 1622024 | tf_op jit(solution)/shard_map/ppermute | solution.py:575
  1085.8 80.9 %collective-permute-start.128 = (bf16[528,512]{1,0:T(8,128)(2,1)}, bf16[528,512]{1,0:T(8,128)(2,1)}, u32[]{:S(2)}, u32[]{:S(2)}) collective-permute-start(bf16[528,512]{1,0:T(8,128)(2,1)} %get-tuple-element.157), channel_id=1, source_target_pairs={{0,1},{1,2},{2,3},{4,5},{5,6},{6,7},{8,9},{9,10},{10,11},{12,13},{... | collective-permute-start | bytes 1622024 | tf_op jit(solution)/shard_map/ppermute | solution.py:575
  1091.0 47.9 %collective-permute-start.130 = (bf16[528,512]{1,0:T(8,128)(2,1)}, bf16[528,512]{1,0:T(8,128)(2,1)}, u32[]{:S(2)}, u32[]{:S(2)}) collective-permute-start(bf16[528,512]{1,0:T(8,128)(2,1)} %get-tuple-element.158), channel_id=1, source_target_pairs={{2,1},{3,2},{6,5},{7,6},{10,9},{11,10},{14,13},{15,14},{18,17},{19... | collective-permute-start | bytes 1622024 | tf_op jit(solution)/shard_map/ppermute | solution.py:576
  1093.3 71.6 %collective-permute-start.125 = (bf16[528,512]{1,0:T(8,128)(2,1)}, bf16[528,512]{1,0:T(8,128)(2,1)}, u32[]{:S(2)}, u32[]{:S(2)}) collective-permute-start(bf16[528,512]{1,0:T(8,128)(2,1)} %bitcast_add_fusion.5), channel_id=1, source_target_pairs={{1,0},{2,1},{3,2},{5,4},{6,5},{7,6},{9,8},{10,9},{11,10},{13,12},{... | collective-permute-start | bytes 1622024 | tf_op jit(solution)/shard_map/ppermute | solution.py:576
  (297 other events, 4164.0 us)
Sparse Core Ops, SparseCore 0:
  234.5 106.5 all-gather.1
  754.0 227.3 all-reduce.14
  995.9 129.5 all-reduce.16
  1139.0 87.9 all-reduce.18

commit v3 on v2

--- a/solution.py
+++ b/solution.py
@@ -541,6 +541,185 @@
     )(left, right)
 
 
+def residual_kernel(place_ref, resid_ref, own_ref, right_ref, left_ref, *outs):
+    next_ref, low_ref, branch_ref, square_ref = outs
+    branch = own_ref[0].astype(F32) + right_ref[...].astype(F32) + left_ref[...].astype(F32)
+    total = resid_ref[...] + branch
+    next_ref[...] = total
+    low_ref[...] = total.astype(BF16)
+    branch_ref[...] = jnp.sum(branch * branch, axis=1, keepdims=True)
+    square_ref[...] = jnp.sum(total * total, axis=1, keepdims=True)
+
+
+def residual_add(place, resid, pieces):
+    blocks, right, left = pieces
+    rows, width = resid.shape
+    tile = row_tiles(rows, 256)
+    spec = pl.BlockSpec((tile, width), lambda t, p: (t, 0))
+    column = pl.BlockSpec((tile, 1), lambda t, p: (t, 0))
+    return pl.pallas_call(
+        residual_kernel,
+        grid_spec=pltpu.PrefetchScalarGridSpec(
+            num_scalar_prefetch=1,
+            grid=(rows // tile,),
+            in_specs=[
+                spec,
+                pl.BlockSpec((1, tile, width), lambda t, p: (p[0], t, 0)),
+                spec,
+                spec,
+            ],
+            out_specs=[spec, spec, column, column],
+        ),
+        out_shape=[
+            jax.ShapeDtypeStruct((rows, width), F32),
+            jax.ShapeDtypeStruct((rows, width), BF16),
+            jax.ShapeDtypeStruct((rows, 1), F32),
+            jax.ShapeDtypeStruct((rows, 1), F32),
+        ],
+        compiler_params=PARAMS,
+        cost_estimate=cost(8 * rows * width, 16 * rows * width),
+        name="residual_add",
+    )(place, resid, blocks, right, left)
+
+
+def gradient_kernel(rows, model_width, place_ref, *refs):
+    own_ref, right_ref, left_ref, carried_ref, resid_ref, inverse_ref, gain_ref = refs[:7]
+    next_ref, low_ref = refs[7:]
+    width = gain_ref.shape[1]
+    tile = row_tiles(rows, 128)
+    extra = pl.ds(rows, PAD_ROWS)
+    dots = own_ref[0, extra, :].astype(F32)
+    dots = dots + right_ref[extra, :].astype(F32) + left_ref[extra, :].astype(F32)
+    square = lax.broadcasted_iota(jnp.int32, (tile, tile), 0) == lax.broadcasted_iota(
+        jnp.int32, (tile, tile), 1
+    )
+    for step in range(rows // tile):
+        span = pl.ds(step * tile, tile)
+        line, begin = divmod(step * tile, width)
+        row = dots[line : line + 1, begin : begin + tile]
+        dot = jnp.sum(jnp.where(square, row, 0.0), axis=1, keepdims=True)
+        shard = own_ref[0, span, :].astype(F32)
+        shard = shard + right_ref[span, :].astype(F32) + left_ref[span, :].astype(F32)
+        inverse = inverse_ref[span, :]
+        normed = resid_ref[span, :] * inverse
+        grad = carried_ref[span, :] + inverse * (
+            shard * gain_ref[...] - normed * (dot * (1.0 / model_width))
+        )
+        next_ref[span, :] = grad
+        low_ref[span, :] = grad.astype(BF16)
+
+
+def gradient_step(place, pieces, carried, resid, inverse, gain_part, model_width):
+    blocks, right, left = pieces
+    rows, width = resid.shape
+    whole = lambda shape: pl.BlockSpec(shape, lambda t, p: (0,) * len(shape))
+    return pl.pallas_call(
+        functools.partial(gradient_kernel, rows, model_width),
+        grid_spec=pltpu.PrefetchScalarGridSpec(
+            num_scalar_prefetch=1,
+            grid=(1,),
+            in_specs=[
+                pl.BlockSpec((1, rows + PAD_ROWS, width), lambda t, p: (p[0], 0, 0)),
+                whole(right.shape),
+                whole(left.shape),
+                whole(carried.shape),
+                whole(resid.shape),
+                whole(inverse.shape),
+                whole((1, width)),
+            ],
+            out_specs=[whole(resid.shape), whole(resid.shape)],
+        ),
+        out_shape=[
+            jax.ShapeDtypeStruct((rows, width), F32),
+            jax.ShapeDtypeStruct((rows, width), BF16),
+        ],
+        compiler_params=PARAMS,
+        cost_estimate=cost(10 * rows * width, 20 * rows * width),
+        name="gradient_step",
+    )(place, blocks, right, left, carried, resid, inverse, gain_part.reshape(1, width))
+
+
+def split_kernel(widths, own_ref, *refs):
+    count = len(widths)
+    kept_ref, away_ref = refs[2 * count :]
+    begin = 0
+    for j, width in enumerate(widths):
+        kept_ref[:, begin : begin + width] = refs[j][...]
+        away_ref[:, begin : begin + width] = refs[count + j][...]
+        begin += width
+
+
+def split_rows(own, arrays):
+    rows = arrays[0].shape[0] // 2
+    widths = [a.shape[1] for a in arrays]
+    tile = row_tiles(rows, 256)
+    steps = rows // tile
+    kept = [pl.BlockSpec((tile, w), lambda t, o: (o[0] * steps + t, 0)) for w in widths]
+    away = [pl.BlockSpec((tile, w), lambda t, o: ((1 - o[0]) * steps + t, 0)) for w in widths]
+    spec = pl.BlockSpec((tile, sum(widths)), lambda t, o: (t, 0))
+    return pl.pallas_call(
+        functools.partial(split_kernel, widths),
+        grid_spec=pltpu.PrefetchScalarGridSpec(
+            num_scalar_prefetch=1,
+            grid=(steps,),
+            in_specs=kept + away,
+            out_specs=[spec, spec],
+        ),
+        out_shape=[jax.ShapeDtypeStruct((rows, sum(widths)), BF16)] * 2,
+        compiler_params=PARAMS,
+        cost_estimate=cost(rows * sum(widths), 8 * rows * sum(widths)),
+        name="split_rows",
+    )(own.reshape(1), *arrays, *arrays)
+
+
+def finish_kernel(widths, steps, own_ref, *refs):
+    sources, outs = refs[:4], refs[4:]
+    step = pl.program_id(0)
+    for kind in range(2):
+        for part in range(2):
+            half = own_ref[0] if kind == 0 else 1 - own_ref[0]
+            begin = (half * 2 + part) * steps
+
+            @pl.when((step >= begin) & (step < begin + steps))
+            def _(source=sources[2 * kind + part]):
+                first = 0
+                for out, width in zip(outs, widths):
+                    out[...] = source[:, first : first + width].astype(F32)
+                    first += width
+
+
+def finish_rows(own, held, arrived, widths):
+    rows = held[0].shape[0]
+    tile = row_tiles(rows, 128)
+    steps = rows // tile
+
+    def place(kind, part):
+        def index(t, o):
+            half = o[0] if kind == 0 else 1 - o[0]
+            return (jnp.clip(t - (half * 2 + part) * steps, 0, steps - 1), 0)
+
+        return index
+
+    specs = [
+        pl.BlockSpec((tile, sum(widths)), place(kind, part))
+        for kind in range(2)
+        for part in range(2)
+    ]
+    return pl.pallas_call(
+        functools.partial(finish_kernel, widths, steps),
+        grid_spec=pltpu.PrefetchScalarGridSpec(
+            num_scalar_prefetch=1,
+            grid=(4 * steps,),
+            in_specs=specs,
+            out_specs=[pl.BlockSpec((tile, w), lambda t, o: (t, 0)) for w in widths],
+        ),
+        out_shape=[jax.ShapeDtypeStruct((4 * rows, w), F32) for w in widths],
+        compiler_params=PARAMS,
+        cost_estimate=cost(rows * sum(widths), 24 * rows * sum(widths)),
+        name="finish_rows",
+    )(own.reshape(1), *held, *arrived)
+
+
 def line_gather(part):
     count = lax.axis_size("mp")
     right, left = [part], [part]
@@ -574,7 +753,7 @@
             to_right, to_left = to_right + right, to_left + left
         right = lax.ppermute(to_right, "mp", [(j, j + 1) for j in range(k)])
         left = lax.ppermute(to_left, "mp", [(j, j - 1) for j in range(count - k, count)])
-    return block_at(blocks, place).astype(F32) + right.astype(F32) + left.astype(F32)
+    return blocks, right, left
 
 
 def scatter_sum_rows(partial_value, normed, row_values, *lines):
@@ -585,26 +764,86 @@
     extra = jnp.tile(row_values.reshape(places, width), (1, count))
     extra = jnp.concatenate([extra] + [line[None] for line in lines], axis=0)
     extra = jnp.pad(extra, ((0, PAD_ROWS - extra.shape[0]), (0, 0)))
-    total = scatter_sum(pack_rows(partial_value, normed, extra, count))
-    sums = [total[-1]] + [total[rows + places + j] for j in range(len(lines))]
-    return total[:rows], total[rows : rows + places].reshape(rows), sums
+    pieces = scatter_sum(pack_rows(partial_value, normed, extra, count))
+    tails = [block_at(pieces[0], lax.axis_index("mp"))] + list(pieces[1:])
+    tail = sum(part[rows:].astype(F32) for part in tails)
+    sums = [tail[-1]] + [tail[places + j] for j in range(len(lines))]
+    return pieces, sums
 
 
 def sum_groups(values, turn):
     count = lax.axis_size("dp")
     listed = [(j + turn) % count for j in range(count)]
-    return [v.astype(F32) for v in lax.psum(tuple(values), "dp", axis_index_groups=[listed])]
+    return lax.psum(tuple(values), "dp", axis_index_groups=[listed])
+
+
+class GroupSum:
+    def __init__(self, arrays):
+        self.arrays = [array.astype(BF16) for array in arrays]
+        count = lax.axis_size("dp")
+        self.bits = count.bit_length() - 1
+        place = lax.axis_index("dp")
+        self.own = [lax.rem(place // 2**bit, 2) for bit in range(self.bits)]
+        self.orders = [list(range(1, self.bits)), list(range(1, self.bits))[::-1]]
+        self.plan = [self.first]
+        self.plan += [lambda *t, k=k: self.reduce(k, *t) for k in range(self.bits - 1)]
+        self.plan += [lambda *t, k=k: self.spread(k, *t) for k in reversed(range(self.bits - 1))]
+        self.plan += [self.last]
+
+    def swap(self, values, bit):
+        count = lax.axis_size("dp")
+        return lax.ppermute(values, "dp", [(j, j ^ (1 << bit)) for j in range(count)])
+
+    def half(self, values, which):
+        rows = values.shape[0] // 2
+        return lax.dynamic_slice_in_dim(values, which * rows, rows, 0)
+
+    def first(self, *after):
+        kept, away = split_rows(self.own[0], self.arrays)
+        total = kept + self.swap(tie(away, *after), 0)
+        rows = total.shape[0] // 2
+        self.parts = [total[:rows], total[rows:]]
+
+    def reduce(self, k, *after):
+        for p in range(2):
+            bit = self.orders[p][k]
+            own = self.own[bit]
+            arrived = self.swap(tie(self.half(self.parts[p], 1 - own), *after), bit)
+            self.parts[p] = self.half(self.parts[p], own) + arrived
+
+    def both(self, values, arrived, own):
+        low = jnp.where(own == 0, values, arrived)
+        high = jnp.where(own == 0, arrived, values)
+        return jnp.concatenate([low, high], axis=0)
+
+    def spread(self, k, *after):
+        for p in range(2):
+            bit = self.orders[p][k]
+            arrived = self.swap(tie(self.parts[p], *after), bit)
+            self.parts[p] = self.both(self.parts[p], arrived, self.own[bit])
+
+    def last(self, *after):
+        arrived = [self.swap(tie(part, *after), 0) for part in self.parts]
+        widths = [a.shape[1] for a in self.arrays]
+        self.parts = finish_rows(self.own[0], self.parts, arrived, widths)
+
+    def step(self, *after):
+        self.plan.pop(0)(*after)
+        return tuple(self.parts)
+
+    def result(self):
+        while self.plan:
+            self.step()
+        return self.parts
 
 
 def norm_backward(
     normed_grad, normed, row_values, lines, resid, inverse, gain_part, model_width, carried
 ):
-    shard_grad, row_dot, sums = scatter_sum_rows(normed_grad, normed, row_values, *lines)
-    normed_part = resid * inverse
-    input_grad = carried + inverse * (
-        shard_grad * gain_part - normed_part * (row_dot / model_width)[:, None]
-    )
-    return input_grad, sums
+    place = lax.axis_index("mp").astype(jnp.int32).reshape(1)
+    pieces, sums = scatter_sum_rows(normed_grad, normed, row_values, *lines)
+    grads = gradient_step(place, pieces, carried, resid, inverse, gain_part, model_width)
+    return grads, sums
 
 
 def row_product(*pairs):
@@ -653,57 +892,66 @@
         return lax.dynamic_slice_in_dim(gain, offset, width).astype(F32)
 
     blank = [None] * CHUNKS
+    low_one, low_two, low_three = list(blank), list(blank), list(blank)
+    low_two_grad, low_one_grad = list(blank), list(blank)
+    place = lax.axis_index("mp").astype(jnp.int32).reshape(1)
     token_parts = cut(tokens)
     resid_zero = [t.astype(F32) for t in token_parts]
     cot_shard = [c.astype(F32) * v for c, v in zip(cut(out_cotangent), valid)]
 
+    cot_low = join([c.astype(BF16) for c in cot_shard])
+    cot_joined = lax.all_gather(cot_low, "mp", axis=1, tiled=True)
+    cot_full = cut(cot_joined)
     n1, r1, lq, lk, lv, lo, lo32, lden, b1, resid_one = [list(blank) for _ in range(10)]
     for c in order:
-        n1[c], r1[c] = gather_norm(line_gather(token_parts[c]), gain_first)
+        part = tie(token_parts[c], r1[c - 1]) if c else token_parts[c]
+        n1[c], r1[c] = gather_norm(line_gather(part), gain_first)
         lq[c] = nn(n1[c], lin_query).astype(BF16)
         lk[c] = nn(n1[c], lin_key).astype(BF16)
         lv[c] = nn(n1[c], lin_value).astype(BF16)
         lo[c], lo32[c], lden[c] = linear_forward(
-            c, seq_lengths, lq[c], lk[: c + 1], lv[: c + 1]
+            c,
+            tie(seq_lengths, cot_joined) if c else seq_lengths,
+            lq[c],
+            lk[: c + 1],
+            lv[: c + 1],
         )
-        b1[c] = scatter_sum(block_product(lo[c], lin_out, count))
-        resid_one[c] = resid_zero[c] + b1[c]
-    cot_joined = lax.all_gather(
-        join([c.astype(BF16) for c in cot_shard]), "mp", axis=1, tiled=True
-    )
-    cot_full = cut(cot_joined)
+        pieces = scatter_sum(block_product(lo[c], lin_out, count))
+        resid_one[c], low_one[c], b1[c], _ = residual_add(place, resid_zero[c], pieces)
     n2, r2, wq, wk, wv, wo, b2, resid_two = [list(blank) for _ in range(8)]
     for c in order:
-        n2[c], r2[c] = gather_norm(line_gather(resid_one[c].astype(BF16)), gain_second)
+        n2[c], r2[c] = gather_norm(line_gather(low_one[c]), gain_second)
         wq[c] = nn(n2[c], win_query).astype(BF16)
         wk[c] = nn(n2[c], win_key).astype(BF16)
         wv[c] = nn(n2[c], win_value).astype(BF16)
         before = [wk[c - 1], wv[c - 1]] if c else []
         wo[c] = window_forward(c, seq_lengths, wq[c], wk[c], wv[c], before)
-        b2[c] = scatter_sum(block_product(wo[c], win_out, count))
-        resid_two[c] = resid_one[c] + b2[c]
+        pieces = scatter_sum(block_product(wo[c], win_out, count))
+        resid_two[c], low_two[c], b2[c], _ = residual_add(place, resid_one[c], pieces)
     n3, r3, hid, dg, du, b3, resid_three, dn3, resid_two_grad = [list(blank) for _ in range(9)]
     gates, uppers = list(blank), list(blank)
     for c in order:
-        n3[c], r3[c] = gather_norm(line_gather(resid_two[c].astype(BF16)), gain_third)
+        n3[c], r3[c] = gather_norm(line_gather(low_two[c]), gain_third)
         gates[c] = nn(n3[c], gate_weight)
         uppers[c] = nn(n3[c], up_weight)
-    def masked_squares(values):
-        return sum(jnp.sum(v * jnp.sum(p * p, axis=1, keepdims=True)) for v, p in zip(valid, values))
+    def masked(values):
+        return sum(jnp.sum(v * p) for v, p in zip(valid, values))
 
     def stat_line(*values):
         block = jnp.pad(jnp.stack(values), (0, width - len(values)))
         return jnp.tile(block, count)
 
-    stats = stat_line(masked_squares(resid_zero), masked_squares(b1), masked_squares(b2))
+    stats = stat_line(
+        masked([jnp.sum(x * x, axis=1, keepdims=True) for x in resid_zero]), masked(b1), masked(b2)
+    )
     sums_three, sums_two, sums_one = list(blank), list(blank), list(blank)
     for c in order:
-        hid[c] = hidden_forward(gates[c], uppers[c], cot_joined)
+        hid[c] = hidden_forward(gates[c], uppers[c], cot_joined if c else seq_lengths)
     for c in reversed(order):
         hid_grad = nt(cot_full[c], down_weight)
         dg[c], du[c], row_values = hidden_backward(gates[c], uppers[c], hid_grad)
         dn3[c] = nt(dg[c], gate_weight) + nt(du[c], up_weight)
-        resid_two_grad[c], sums_three[c] = norm_backward(
+        (resid_two_grad[c], low_two_grad[c]), sums_three[c] = norm_backward(
             dn3[c],
             n3[c],
             row_values[:, 0],
@@ -715,27 +963,28 @@
             cot_shard[c],
         )
     for c in order:
-        b3[c] = scatter_sum(block_product(hid[c], down_weight, count))
-        resid_three[c] = resid_two[c] + b3[c]
+        pieces = scatter_sum(block_product(hid[c], down_weight, count))
+        _, low_three[c], b3[c], resid_three[c] = residual_add(place, resid_two[c], pieces)
     ffn_normed, ffn_hid = join(n3), join(hid)
+    down_grad = tn(ffn_hid, cot_joined).astype(BF16)
+    down_sums = sum_groups([down_grad], 3)
     ffn_grads = [
         tn(ffn_normed, join(dg)).astype(BF16),
         tn(ffn_normed, join(du)).astype(BF16),
-        tn(ffn_hid, join(cot_full)).astype(BF16),
     ]
     ffn_sums = sum_groups(ffn_grads, 0)
     cot_two, wdq, wdk, wdv, dn2, resid_one_grad = [list(blank) for _ in range(6)]
     carry = []
     for c in reversed(order):
-        shard = resid_two_grad[c] if c else tie(resid_two_grad[c], *ffn_grads)
-        cot_two[c] = gather_join(line_gather(shard.astype(BF16)))
+        shard = tie(low_two_grad[c], *(ffn_grads if c == 0 else [down_grad]))
+        cot_two[c] = gather_join(line_gather(shard))
         mixed_grad = nt(cot_two[c], win_out).astype(BF16)
         before = [wk[c - 1], wv[c - 1]] if c else []
         (wdq[c], wdk[c], wdv[c]), carry = window_backward(
             c, seq_lengths, wq[c], wk[c], wv[c], before, mixed_grad, carry
         )
         dn2[c] = nt(wdq[c], win_query) + nt(wdk[c], win_key) + nt(wdv[c], win_value)
-        resid_one_grad[c], sums_two[c] = norm_backward(
+        (resid_one_grad[c], low_one_grad[c]), sums_two[c] = norm_backward(
             dn2[c],
             n2[c],
             row_product((wdq[c], wq[c]), (wdk[c], wk[c]), (wdv[c], wv[c])),
@@ -753,12 +1002,12 @@
         tn(win_normed, join(wdv)).astype(BF16),
         tn(join(wo), join(cot_two)).astype(BF16),
     ]
-    win_sums = sum_groups(win_grads[:3] + [tie(win_grads[3], *ffn_sums)], 1)
+    win_sums = sum_groups(win_grads, 1)
     cot_one, ldq, ldk, ldv, dn1, tokens_grad = [list(blank) for _ in range(6)]
     pending = [[] for _ in order]
     for c in reversed(order):
-        shard = resid_one_grad[c] if c else tie(resid_one_grad[c], *win_grads[:3])
-        cot_one[c] = gather_join(line_gather(shard.astype(BF16)))
+        shard = low_one_grad[c] if c else tie(low_one_grad[c], *win_grads)
+        cot_one[c] = gather_join(line_gather(shard))
         mixed_grad = nt(cot_one[c], lin_out)
         carry = []
         if pending[c]:
@@ -777,8 +1026,8 @@
         for earlier, pair in enumerate(back):
             pending[earlier].append(pair)
         dn1[c] = nt(ldq[c], lin_query) + nt(ldk[c], lin_key) + nt(ldv[c], lin_value)
-        stats = stat_line(masked_squares(b3), masked_squares(resid_three))
-        tokens_grad[c], sums_one[c] = norm_backward(
+        stats = stat_line(masked(b3), masked(resid_three))
+        (tokens_grad[c], _), sums_one[c] = norm_backward(
             dn1[c],
             n1[c],
             row_product((ldq[c], lq[c]), (ldk[c], lk[c]), (ldv[c], lv[c])),
@@ -796,7 +1045,7 @@
         tn(lin_normed, join(ldv)).astype(BF16),
         tn(join(lo), join(cot_one)).astype(BF16),
     ]
-    lin_sums = sum_groups(lin_grads[:3] + [tie(lin_grads[3], *win_sums)], 2)
+    lin_sums = sum_groups(lin_grads, 2)
     small = lax.psum(
         jnp.concatenate(
             [sum(part[0] for part in sums) for sums in (sums_one, sums_two, sums_three)]
@@ -809,8 +1058,12 @@
         for s, gain in enumerate((gain_first, gain_second, gain_third))
     ]
     rms_values = jnp.sqrt(small[3 * width : -1] / (small[-1] * model_width))
+    down_sums = [tie(v.astype(F32), wdq[0]) for v in down_sums]
+    ffn_sums = [tie(v.astype(F32), ldq[0]) for v in ffn_sums]
+    win_sums = [tie(v.astype(F32), tokens_grad[0]) for v in win_sums]
+    lin_sums = [v.astype(F32) for v in lin_sums]
     return (
-        join([v.astype(BF16) for v in resid_three]),
+        join(low_three),
         join(tokens_grad),
         gain_grads[0],
         lin_sums[0],
@@ -825,7 +1078,7 @@
         gain_grads[2],
         ffn_sums[0],
         ffn_sums[1],
-        ffn_sums[2],
+        down_sums[0],
         rms_values,
     )
 

time: 1260 us -> 1160 us (0.921)
  waiting for transfers between devices: 396 us -> 214 us
  starting transfers between devices: 327 us -> 376 us
  local copies, waits for them, and re-layouts: 77 us -> 105 us
  other arithmetic: 123 us -> 97.2 us
  matrix products: 156 us -> 175 us
  Pallas kernels: 118 us -> 131 us
    ppermute x36, starting transfers between devices: 144 us -> 220 us  [scatter_sum(): right = lax.ppermute(to_right, 'mp', [(j, j + 1) for j in range(k)])]
    psum x3 -> x4, waiting for transfers between devices: 110 us -> 33.7 us  [sum_groups(): return lax.psum(tuple(values), 'dp', axis_index_groups=[listed])]
    ppermute x30, waiting for transfers between devices: 165 us -> 93.6 us  [line_gather(): lax.ppermute(left[-1], 'mp', [(j, j - 1) for j in range(1, count - k + 1)])]
    convert_element_type x17 -> x5, other arithmetic: 56 us -> 13.1 us  [the longest x4 10.4 us: per_device(): lin_sums = [v.astype(F32) for v in lin_sums]]
    ppermute x36, waiting for transfers between devices: 34.1 us -> 4.16 us  [scatter_sum(): lax.ppermute(to_left, 'mp', [(j, j - 1) for j in range(count - k, count)])]
    ppermute x30, starting transfers between devices: 105 us -> 77.2 us  [line_gather(): lax.ppermute(right[-1], 'mp', [(j, j + 1) for j in range(k - 1, count - 1)])]
    add x7 -> x13, other arithmetic: 12.7 us -> 38.4 us  [the longest x11 36.8 us: tie(): return value + zero.astype(value.dtype)]
    unnamed x389 -> x489, local copies, waits for them, and re-layouts: 49.5 us -> 72.8 us
  transfers between devices with their start and end apart: 136 -> 137, of which waited for: 50 -> 36; matrix products, arithmetic and copies ran while one was open for 21% -> 26% of each run, Pallas kernels for 8% -> 10%
where the time goes in v3:
time: 1160 us; the launch traced here: 1150 us
  starting transfers between devices  376 us (32%)
  waiting for transfers between devices  214 us (18%)
  matrix products  175 us (15%)
  Pallas kernels  131 us (11%)
  local copies, waits for them, and re-layouts  105 us (9%)
  other arithmetic  97.2 us (8%)
  between operations  34.4 us (3%)
  blocking collectives  13.6 us (1%)
    ppermute x36, starting transfers between devices, scatter_sum(): right = lax.ppermute(to_right, 'mp', [(j, j + 1) for j in range(k)])  220 us
    ppermute x30, waiting for transfers between devices, line_gather(): lax.ppermute(left[-1], 'mp', [(j, j - 1) for j in range(1, count - k + 1)])  93.6 us
    ppermute x30, starting transfers between devices, line_gather(): lax.ppermute(right[-1], 'mp', [(j, j + 1) for j in range(k - 1, count - 1)])  77.2 us
    dot_general x22, matrix products, nt(): lax.dot_general(left, right, (((1,), (1,)), ((), ())), preferred_element_...  75.4 us
    ppermute x36, waiting for transfers between devices, scatter_sum(): right = lax.ppermute(to_right, 'mp', [(j, j + 1) for j in range(k)])  75 us
    unnamed x489, local copies, waits for them, and re-layouts  72.8 us
    dot_general x11, matrix products, tn(): lax.dot_general(left, right, (((0,), (0,)), ((), ())), preferred_element_...  59.9 us
    ppermute x30, starting transfers between devices, line_gather(): lax.ppermute(left[-1], 'mp', [(j, j - 1) for j in range(1, count - k + 1)])  39.8 us
  transfers between devices with their start and end apart: 137, of which 36 were waited for; matrix products, arithmetic and copies ran while one was open for 26% of the time, Pallas kernels for 10%

profile of v3, /device:TPU:0, one launch (start us, length us, event | category | flops | bytes accessed | tf_op | source)
XLA Modules:
  0.0 1146.2 jit_solution(5159943010189709302)
XLA Ops:
  15.4 10.0 collective-permute-done.3.refs_3_
  75.3 20.0 %collective-permute-done.6 = bf16[512,512]{1,0:T(8,128)(2,1)} collective-permute-done((bf16[512,512]{1,0:T(8,128)(2,1)}, bf16[512,512]{1,0:T(8,128)(2,1)}, u32[]{:S(2)}, u32[]{:S(2)}) %collective-permute-start.6) | collective-permute-done | bytes 524320 | tf_op jit(solution)/shard_map/ppermute | solution.py:754
  97.8 32.2 %collective-permute-start.7 = (bf16[512,512]{1,0:T(8,128)(2,1)}, bf16[512,512]{1,0:T(8,128)(2,1)}, u32[]{:S(2)}, u32[]{:S(2)}) collective-permute-start(bf16[512,512]{1,0:T(8,128)(2,1)} %get-tuple-element.216), channel_id=1, source_target_pairs={{0,1},{1,2},{4,5},{5,6},{8,9},{9,10},{12,13},{13,14},{16,17},{17,1... | collective-permute-start | bytes 1572872 | tf_op jit(solution)/shard_map/ppermute | solution.py:754
  142.0 8.4 collective-permute-done.7
  162.3 9.2 collective-permute-done.8.right_ref
  183.7 8.8 collective-permute-done.15.refs_3_
  194.6 9.2 collective-permute-done.41.refs_5_
  263.7 11.3 collective-permute-start.43
  347.8 8.8 collective-permute-done.27.refs_3_
  358.8 8.6 collective-permute-done.53.refs_5_
  398.0 11.0 collective-permute-start.55
  470.6 8.3 fusion.23.grad_ref
  650.9 11.0 convolution_convert_fusion.1
  680.0 8.6 convolution_convert_fusion.2
  737.0 8.6 window_backward.2
  756.5 9.4 window_backward.3
  804.5 10.4 collective-permute-start.109
  833.3 12.7 %collective-permute-start.110 = (bf16[528,512]{1,0:T(8,128)(2,1)S(1)}, bf16[528,512]{1,0:T(8,128)(2,1)S(1)}, u32[]{:S(2)}, u32[]{:S(2)}) collective-permute-start(bf16[528,512]{1,0:T(8,128)(2,1)S(1)} %bitcast_add_fusion.11), channel_id=1, source_target_pairs={{0,1},{1,2},{2,3},{4,5},{5,6},{6,7},{8,9},{9,10},{10,11},{12,13},{... | collective-permute-start | bytes 1622024 | tf_op jit(solution)/shard_map/ppermute | solution.py:754
  907.7 9.0 convert_add_fusion
  928.6 12.1 %linear_backward.2 = (bf16[512,64]{1,0:T(8,128)(2,1)S(1)}, bf16[512,64]{1,0:T(8,128)(2,1)S(1)}, bf16[512,512]{1,0:T(8,128)(2,1)S(1)}, f32[512,64]{1,0:T(8,128)S(1)}, f32[512,512]{1,0:T(8,128)S(1)}) custom-call(s32[1,3]{1,0:T(1,128)S(1)} %copy-done.171, bf16[512,64]{1,0:T(8,128)(2,1)S(1)} %copy-done.169, bf16[512,64]{1,0:T(8,128)(2,1)S(1)} %copy-done.131, ...), custom_call_target="tpu_custom_call" | custom-call | flops 2684354560 | bytes 4194304 | tf_op jit(solution)/shard_map/linear_backward/pallas_call | solution.py:264
  968.0 12.8 %collective-permute-start.126 = (bf16[528,512]{1,0:T(8,128)(2,1)}, bf16[528,512]{1,0:T(8,128)(2,1)}, u32[]{:S(2)}, u32[]{:S(2)}) collective-permute-start(bf16[528,512]{1,0:T(8,128)(2,1)} %get-tuple-element.190), channel_id=1, source_target_pairs={{0,1},{4,5},{8,9},{12,13},{16,17},{20,21},{24,25},{28,29}} | collective-permute-start | bytes 1622024 | tf_op jit(solution)/shard_map/ppermute | solution.py:754
  990.4 8.3 convert_add_fusion.1
  1054.3 13.6 %psum.84 = f32[1542]{0:T(1024)S(1)} all-reduce(f32[1542]{0:T(1024)S(1)} %concatenate.85), channel_id=1, replica_groups=mesh['dp'=8,'mp'=4] {'dp'}, use_global_device_ids=true, to_apply=%region_25.26 | all-reduce | flops 1542 | bytes 12336 | tf_op jit(solution)/shard_map/psum | solution.py:1049
  1095.2 33.7 %all-reduce.22.cloned.1.call-done = (bf16[2048,64]{0,1:T(8,128)(2,1)}, bf16[2048,64]{0,1:T(8,128)(2,1)}, bf16[2048,512]{1,0:T(8,128)(2,1)}, bf16[512,2048]{1,0:T(8,128)(2,1)}) async-done(((bf16[2048,64]{0,1:T(8,128)(2,1)}, bf16[2048,64]{0,1:T(8,128)(2,1)}, bf16[2048,512]{1,0:T(8,128)(2,1)}, bf16[512,2048]{1,0:T(8,128)(2,1)}), (bf16[2048,64]{0,1:T(8,128)(2,1)}, bf16[2048,64]{0,1:T(8,128)(2,1)}, ...) | async-done | bytes 4718608 | tf_op jit(solution)/shard_map/psum | solution.py:777
  (990 shorter events, 815.7 us)
Async XLA Ops:
  7.2 225.1 %all-gather.2.cloned.1.call-start = ((), (), s32[]{:S(2)}) async-start(), calls=%async_computation | async-start | bytes 5242880 | tf_op jit(solution)/shard_map/all_gather | solution.py:903
  97.8 52.6 %collective-permute-start.7 = (bf16[512,512]{1,0:T(8,128)(2,1)}, bf16[512,512]{1,0:T(8,128)(2,1)}, u32[]{:S(2)}, u32[]{:S(2)}) collective-permute-start(bf16[512,512]{1,0:T(8,128)(2,1)} %get-tuple-element.216), channel_id=1, source_target_pairs={{0,1},{1,2},{4,5},{5,6},{8,9},{9,10},{12,13},{13,14},{16,17},{17,1... | collective-permute-start | bytes 1572872 | tf_op jit(solution)/shard_map/ppermute | solution.py:754
  480.0 43.2 %collective-permute-start.31 = (bf16[512,512]{1,0:T(8,128)(2,1)}, bf16[512,512]{1,0:T(8,128)(2,1)S(1)}, u32[]{:S(2)}, u32[]{:S(2)}) collective-permute-start(bf16[512,512]{1,0:T(8,128)(2,1)} %get-tuple-element.200), channel_id=1, source_target_pairs={{0,1},{1,2},{4,5},{5,6},{8,9},{9,10},{12,13},{13,14},{16,17},{17,1... | collective-permute-start | bytes 1572872 | tf_op jit(solution)/shard_map/ppermute | solution.py:754
  529.4 31.2 %collective-permute-start.66 = (bf16[512,512]{1,0:T(8,128)(2,1)}, bf16[512,512]{1,0:T(8,128)(2,1)}, u32[]{:S(2)}, u32[]{:S(2)}) collective-permute-start(bf16[512,512]{1,0:T(8,128)(2,1)} %get-tuple-element.210), channel_id=1, source_target_pairs={{0,1},{4,5},{8,9},{12,13},{16,17},{20,21},{24,25},{28,29}} | collective-permute-start | bytes 1572872 | tf_op jit(solution)/shard_map/ppermute | solution.py:754
  624.9 282.8 %all-reduce.16.cloned.1.call-start = ((), (), s32[]{:S(2)}) async-start(), calls=%async_computation.1 | async-start | bytes 11534336 | tf_op jit(solution)/shard_map/psum | solution.py:777
  633.9 36.4 %collective-permute-start.89 = (bf16[528,512]{1,0:T(8,128)(2,1)S(1)}, bf16[528,512]{1,0:T(8,128)(2,1)S(1)}, u32[]{:S(2)}, u32[]{:S(2)}) collective-permute-start(bf16[528,512]{1,0:T(8,128)(2,1)S(1)} %get-tuple-element.195), channel_id=1, source_target_pairs={{1,0},{2,1},{3,2},{5,4},{6,5},{7,6},{9,8},{10,9},{11,10},{13,12},{... | collective-permute-start | bytes 1622024 | tf_op jit(solution)/shard_map/ppermute | solution.py:755
  643.5 26.9 %collective-permute-start.86 = (bf16[528,512]{1,0:T(8,128)(2,1)S(1)}, bf16[528,512]{1,0:T(8,128)(2,1)S(1)}, u32[]{:S(2)}, u32[]{:S(2)}) collective-permute-start(bf16[528,512]{1,0:T(8,128)(2,1)S(1)} %bitcast_add_fusion.19), channel_id=1, source_target_pairs={{0,1},{1,2},{2,3},{4,5},{5,6},{6,7},{8,9},{9,10},{10,11},{12,13},{... | collective-permute-start | bytes 1622024 | tf_op jit(solution)/shard_map/ppermute | solution.py:754
  662.7 29.6 %collective-permute-start.77 = (bf16[528,512]{1,0:T(8,128)(2,1)}, bf16[528,512]{1,0:T(8,128)(2,1)}, u32[]{:S(2)}, u32[]{:S(2)}) collective-permute-start(bf16[528,512]{1,0:T(8,128)(2,1)} %get-tuple-element.183), channel_id=1, source_target_pairs={{1,0},{2,1},{3,2},{5,4},{6,5},{7,6},{9,8},{10,9},{11,10},{13,12},{... | collective-permute-start | bytes 1622024 | tf_op jit(solution)/shard_map/ppermute | solution.py:755
  664.9 27.4 %collective-permute-start.74 = (bf16[528,512]{1,0:T(8,128)(2,1)}, bf16[528,512]{1,0:T(8,128)(2,1)}, u32[]{:S(2)}, u32[]{:S(2)}) collective-permute-start(bf16[528,512]{1,0:T(8,128)(2,1)} %bitcast_add_fusion.23), channel_id=1, source_target_pairs={{0,1},{1,2},{2,3},{4,5},{5,6},{6,7},{8,9},{9,10},{10,11},{12,13},{... | collective-permute-start | bytes 1622024 | tf_op jit(solution)/shard_map/ppermute | solution.py:754
  673.2 32.1 %collective-permute-start.93 = (bf16[512,512]{1,0:T(8,128)(2,1)}, bf16[512,512]{1,0:T(8,128)(2,1)}, u32[]{:S(2)}, u32[]{:S(2)}) collective-permute-start(bf16[512,512]{1,0:T(8,128)(2,1)} %broadcast_add_fusion.1.own_ref), channel_id=1, source_target_pairs={{1,0},{2,1},{3,2},{5,4},{6,5},{7,6},{9,8},{10,9},{11,10},{13,12},{... | collective-permute-start | bytes 1572872 | tf_op jit(solution)/shard_map/ppermute | solution.py:730
  674.6 32.0 %collective-permute-start.90 = (bf16[512,512]{1,0:T(8,128)(2,1)}, bf16[512,512]{1,0:T(8,128)(2,1)}, u32[]{:S(2)}, u32[]{:S(2)}) collective-permute-start(bf16[512,512]{1,0:T(8,128)(2,1)} %broadcast_add_fusion.1.own_ref), channel_id=1, source_target_pairs={{0,1},{1,2},{2,3},{4,5},{5,6},{6,7},{8,9},{9,10},{10,11},{12,13},{... | collective-permute-start | bytes 1572872 | tf_op jit(solution)/shard_map/ppermute | solution.py:728
  691.0 299.5 %all-reduce.18.cloned.1.call-start = ((), (), s32[]{:S(2)}) async-start(), calls=%async_computation.2 | async-start | bytes 23068672 | tf_op jit(solution)/shard_map/psum | solution.py:777
  804.5 28.7 %collective-permute-start.109 = (bf16[528,512]{1,0:T(8,128)(2,1)S(1)}, bf16[528,512]{1,0:T(8,128)(2,1)S(1)}, u32[]{:S(2)}, u32[]{:S(2)}) collective-permute-start(bf16[528,512]{1,0:T(8,128)(2,1)S(1)} %get-tuple-element.192), channel_id=1, source_target_pairs={{0,1},{1,2},{4,5},{5,6},{8,9},{9,10},{12,13},{13,14},{16,17},{17,1... | collective-permute-start | bytes 1622024 | tf_op jit(solution)/shard_map/ppermute | solution.py:754
  816.8 29.2 %collective-permute-start.97 = (bf16[528,512]{1,0:T(8,128)(2,1)S(1)}, bf16[528,512]{1,0:T(8,128)(2,1)S(1)}, u32[]{:S(2)}, u32[]{:S(2)}) collective-permute-start(bf16[528,512]{1,0:T(8,128)(2,1)S(1)} %get-tuple-element.180), channel_id=1, source_target_pairs={{0,1},{1,2},{4,5},{5,6},{8,9},{9,10},{12,13},{13,14},{16,17},{17,1... | collective-permute-start | bytes 1622024 | tf_op jit(solution)/shard_map/ppermute | solution.py:754
  830.6 27.2 %collective-permute-start.113 = (bf16[528,512]{1,0:T(8,128)(2,1)S(1)}, bf16[528,512]{1,0:T(8,128)(2,1)S(1)}, u32[]{:S(2)}, u32[]{:S(2)}) collective-permute-start(bf16[528,512]{1,0:T(8,128)(2,1)S(1)} %get-tuple-element.191), channel_id=1, source_target_pairs={{1,0},{2,1},{3,2},{5,4},{6,5},{7,6},{9,8},{10,9},{11,10},{13,12},{... | collective-permute-start | bytes 1622024 | tf_op jit(solution)/shard_map/ppermute | solution.py:755
  831.9 47.1 %collective-permute-start.101 = (bf16[528,512]{1,0:T(8,128)(2,1)}, bf16[528,512]{1,0:T(8,128)(2,1)}, u32[]{:S(2)}, u32[]{:S(2)}) collective-permute-start(bf16[528,512]{1,0:T(8,128)(2,1)} %get-tuple-element.179), channel_id=1, source_target_pairs={{1,0},{2,1},{3,2},{5,4},{6,5},{7,6},{9,8},{10,9},{11,10},{13,12},{... | collective-permute-start | bytes 1622024 | tf_op jit(solution)/shard_map/ppermute | solution.py:755
  846.9 32.1 %collective-permute-start.98 = (bf16[528,512]{1,0:T(8,128)(2,1)}, bf16[528,512]{1,0:T(8,128)(2,1)}, u32[]{:S(2)}, u32[]{:S(2)}) collective-permute-start(bf16[528,512]{1,0:T(8,128)(2,1)} %bitcast_add_fusion.15), channel_id=1, source_target_pairs={{0,1},{1,2},{2,3},{4,5},{5,6},{6,7},{8,9},{9,10},{10,11},{12,13},{... | collective-permute-start | bytes 1622024 | tf_op jit(solution)/shard_map/ppermute | solution.py:754
  860.3 33.3 %collective-permute-start.117 = (bf16[512,512]{1,0:T(8,128)(2,1)}, bf16[512,512]{1,0:T(8,128)(2,1)}, u32[]{:S(2)}, u32[]{:S(2)}) collective-permute-start(bf16[512,512]{1,0:T(8,128)(2,1)} %get-tuple-element.133.own_ref), channel_id=1, source_target_pairs={{1,0},{2,1},{3,2},{5,4},{6,5},{7,6},{9,8},{10,9},{11,10},{13,12},{... | collective-permute-start | bytes 1572872 | tf_op jit(solution)/shard_map/ppermute | solution.py:730
  861.7 33.1 %collective-permute-start.114 = (bf16[512,512]{1,0:T(8,128)(2,1)}, bf16[512,512]{1,0:T(8,128)(2,1)}, u32[]{:S(2)}, u32[]{:S(2)}) collective-permute-start(bf16[512,512]{1,0:T(8,128)(2,1)} %get-tuple-element.133.own_ref), channel_id=1, source_target_pairs={{0,1},{1,2},{2,3},{4,5},{5,6},{6,7},{8,9},{9,10},{10,11},{12,13},{... | collective-permute-start | bytes 1572872 | tf_op jit(solution)/shard_map/ppermute | solution.py:728
  876.4 206.7 %all-reduce.20.cloned.1.call-start = ((), (), s32[]{:S(2)}) async-start(), calls=%async_computation.3 | async-start | bytes 16777216 | tf_op jit(solution)/shard_map/psum | solution.py:777
  899.5 229.5 %all-reduce.22.cloned.1.call-start = ((), (), s32[]{:S(2)}) async-start(), calls=%async_computation.4 | async-start | bytes 9437184 | tf_op jit(solution)/shard_map/psum | solution.py:777
  966.5 47.7 %collective-permute-start.129 = (bf16[528,512]{1,0:T(8,128)(2,1)}, bf16[528,512]{1,0:T(8,128)(2,1)}, u32[]{:S(2)}, u32[]{:S(2)}) collective-permute-start(bf16[528,512]{1,0:T(8,128)(2,1)} %get-tuple-element.189), channel_id=1, source_target_pairs={{3,2},{7,6},{11,10},{15,14},{19,18},{23,22},{27,26},{31,30}} | collective-permute-start | bytes 1622024 | tf_op jit(solution)/shard_map/ppermute | solution.py:755
  968.0 56.3 %collective-permute-start.126 = (bf16[528,512]{1,0:T(8,128)(2,1)}, bf16[528,512]{1,0:T(8,128)(2,1)}, u32[]{:S(2)}, u32[]{:S(2)}) collective-permute-start(bf16[528,512]{1,0:T(8,128)(2,1)} %get-tuple-element.190), channel_id=1, source_target_pairs={{0,1},{4,5},{8,9},{12,13},{16,17},{20,21},{24,25},{28,29}} | collective-permute-start | bytes 1622024 | tf_op jit(solution)/shard_map/ppermute | solution.py:754
  988.4 27.7 %collective-permute-start.120 = (bf16[528,512]{1,0:T(8,128)(2,1)}, bf16[528,512]{1,0:T(8,128)(2,1)}, u32[]{:S(2)}, u32[]{:S(2)}) collective-permute-start(bf16[528,512]{1,0:T(8,128)(2,1)} %get-tuple-element.178), channel_id=1, source_target_pairs={{0,1},{4,5},{8,9},{12,13},{16,17},{20,21},{24,25},{28,29}} | collective-permute-start | bytes 1622024 | tf_op jit(solution)/shard_map/ppermute | solution.py:754
  (350 other events, 4523.1 us)
Sparse Core Ops, SparseCore 0:
  46.7 100.9 all-gather.1
  629.6 99.6 all-reduce.15
  734.1 161.2 all-reduce.17
  900.3 131.9 all-reduce.19
  1042.5 86.3 all-reduce.21

commit v4 on v3

--- a/solution.py
+++ b/solution.py
@@ -302,7 +302,7 @@
 def window_forward(chunk, lengths, query, key, value, before):
     rows, wide = query.shape
     heads = wide // HEAD_DIM
-    tile = min(128, rows)
+    tile = min(256, rows)
     return pl.pallas_call(
         functools.partial(window_forward_kernel, chunk, rows, tile),
         grid=(heads,),
@@ -318,7 +318,7 @@
 def window_backward(chunk, lengths, query, key, value, before, grad, carry):
     rows, wide = query.shape
     heads = wide // HEAD_DIM
-    tile = min(128, rows)
+    tile = min(256, rows)
     carry = list(carry)
     edges = 2 if chunk else 0
     outs = pl.pallas_call(
@@ -911,7 +911,7 @@
         lv[c] = nn(n1[c], lin_value).astype(BF16)
         lo[c], lo32[c], lden[c] = linear_forward(
             c,
-            tie(seq_lengths, cot_joined) if c else seq_lengths,
+            seq_lengths,
             lq[c],
             lk[: c + 1],
             lv[: c + 1],
@@ -925,7 +925,8 @@
         wk[c] = nn(n2[c], win_key).astype(BF16)
         wv[c] = nn(n2[c], win_value).astype(BF16)
         before = [wk[c - 1], wv[c - 1]] if c else []
-        wo[c] = window_forward(c, seq_lengths, wq[c], wk[c], wv[c], before)
+        spans = seq_lengths if c else tie(seq_lengths, cot_joined)
+        wo[c] = window_forward(c, spans, wq[c], wk[c], wv[c], before)
         pieces = scatter_sum(block_product(wo[c], win_out, count))
         resid_two[c], low_two[c], b2[c], _ = residual_add(place, resid_one[c], pieces)
     n3, r3, hid, dg, du, b3, resid_three, dn3, resid_two_grad = [list(blank) for _ in range(9)]
@@ -963,8 +964,13 @@
             cot_shard[c],
         )
     for c in order:
-        pieces = scatter_sum(block_product(hid[c], down_weight, count))
-        _, low_three[c], b3[c], resid_three[c] = residual_add(place, resid_two[c], pieces)
+        partial_sum = nn(hid[c], down_weight).astype(BF16)
+        branch = lax.psum_scatter(partial_sum, "mp", scatter_dimension=1, tiled=True)
+        branch = branch.astype(F32)
+        total = resid_two[c] + branch
+        low_three[c] = total.astype(BF16)
+        b3[c] = jnp.sum(branch * branch, axis=1, keepdims=True)
+        resid_three[c] = jnp.sum(total * total, axis=1, keepdims=True)
     ffn_normed, ffn_hid = join(n3), join(hid)
     down_grad = tn(ffn_hid, cot_joined).astype(BF16)
     down_sums = sum_groups([down_grad], 3)

time: 1160 us -> 1140 us (0.983)
  starting transfers between devices: 376 us -> 347 us
  waiting for transfers between devices: 214 us -> 239 us
  Pallas kernels: 131 us -> 113 us
    ppermute x36 -> x30, starting transfers between devices: 220 us -> 192 us  [scatter_sum(): right = lax.ppermute(to_right, 'mp', [(j, j + 1) for j in range(k)])]
    ppermute x36 -> x30, waiting for transfers between devices: 4.16 us -> 30.9 us  [scatter_sum(): lax.ppermute(to_left, 'mp', [(j, j - 1) for j in range(count - k, count)])]
    ppermute x36 -> x30, waiting for transfers between devices: 75 us -> 55.2 us  [scatter_sum(): right = lax.ppermute(to_right, 'mp', [(j, j + 1) for j in range(k)])]
    dot_general x16 -> x18, matrix products: 39.6 us -> 47.7 us  [nn(): lax.dot_general(left, right, (((1,), (0,)), ((), ())), preferred_element_...]
    ppermute x36 -> x30, starting transfers between devices: 38.9 us -> 33.5 us  [scatter_sum(): lax.ppermute(to_left, 'mp', [(j, j - 1) for j in range(count - k, count)])]
    add x36 -> x30, other arithmetic: 28 us -> 23.2 us  [scatter_sum(): to_right, to_left = (to_right + right, to_left + left)]
    unnamed x489 -> x483, local copies, waits for them, and re-layouts: 72.8 us -> 68.8 us
  transfers between devices with their start and end apart: 137 -> 127, of which waited for: 36 -> 31; matrix products, arithmetic and copies ran while one was open for 26% -> 26% of each run, Pallas kernels for 10% -> 10%
where the time goes in v4:
time: 1140 us; the launch traced here: 1130 us
  starting transfers between devices  347 us (30%)
  waiting for transfers between devices  239 us (21%)
  matrix products  182 us (16%)
  Pallas kernels  113 us (10%)
  local copies, waits for them, and re-layouts  101 us (9%)
  other arithmetic  94.8 us (8%)
  between operations  34.9 us (3%)
  blocking collectives  13.6 us (1%)
    ppermute x30, starting transfers between devices, scatter_sum(): right = lax.ppermute(to_right, 'mp', [(j, j + 1) for j in range(k)])  192 us
    ppermute x30, waiting for transfers between devices, line_gather(): lax.ppermute(left[-1], 'mp', [(j, j - 1) for j in range(1, count - k + 1)])  103 us
    ppermute x30, starting transfers between devices, line_gather(): lax.ppermute(right[-1], 'mp', [(j, j + 1) for j in range(k - 1, count - 1)])  80.7 us
    dot_general x22, matrix products, nt(): lax.dot_general(left, right, (((1,), (1,)), ((), ())), preferred_element_...  73.9 us
    unnamed x483, local copies, waits for them, and re-layouts  68.8 us
    dot_general x11, matrix products, tn(): lax.dot_general(left, right, (((0,), (0,)), ((), ())), preferred_element_...  60.8 us
    ppermute x30, waiting for transfers between devices, scatter_sum(): right = lax.ppermute(to_right, 'mp', [(j, j + 1) for j in range(k)])  55.2 us
    dot_general x18, matrix products, nn(): lax.dot_general(left, right, (((1,), (0,)), ((), ())), preferred_element_...  47.7 us
  transfers between devices with their start and end apart: 127, of which 31 were waited for; matrix products, arithmetic and copies ran while one was open for 26% of the time, Pallas kernels for 10%

profile of v4, /device:TPU:0, one launch (start us, length us, event | category | flops | bytes accessed | tf_op | source)
XLA Modules:
  0.0 1125.0 jit_solution(3968747308785363370)
XLA Ops:
  15.4 10.0 collective-permute-done.3.refs_3_
  28.9 11.5 %collective-permute-done.4.refs_4_ = bf16[512,512]{1,0:T(8,128)(2,1)} collective-permute-done((bf16[512,512]{1,0:T(8,128)(2,1)S(1)}, bf16[512,512]{1,0:T(8,128)(2,1)}, u32[]{:S(2)}, u32[]{:S(2)}) %collective-permute-start.4) | collective-permute-done | bytes 524320 | tf_op jit(solution)/shard_map/ppermute | solution.py:730
  101.0 11.0 collective-permute-start.7
  147.7 23.7 %collective-permute-done.11.left_ref = bf16[512,512]{1,0:T(8,128)(2,1)S(1)} collective-permute-done((bf16[512,512]{1,0:T(8,128)(2,1)}, bf16[512,512]{1,0:T(8,128)(2,1)S(1)}, u32[]{:S(2)}, u32[]{:S(2)}) %collective-permute-start.11) | collective-permute-done | bytes 524320 | tf_op jit(solution)/shard_map/ppermute | solution.py:755
  171.4 10.3 collective-permute-done.8.right_ref
  199.3 13.4 %collective-permute-done.12.refs_0_ = bf16[512,512]{1,0:T(8,128)(2,1)S(1)} collective-permute-done((bf16[512,512]{1,0:T(8,128)(2,1)S(1)}, bf16[512,512]{1,0:T(8,128)(2,1)S(1)}, u32[]{:S(2)}, u32[]{:S(2)}) %collective-permute-start.12) | collective-permute-done | bytes 524320 | tf_op jit(solution)/shard_map/ppermute | solution.py:728
  214.9 13.7 %collective-permute-done.37 = bf16[512,512]{1,0:T(8,128)(2,1)S(1)} collective-permute-done((bf16[512,512]{1,0:T(8,128)(2,1)S(1)}, bf16[512,512]{1,0:T(8,128)(2,1)S(1)}, u32[]{:S(2)}, u32[]{:S(2)}) %collective-permute-start.37) | collective-permute-done | bytes 524320 | tf_op jit(solution)/shard_map/ppermute | solution.py:754
  303.3 15.4 %collective-permute-start.19 = (bf16[512,512]{1,0:T(8,128)(2,1)S(1)}, bf16[512,512]{1,0:T(8,128)(2,1)S(1)}, u32[]{:S(2)}, u32[]{:S(2)}) collective-permute-start(bf16[512,512]{1,0:T(8,128)(2,1)S(1)} %get-tuple-element.192), channel_id=1, source_target_pairs={{0,1},{1,2},{4,5},{5,6},{8,9},{9,10},{12,13},{13,14},{16,17},{17,1... | collective-permute-start | bytes 1572872 | tf_op jit(solution)/shard_map/ppermute | solution.py:754
  374.6 10.2 collective-permute-start.50
  394.6 8.4 collective-permute-start.54
  430.0 23.7 %collective-permute-done.58.refs_4_ = bf16[512,512]{1,0:T(8,128)(2,1)} collective-permute-done((bf16[512,512]{1,0:T(8,128)(2,1)}, bf16[512,512]{1,0:T(8,128)(2,1)}, u32[]{:S(2)}, u32[]{:S(2)}) %collective-permute-start.58) | collective-permute-done | bytes 524320 | tf_op jit(solution)/shard_map/ppermute | solution.py:730
  464.1 14.7 %collective-permute-done.59.refs_5_ = bf16[512,512]{1,0:T(8,128)(2,1)S(1)} collective-permute-done((bf16[512,512]{1,0:T(8,128)(2,1)}, bf16[512,512]{1,0:T(8,128)(2,1)S(1)}, u32[]{:S(2)}, u32[]{:S(2)}) %collective-permute-start.59) | collective-permute-done | bytes 524320 | tf_op jit(solution)/shard_map/ppermute | solution.py:730
  526.3 8.7 fusion.96
  610.5 13.2 %collective-permute-start.61 = (bf16[528,512]{1,0:T(8,128)(2,1)S(1)}, bf16[528,512]{1,0:T(8,128)(2,1)S(1)}, u32[]{:S(2)}, u32[]{:S(2)}) collective-permute-start(bf16[528,512]{1,0:T(8,128)(2,1)S(1)} %get-tuple-element.176), channel_id=1, source_target_pairs={{0,1},{1,2},{4,5},{5,6},{8,9},{9,10},{12,13},{13,14},{16,17},{17,1... | collective-permute-start | bytes 1622024 | tf_op jit(solution)/shard_map/ppermute | solution.py:754
  632.0 11.4 %convolution_convert_fusion.1 = bf16[2048,1408]{1,0:T(8,128)(2,1)} fusion(bf16[1024,2048]{1,0:T(8,128)(2,1)} %constant_dynamic-update-slice_fusion, bf16[512,1408]{1,0:T(8,128)(2,1)S(1)} %copy-done.176, bf16[512,1408]{1,0:T(8,128)(2,1)S(1)} %copy-done.173), kind=kOutput, calls=%fused_computation.4 | convolution fusion | flops 5914230784 | bytes 12845056 | tf_op jit(solution)/shard_map/dot_general | solution.py:33
  661.8 8.6 convolution_convert_fusion.2
  783.6 10.6 collective-permute-start.97
  795.2 11.4 %collective-permute-start.85 = (bf16[528,512]{1,0:T(8,128)(2,1)S(1)}, bf16[528,512]{1,0:T(8,128)(2,1)S(1)}, u32[]{:S(2)}, u32[]{:S(2)}) collective-permute-start(bf16[528,512]{1,0:T(8,128)(2,1)S(1)} %get-tuple-element.172), channel_id=1, source_target_pairs={{0,1},{1,2},{4,5},{5,6},{8,9},{9,10},{12,13},{13,14},{16,17},{17,1... | collective-permute-start | bytes 1622024 | tf_op jit(solution)/shard_map/ppermute | solution.py:754
  815.2 10.2 collective-permute-start.98
  887.3 9.5 convert_add_fusion
  908.9 12.1 %linear_backward.2 = (bf16[512,64]{1,0:T(8,128)(2,1)S(1)}, bf16[512,64]{1,0:T(8,128)(2,1)S(1)}, bf16[512,512]{1,0:T(8,128)(2,1)S(1)}, f32[512,64]{1,0:T(8,128)S(1)}, f32[512,512]{1,0:T(8,128)S(1)}) custom-call(s32[1,3]{1,0:T(1,128)S(1)} %copy-done.166, bf16[512,64]{1,0:T(8,128)(2,1)S(1)} %copy-done.165, bf16[512,64]{1,0:T(8,128)(2,1)S(1)} %copy-done.131, ...), custom_call_target="tpu_custom_call" | custom-call | flops 2684354560 | bytes 4194304 | tf_op jit(solution)/shard_map/linear_backward/pallas_call | solution.py:264
  948.3 12.2 %collective-permute-start.114 = (bf16[528,512]{1,0:T(8,128)(2,1)}, bf16[528,512]{1,0:T(8,128)(2,1)}, u32[]{:S(2)}, u32[]{:S(2)}) collective-permute-start(bf16[528,512]{1,0:T(8,128)(2,1)} %get-tuple-element.182), channel_id=1, source_target_pairs={{0,1},{4,5},{8,9},{12,13},{16,17},{20,21},{24,25},{28,29}} | collective-permute-start | bytes 1622024 | tf_op jit(solution)/shard_map/ppermute | solution.py:754
  1034.0 13.6 %psum.84 = f32[1542]{0:T(1024)S(1)} all-reduce(f32[1542]{0:T(1024)S(1)} %concatenate.85), channel_id=1, replica_groups=mesh['dp'=8,'mp'=4] {'dp'}, use_global_device_ids=true, to_apply=%region_31.32 | all-reduce | flops 1542 | bytes 12336 | tf_op jit(solution)/shard_map/psum | solution.py:1055
  1074.9 32.3 %all-reduce.22.cloned.1.call-done = (bf16[2048,64]{0,1:T(8,128)(2,1)}, bf16[2048,64]{0,1:T(8,128)(2,1)}, bf16[2048,512]{1,0:T(8,128)(2,1)}, bf16[512,2048]{1,0:T(8,128)(2,1)}) async-done(((bf16[2048,64]{0,1:T(8,128)(2,1)}, bf16[2048,64]{0,1:T(8,128)(2,1)}, bf16[2048,512]{1,0:T(8,128)(2,1)}, bf16[512,2048]{1,0:T(8,128)(2,1)}), (bf16[2048,64]{0,1:T(8,128)(2,1)}, bf16[2048,64]{0,1:T(8,128)(2,1)}, ...) | async-done | bytes 4718608 | tf_op jit(solution)/shard_map/psum | solution.py:777
  (959 shorter events, 770.2 us)
Async XLA Ops:
  7.2 269.3 %all-gather.2.cloned.1.call-start = ((), (), s32[]{:S(2)}) async-start(), calls=%async_computation.2 | async-start | bytes 5242880 | tf_op jit(solution)/shard_map/all_gather | solution.py:903
  89.5 464.4 %reduce-scatter.3.cloned.1.call-start = ((), (), s32[]{:S(2)}) async-start(), calls=%async_computation.3 | async-start | bytes 2621440 | tf_op jit(solution)/shard_map/reduce_scatter | solution.py:968
  101.0 36.1 %collective-permute-start.7 = (bf16[512,512]{1,0:T(8,128)(2,1)}, bf16[512,512]{1,0:T(8,128)(2,1)}, u32[]{:S(2)}, u32[]{:S(2)}) collective-permute-start(bf16[512,512]{1,0:T(8,128)(2,1)} %get-tuple-element.200), channel_id=1, source_target_pairs={{0,1},{1,2},{4,5},{5,6},{8,9},{9,10},{12,13},{13,14},{16,17},{17,1... | collective-permute-start | bytes 1572872 | tf_op jit(solution)/shard_map/ppermute | solution.py:754
  130.9 40.5 %collective-permute-start.11 = (bf16[512,512]{1,0:T(8,128)(2,1)}, bf16[512,512]{1,0:T(8,128)(2,1)S(1)}, u32[]{:S(2)}, u32[]{:S(2)}) collective-permute-start(bf16[512,512]{1,0:T(8,128)(2,1)} %get-tuple-element.199), channel_id=1, source_target_pairs={{1,0},{2,1},{3,2},{5,4},{6,5},{7,6},{9,8},{10,9},{11,10},{13,12},{... | collective-permute-start | bytes 1572872 | tf_op jit(solution)/shard_map/ppermute | solution.py:755
  132.4 56.8 %collective-permute-start.36 = (bf16[512,512]{1,0:T(8,128)(2,1)}, bf16[512,512]{1,0:T(8,128)(2,1)S(1)}, u32[]{:S(2)}, u32[]{:S(2)}) collective-permute-start(bf16[512,512]{1,0:T(8,128)(2,1)} %get-tuple-element.206), channel_id=1, source_target_pairs={{0,1},{4,5},{8,9},{12,13},{16,17},{20,21},{24,25},{28,29}} | collective-permute-start | bytes 1572872 | tf_op jit(solution)/shard_map/ppermute | solution.py:754
  138.3 43.4 %collective-permute-start.8 = (bf16[512,512]{1,0:T(8,128)(2,1)S(1)}, bf16[512,512]{1,0:T(8,128)(2,1)S(1)}, u32[]{:S(2)}, u32[]{:S(2)}) collective-permute-start(bf16[512,512]{1,0:T(8,128)(2,1)S(1)} %bitcast_add_fusion.39), channel_id=1, source_target_pairs={{0,1},{1,2},{2,3},{4,5},{5,6},{6,7},{8,9},{9,10},{10,11},{12,13},{... | collective-permute-start | bytes 1572872 | tf_op jit(solution)/shard_map/ppermute | solution.py:754
  146.9 42.4 %collective-permute-start.40 = (bf16[512,512]{1,0:T(8,128)(2,1)S(1)}, bf16[512,512]{1,0:T(8,128)(2,1)S(1)}, u32[]{:S(2)}, u32[]{:S(2)}) collective-permute-start(bf16[512,512]{1,0:T(8,128)(2,1)S(1)} %bitcast_add_fusion.28), channel_id=1, source_target_pairs={{2,1},{3,2},{6,5},{7,6},{10,9},{11,10},{14,13},{15,14},{18,17},{19... | collective-permute-start | bytes 1572872 | tf_op jit(solution)/shard_map/ppermute | solution.py:755
  189.4 39.2 %collective-permute-start.37 = (bf16[512,512]{1,0:T(8,128)(2,1)S(1)}, bf16[512,512]{1,0:T(8,128)(2,1)S(1)}, u32[]{:S(2)}, u32[]{:S(2)}) collective-permute-start(bf16[512,512]{1,0:T(8,128)(2,1)S(1)} %get-tuple-element.204), channel_id=1, source_target_pairs={{0,1},{1,2},{4,5},{5,6},{8,9},{9,10},{12,13},{13,14},{16,17},{17,1... | collective-permute-start | bytes 1572872 | tf_op jit(solution)/shard_map/ppermute | solution.py:754
  198.1 35.0 %collective-permute-start.16 = (bf16[512,512]{1,0:T(8,128)(2,1)S(1)}, bf16[512,512]{1,0:T(8,128)(2,1)S(1)}, u32[]{:S(2)}, u32[]{:S(2)}) collective-permute-start(bf16[512,512]{1,0:T(8,128)(2,1)S(1)} %collective-permute-done.15.refs_3_), channel_id=1, source_target_pairs={{1,0},{2,1},{5,4},{6,5},{9,8},{10,9},{13,12},{14,13},{17,16},{18,1... | collective-permute-start | bytes 1572872 | tf_op jit(solution)/shard_map/ppermute | solution.py:730
  422.4 133.9 %reduce-scatter.5.cloned.1.call-start = ((), (), s32[]{:S(2)}) async-start(), calls=%async_computation.4 | async-start | bytes 2621440 | tf_op jit(solution)/shard_map/reduce_scatter | solution.py:968
  594.7 292.6 %all-reduce.16.cloned.1.call-start = ((), (), s32[]{:S(2)}) async-start(), calls=%async_computation.5 | async-start | bytes 11534336 | tf_op jit(solution)/shard_map/psum | solution.py:777
  603.8 48.3 %collective-permute-start.77 = (bf16[528,512]{1,0:T(8,128)(2,1)S(1)}, bf16[528,512]{1,0:T(8,128)(2,1)S(1)}, u32[]{:S(2)}, u32[]{:S(2)}) collective-permute-start(bf16[528,512]{1,0:T(8,128)(2,1)S(1)} %get-tuple-element.187), channel_id=1, source_target_pairs={{1,0},{2,1},{3,2},{5,4},{6,5},{7,6},{9,8},{10,9},{11,10},{13,12},{... | collective-permute-start | bytes 1622024 | tf_op jit(solution)/shard_map/ppermute | solution.py:755
  610.5 34.9 %collective-permute-start.61 = (bf16[528,512]{1,0:T(8,128)(2,1)S(1)}, bf16[528,512]{1,0:T(8,128)(2,1)S(1)}, u32[]{:S(2)}, u32[]{:S(2)}) collective-permute-start(bf16[528,512]{1,0:T(8,128)(2,1)S(1)} %get-tuple-element.176), channel_id=1, source_target_pairs={{0,1},{1,2},{4,5},{5,6},{8,9},{9,10},{12,13},{13,14},{16,17},{17,1... | collective-permute-start | bytes 1622024 | tf_op jit(solution)/shard_map/ppermute | solution.py:754
  655.0 32.7 %collective-permute-start.81 = (bf16[512,512]{1,0:T(8,128)(2,1)}, bf16[512,512]{1,0:T(8,128)(2,1)}, u32[]{:S(2)}, u32[]{:S(2)}) collective-permute-start(bf16[512,512]{1,0:T(8,128)(2,1)} %broadcast_add_fusion.1.own_ref), channel_id=1, source_target_pairs={{1,0},{2,1},{3,2},{5,4},{6,5},{7,6},{9,8},{10,9},{11,10},{13,12},{... | collective-permute-start | bytes 1572872 | tf_op jit(solution)/shard_map/ppermute | solution.py:730
  656.4 32.6 %collective-permute-start.78 = (bf16[512,512]{1,0:T(8,128)(2,1)}, bf16[512,512]{1,0:T(8,128)(2,1)}, u32[]{:S(2)}, u32[]{:S(2)}) collective-permute-start(bf16[512,512]{1,0:T(8,128)(2,1)} %broadcast_add_fusion.1.own_ref), channel_id=1, source_target_pairs={{0,1},{1,2},{2,3},{4,5},{5,6},{6,7},{8,9},{9,10},{10,11},{12,13},{... | collective-permute-start | bytes 1572872 | tf_op jit(solution)/shard_map/ppermute | solution.py:728
  672.8 297.3 %all-reduce.18.cloned.1.call-start = ((), (), s32[]{:S(2)}) async-start(), calls=%async_computation.6 | async-start | bytes 23068672 | tf_op jit(solution)/shard_map/psum | solution.py:777
  813.8 44.8 %collective-permute-start.89 = (bf16[528,512]{1,0:T(8,128)(2,1)}, bf16[528,512]{1,0:T(8,128)(2,1)}, u32[]{:S(2)}, u32[]{:S(2)}) collective-permute-start(bf16[528,512]{1,0:T(8,128)(2,1)} %get-tuple-element.171), channel_id=1, source_target_pairs={{1,0},{2,1},{3,2},{5,4},{6,5},{7,6},{9,8},{10,9},{11,10},{13,12},{... | collective-permute-start | bytes 1622024 | tf_op jit(solution)/shard_map/ppermute | solution.py:755
  826.3 32.3 %collective-permute-start.86 = (bf16[528,512]{1,0:T(8,128)(2,1)}, bf16[528,512]{1,0:T(8,128)(2,1)}, u32[]{:S(2)}, u32[]{:S(2)}) collective-permute-start(bf16[528,512]{1,0:T(8,128)(2,1)} %bitcast_add_fusion.15), channel_id=1, source_target_pairs={{0,1},{1,2},{2,3},{4,5},{5,6},{6,7},{8,9},{9,10},{10,11},{12,13},{... | collective-permute-start | bytes 1622024 | tf_op jit(solution)/shard_map/ppermute | solution.py:754
  840.1 33.0 %collective-permute-start.105 = (bf16[512,512]{1,0:T(8,128)(2,1)}, bf16[512,512]{1,0:T(8,128)(2,1)}, u32[]{:S(2)}, u32[]{:S(2)}) collective-permute-start(bf16[512,512]{1,0:T(8,128)(2,1)} %get-tuple-element.125.own_ref), channel_id=1, source_target_pairs={{1,0},{2,1},{3,2},{5,4},{6,5},{7,6},{9,8},{10,9},{11,10},{13,12},{... | collective-permute-start | bytes 1572872 | tf_op jit(solution)/shard_map/ppermute | solution.py:730
  841.7 32.7 %collective-permute-start.102 = (bf16[512,512]{1,0:T(8,128)(2,1)}, bf16[512,512]{1,0:T(8,128)(2,1)}, u32[]{:S(2)}, u32[]{:S(2)}) collective-permute-start(bf16[512,512]{1,0:T(8,128)(2,1)} %get-tuple-element.125.own_ref), channel_id=1, source_target_pairs={{0,1},{1,2},{2,3},{4,5},{5,6},{6,7},{8,9},{9,10},{10,11},{12,13},{... | collective-permute-start | bytes 1572872 | tf_op jit(solution)/shard_map/ppermute | solution.py:728
  856.0 206.7 %all-reduce.20.cloned.1.call-start = ((), (), s32[]{:S(2)}) async-start(), calls=%async_computation.7 | async-start | bytes 16777216 | tf_op jit(solution)/shard_map/psum | solution.py:777
  879.6 227.6 %all-reduce.22.cloned.1.call-start = ((), (), s32[]{:S(2)}) async-start(), calls=%async_computation.8 | async-start | bytes 9437184 | tf_op jit(solution)/shard_map/psum | solution.py:777
  946.8 47.0 %collective-permute-start.117 = (bf16[528,512]{1,0:T(8,128)(2,1)}, bf16[528,512]{1,0:T(8,128)(2,1)}, u32[]{:S(2)}, u32[]{:S(2)}) collective-permute-start(bf16[528,512]{1,0:T(8,128)(2,1)} %get-tuple-element.181), channel_id=1, source_target_pairs={{3,2},{7,6},{11,10},{15,14},{19,18},{23,22},{27,26},{31,30}} | collective-permute-start | bytes 1622024 | tf_op jit(solution)/shard_map/ppermute | solution.py:755
  948.3 55.7 %collective-permute-start.114 = (bf16[528,512]{1,0:T(8,128)(2,1)}, bf16[528,512]{1,0:T(8,128)(2,1)}, u32[]{:S(2)}, u32[]{:S(2)}) collective-permute-start(bf16[528,512]{1,0:T(8,128)(2,1)} %get-tuple-element.182), channel_id=1, source_target_pairs={{0,1},{4,5},{8,9},{12,13},{16,17},{20,21},{24,25},{28,29}} | collective-permute-start | bytes 1622024 | tf_op jit(solution)/shard_map/ppermute | solution.py:754
  (337 other events, 4132.6 us)
Sparse Core Ops, SparseCore 0:
  89.6 135.8 all-gather.1
  422.6 55.5 reduce-scatter.2
  503.7 47.2 reduce-scatter.4
  599.1 102.5 all-reduce.15
  713.5 164.1 all-reduce.17
  882.6 128.0 all-reduce.19
  1022.1 85.0 all-reduce.21

commit v5 on v4

--- a/solution.py
+++ b/solution.py
@@ -257,7 +257,7 @@
 def linear_backward(chunk, lengths, query, keys, values, grad, mixed, total, carry):
     rows, width = query.shape
     heads = width // FEATURE_SIZE
-    tile = min(256, rows)
+    tile = min(512, rows)
     count = chunk + 1
     wide = heads * HEAD_DIM
     carry = list(carry)
@@ -365,7 +365,7 @@
     own, right, left = pieces
     rows, width = own.shape
     count = len(right) + 1
-    tile = min(128, rows)
+    tile = min(256, rows)
     place = lax.axis_index("mp").astype(jnp.int32).reshape(1)
     piece_spec = pl.BlockSpec((tile, width), lambda t: (t, 0))
     return pl.pallas_call(
@@ -406,7 +406,7 @@
     own, right, left = pieces
     rows, width = own.shape
     count = len(right) + 1
-    tile = min(128, rows)
+    tile = min(256, rows)
     place = lax.axis_index("mp").astype(jnp.int32).reshape(1)
     piece_spec = pl.BlockSpec((tile, width), lambda t: (t, 0))
     return pl.pallas_call(

time: 1140 us -> 1130 us (level)
  transfers between devices with their start and end apart: 127 -> 127, of which waited for: 31 -> 29; matrix products, arithmetic and copies ran while one was open for 26% -> 27% of each run, Pallas kernels for 10% -> 9%
where the time goes in v5:
time: 1130 us; the launch traced here: 1120 us
  starting transfers between devices  345 us (31%)
  waiting for transfers between devices  245 us (22%)
  matrix products  183 us (16%)
  Pallas kernels  103 us (9%)
  local copies, waits for them, and re-layouts  101 us (9%)
  other arithmetic  94.8 us (8%)
  between operations  34.9 us (3%)
  blocking collectives  13.7 us (1%)
    ppermute x30, starting transfers between devices, scatter_sum(): right = lax.ppermute(to_right, 'mp', [(j, j + 1) for j in range(k)])  191 us
    ppermute x30, waiting for transfers between devices, line_gather(): lax.ppermute(left[-1], 'mp', [(j, j - 1) for j in range(1, count - k + 1)])  106 us
    ppermute x30, starting transfers between devices, line_gather(): lax.ppermute(right[-1], 'mp', [(j, j + 1) for j in range(k - 1, count - 1)])  79.9 us
    dot_general x22, matrix products, nt(): lax.dot_general(left, right, (((1,), (1,)), ((), ())), preferred_element_...  73.8 us
    unnamed x483, local copies, waits for them, and re-layouts  69.1 us
    dot_general x11, matrix products, tn(): lax.dot_general(left, right, (((0,), (0,)), ((), ())), preferred_element_...  61.1 us
    ppermute x30, waiting for transfers between devices, scatter_sum(): right = lax.ppermute(to_right, 'mp', [(j, j + 1) for j in range(k)])  54.5 us
    dot_general x18, matrix products, nn(): lax.dot_general(left, right, (((1,), (0,)), ((), ())), preferred_element_...  47.7 us
  transfers between devices with their start and end apart: 127, of which 29 were waited for; matrix products, arithmetic and copies ran while one was open for 27% of the time, Pallas kernels for 9%

profile of v5, /device:TPU:0, one launch (start us, length us, event | category | flops | bytes accessed | tf_op | source)
XLA Modules:
  0.0 1120.4 jit_solution(4984305042255382779)
XLA Ops:
  15.4 10.0 collective-permute-done.3.refs_3_
  28.9 11.5 %collective-permute-done.4.refs_4_ = bf16[512,512]{1,0:T(8,128)(2,1)} collective-permute-done((bf16[512,512]{1,0:T(8,128)(2,1)S(1)}, bf16[512,512]{1,0:T(8,128)(2,1)}, u32[]{:S(2)}, u32[]{:S(2)}) %collective-permute-start.4) | collective-permute-done | bytes 524320 | tf_op jit(solution)/shard_map/ppermute | solution.py:730
  100.1 11.0 collective-permute-start.7
  146.8 22.6 %collective-permute-done.11.left_ref = bf16[512,512]{1,0:T(8,128)(2,1)S(1)} collective-permute-done((bf16[512,512]{1,0:T(8,128)(2,1)}, bf16[512,512]{1,0:T(8,128)(2,1)S(1)}, u32[]{:S(2)}, u32[]{:S(2)}) %collective-permute-start.11) | collective-permute-done | bytes 524320 | tf_op jit(solution)/shard_map/ppermute | solution.py:755
  169.4 10.6 collective-permute-done.8.right_ref
  187.9 8.4 collective-permute-start.37
  198.7 12.2 %collective-permute-done.12.refs_0_ = bf16[512,512]{1,0:T(8,128)(2,1)S(1)} collective-permute-done((bf16[512,512]{1,0:T(8,128)(2,1)S(1)}, bf16[512,512]{1,0:T(8,128)(2,1)S(1)}, u32[]{:S(2)}, u32[]{:S(2)}) %collective-permute-start.12) | collective-permute-done | bytes 524320 | tf_op jit(solution)/shard_map/ppermute | solution.py:728
  212.9 14.7 %collective-permute-done.37 = bf16[512,512]{1,0:T(8,128)(2,1)S(1)} collective-permute-done((bf16[512,512]{1,0:T(8,128)(2,1)S(1)}, bf16[512,512]{1,0:T(8,128)(2,1)S(1)}, u32[]{:S(2)}, u32[]{:S(2)}) %collective-permute-start.37) | collective-permute-done | bytes 524320 | tf_op jit(solution)/shard_map/ppermute | solution.py:754
  302.4 17.0 %collective-permute-start.19 = (bf16[512,512]{1,0:T(8,128)(2,1)S(1)}, bf16[512,512]{1,0:T(8,128)(2,1)S(1)}, u32[]{:S(2)}, u32[]{:S(2)}) collective-permute-start(bf16[512,512]{1,0:T(8,128)(2,1)S(1)} %get-tuple-element.192), channel_id=1, source_target_pairs={{0,1},{1,2},{4,5},{5,6},{8,9},{9,10},{12,13},{13,14},{16,17},{17,1... | collective-permute-start | bytes 1572872 | tf_op jit(solution)/shard_map/ppermute | solution.py:754
  374.0 9.1 collective-permute-start.50
  430.7 14.4 %collective-permute-done.58.refs_4_ = bf16[512,512]{1,0:T(8,128)(2,1)} collective-permute-done((bf16[512,512]{1,0:T(8,128)(2,1)}, bf16[512,512]{1,0:T(8,128)(2,1)}, u32[]{:S(2)}, u32[]{:S(2)}) %collective-permute-start.58) | collective-permute-done | bytes 524320 | tf_op jit(solution)/shard_map/ppermute | solution.py:730
  455.5 23.4 %collective-permute-done.59.refs_5_ = bf16[512,512]{1,0:T(8,128)(2,1)S(1)} collective-permute-done((bf16[512,512]{1,0:T(8,128)(2,1)}, bf16[512,512]{1,0:T(8,128)(2,1)S(1)}, u32[]{:S(2)}, u32[]{:S(2)}) %collective-permute-start.59) | collective-permute-done | bytes 524320 | tf_op jit(solution)/shard_map/ppermute | solution.py:730
  525.5 8.7 fusion.96
  610.0 12.1 %collective-permute-start.61 = (bf16[528,512]{1,0:T(8,128)(2,1)S(1)}, bf16[528,512]{1,0:T(8,128)(2,1)S(1)}, u32[]{:S(2)}, u32[]{:S(2)}) collective-permute-start(bf16[528,512]{1,0:T(8,128)(2,1)S(1)} %get-tuple-element.176), channel_id=1, source_target_pairs={{0,1},{1,2},{4,5},{5,6},{8,9},{9,10},{12,13},{13,14},{16,17},{17,1... | collective-permute-start | bytes 1622024 | tf_op jit(solution)/shard_map/ppermute | solution.py:754
  630.4 11.3 %convolution_convert_fusion.1 = bf16[2048,1408]{1,0:T(8,128)(2,1)} fusion(bf16[1024,2048]{1,0:T(8,128)(2,1)} %constant_dynamic-update-slice_fusion, bf16[512,1408]{1,0:T(8,128)(2,1)S(1)} %copy-done.176, bf16[512,1408]{1,0:T(8,128)(2,1)S(1)} %copy-done.173), kind=kOutput, calls=%fused_computation.4 | convolution fusion | flops 5914230784 | bytes 12845056 | tf_op jit(solution)/shard_map/dot_general | solution.py:33
  660.3 8.6 convolution_convert_fusion.2
  781.3 10.6 collective-permute-start.97
  792.9 11.4 %collective-permute-start.85 = (bf16[528,512]{1,0:T(8,128)(2,1)S(1)}, bf16[528,512]{1,0:T(8,128)(2,1)S(1)}, u32[]{:S(2)}, u32[]{:S(2)}) collective-permute-start(bf16[528,512]{1,0:T(8,128)(2,1)S(1)} %get-tuple-element.172), channel_id=1, source_target_pairs={{0,1},{1,2},{4,5},{5,6},{8,9},{9,10},{12,13},{13,14},{16,17},{17,1... | collective-permute-start | bytes 1622024 | tf_op jit(solution)/shard_map/ppermute | solution.py:754
  813.2 9.8 collective-permute-start.98
  885.8 9.5 convert_add_fusion
  906.0 10.0 linear_backward.2
  942.0 12.0 %collective-permute-start.114 = (bf16[528,512]{1,0:T(8,128)(2,1)}, bf16[528,512]{1,0:T(8,128)(2,1)}, u32[]{:S(2)}, u32[]{:S(2)}) collective-permute-start(bf16[528,512]{1,0:T(8,128)(2,1)} %get-tuple-element.182), channel_id=1, source_target_pairs={{0,1},{4,5},{8,9},{12,13},{16,17},{20,21},{24,25},{28,29}} | collective-permute-start | bytes 1622024 | tf_op jit(solution)/shard_map/ppermute | solution.py:754
  1028.0 13.7 %psum.84 = f32[1542]{0:T(1024)S(1)} all-reduce(f32[1542]{0:T(1024)S(1)} %concatenate.85), channel_id=1, replica_groups=mesh['dp'=8,'mp'=4] {'dp'}, use_global_device_ids=true, to_apply=%region_31.32 | all-reduce | flops 1542 | bytes 12336 | tf_op jit(solution)/shard_map/psum | solution.py:1055
  1069.0 33.6 %all-reduce.22.cloned.1.call-done = (bf16[2048,64]{0,1:T(8,128)(2,1)}, bf16[2048,64]{0,1:T(8,128)(2,1)}, bf16[2048,512]{1,0:T(8,128)(2,1)}, bf16[512,2048]{1,0:T(8,128)(2,1)}) async-done(((bf16[2048,64]{0,1:T(8,128)(2,1)}, bf16[2048,64]{0,1:T(8,128)(2,1)}, bf16[2048,512]{1,0:T(8,128)(2,1)}, bf16[512,2048]{1,0:T(8,128)(2,1)}), (bf16[2048,64]{0,1:T(8,128)(2,1)}, bf16[2048,64]{0,1:T(8,128)(2,1)}, ...) | async-done | bytes 4718608 | tf_op jit(solution)/shard_map/psum | solution.py:777
  (959 shorter events, 769.2 us)
Async XLA Ops:
  7.2 269.0 %all-gather.2.cloned.1.call-start = ((), (), s32[]{:S(2)}) async-start(), calls=%async_computation.2 | async-start | bytes 5242880 | tf_op jit(solution)/shard_map/all_gather | solution.py:903
  88.6 464.5 %reduce-scatter.3.cloned.1.call-start = ((), (), s32[]{:S(2)}) async-start(), calls=%async_computation.3 | async-start | bytes 2621440 | tf_op jit(solution)/shard_map/reduce_scatter | solution.py:968
  100.1 35.1 %collective-permute-start.7 = (bf16[512,512]{1,0:T(8,128)(2,1)}, bf16[512,512]{1,0:T(8,128)(2,1)}, u32[]{:S(2)}, u32[]{:S(2)}) collective-permute-start(bf16[512,512]{1,0:T(8,128)(2,1)} %get-tuple-element.200), channel_id=1, source_target_pairs={{0,1},{1,2},{4,5},{5,6},{8,9},{9,10},{12,13},{13,14},{16,17},{17,1... | collective-permute-start | bytes 1572872 | tf_op jit(solution)/shard_map/ppermute | solution.py:754
  129.1 40.3 %collective-permute-start.11 = (bf16[512,512]{1,0:T(8,128)(2,1)}, bf16[512,512]{1,0:T(8,128)(2,1)S(1)}, u32[]{:S(2)}, u32[]{:S(2)}) collective-permute-start(bf16[512,512]{1,0:T(8,128)(2,1)} %get-tuple-element.199), channel_id=1, source_target_pairs={{1,0},{2,1},{3,2},{5,4},{6,5},{7,6},{9,8},{10,9},{11,10},{13,12},{... | collective-permute-start | bytes 1572872 | tf_op jit(solution)/shard_map/ppermute | solution.py:755
  130.6 57.1 %collective-permute-start.36 = (bf16[512,512]{1,0:T(8,128)(2,1)}, bf16[512,512]{1,0:T(8,128)(2,1)S(1)}, u32[]{:S(2)}, u32[]{:S(2)}) collective-permute-start(bf16[512,512]{1,0:T(8,128)(2,1)} %get-tuple-element.206), channel_id=1, source_target_pairs={{0,1},{4,5},{8,9},{12,13},{16,17},{20,21},{24,25},{28,29}} | collective-permute-start | bytes 1572872 | tf_op jit(solution)/shard_map/ppermute | solution.py:754
  136.5 43.5 %collective-permute-start.8 = (bf16[512,512]{1,0:T(8,128)(2,1)S(1)}, bf16[512,512]{1,0:T(8,128)(2,1)S(1)}, u32[]{:S(2)}, u32[]{:S(2)}) collective-permute-start(bf16[512,512]{1,0:T(8,128)(2,1)S(1)} %bitcast_add_fusion.39), channel_id=1, source_target_pairs={{0,1},{1,2},{2,3},{4,5},{5,6},{6,7},{8,9},{9,10},{10,11},{12,13},{... | collective-permute-start | bytes 1572872 | tf_op jit(solution)/shard_map/ppermute | solution.py:754
  146.0 41.8 %collective-permute-start.40 = (bf16[512,512]{1,0:T(8,128)(2,1)S(1)}, bf16[512,512]{1,0:T(8,128)(2,1)S(1)}, u32[]{:S(2)}, u32[]{:S(2)}) collective-permute-start(bf16[512,512]{1,0:T(8,128)(2,1)S(1)} %bitcast_add_fusion.28), channel_id=1, source_target_pairs={{2,1},{3,2},{6,5},{7,6},{10,9},{11,10},{14,13},{15,14},{18,17},{19... | collective-permute-start | bytes 1572872 | tf_op jit(solution)/shard_map/ppermute | solution.py:755
  187.9 39.8 %collective-permute-start.37 = (bf16[512,512]{1,0:T(8,128)(2,1)S(1)}, bf16[512,512]{1,0:T(8,128)(2,1)S(1)}, u32[]{:S(2)}, u32[]{:S(2)}) collective-permute-start(bf16[512,512]{1,0:T(8,128)(2,1)S(1)} %get-tuple-element.204), channel_id=1, source_target_pairs={{0,1},{1,2},{4,5},{5,6},{8,9},{9,10},{12,13},{13,14},{16,17},{17,1... | collective-permute-start | bytes 1572872 | tf_op jit(solution)/shard_map/ppermute | solution.py:754
  197.4 34.8 %collective-permute-start.16 = (bf16[512,512]{1,0:T(8,128)(2,1)S(1)}, bf16[512,512]{1,0:T(8,128)(2,1)S(1)}, u32[]{:S(2)}, u32[]{:S(2)}) collective-permute-start(bf16[512,512]{1,0:T(8,128)(2,1)S(1)} %collective-permute-done.15.refs_3_), channel_id=1, source_target_pairs={{1,0},{2,1},{5,4},{6,5},{9,8},{10,9},{13,12},{14,13},{17,16},{18,1... | collective-permute-start | bytes 1572872 | tf_op jit(solution)/shard_map/ppermute | solution.py:730
  423.1 132.4 %reduce-scatter.5.cloned.1.call-start = ((), (), s32[]{:S(2)}) async-start(), calls=%async_computation.4 | async-start | bytes 2621440 | tf_op jit(solution)/shard_map/reduce_scatter | solution.py:968
  445.1 33.8 %collective-permute-start.59 = (bf16[512,512]{1,0:T(8,128)(2,1)}, bf16[512,512]{1,0:T(8,128)(2,1)S(1)}, u32[]{:S(2)}, u32[]{:S(2)}) collective-permute-start(bf16[512,512]{1,0:T(8,128)(2,1)} %collective-permute-done.58.refs_4_), channel_id=1, source_target_pairs={{1,0},{5,4},{9,8},{13,12},{17,16},{21,20},{25,24},{29,28}} | collective-permute-start | bytes 1572872 | tf_op jit(solution)/shard_map/ppermute | solution.py:730
  594.0 291.8 %all-reduce.16.cloned.1.call-start = ((), (), s32[]{:S(2)}) async-start(), calls=%async_computation.5 | async-start | bytes 11534336 | tf_op jit(solution)/shard_map/psum | solution.py:777
  602.7 48.0 %collective-permute-start.77 = (bf16[528,512]{1,0:T(8,128)(2,1)S(1)}, bf16[528,512]{1,0:T(8,128)(2,1)S(1)}, u32[]{:S(2)}, u32[]{:S(2)}) collective-permute-start(bf16[528,512]{1,0:T(8,128)(2,1)S(1)} %get-tuple-element.187), channel_id=1, source_target_pairs={{1,0},{2,1},{3,2},{5,4},{6,5},{7,6},{9,8},{10,9},{11,10},{13,12},{... | collective-permute-start | bytes 1622024 | tf_op jit(solution)/shard_map/ppermute | solution.py:755
  610.0 33.8 %collective-permute-start.61 = (bf16[528,512]{1,0:T(8,128)(2,1)S(1)}, bf16[528,512]{1,0:T(8,128)(2,1)S(1)}, u32[]{:S(2)}, u32[]{:S(2)}) collective-permute-start(bf16[528,512]{1,0:T(8,128)(2,1)S(1)} %get-tuple-element.176), channel_id=1, source_target_pairs={{0,1},{1,2},{4,5},{5,6},{8,9},{9,10},{12,13},{13,14},{16,17},{17,1... | collective-permute-start | bytes 1622024 | tf_op jit(solution)/shard_map/ppermute | solution.py:754
  653.5 32.6 %collective-permute-start.81 = (bf16[512,512]{1,0:T(8,128)(2,1)}, bf16[512,512]{1,0:T(8,128)(2,1)}, u32[]{:S(2)}, u32[]{:S(2)}) collective-permute-start(bf16[512,512]{1,0:T(8,128)(2,1)} %broadcast_add_fusion.1.own_ref), channel_id=1, source_target_pairs={{1,0},{2,1},{3,2},{5,4},{6,5},{7,6},{9,8},{10,9},{11,10},{13,12},{... | collective-permute-start | bytes 1572872 | tf_op jit(solution)/shard_map/ppermute | solution.py:730
  654.9 32.5 %collective-permute-start.78 = (bf16[512,512]{1,0:T(8,128)(2,1)}, bf16[512,512]{1,0:T(8,128)(2,1)}, u32[]{:S(2)}, u32[]{:S(2)}) collective-permute-start(bf16[512,512]{1,0:T(8,128)(2,1)} %broadcast_add_fusion.1.own_ref), channel_id=1, source_target_pairs={{0,1},{1,2},{2,3},{4,5},{5,6},{6,7},{8,9},{9,10},{10,11},{12,13},{... | collective-permute-start | bytes 1572872 | tf_op jit(solution)/shard_map/ppermute | solution.py:728
  671.3 292.3 %all-reduce.18.cloned.1.call-start = ((), (), s32[]{:S(2)}) async-start(), calls=%async_computation.6 | async-start | bytes 23068672 | tf_op jit(solution)/shard_map/psum | solution.py:777
  811.8 43.7 %collective-permute-start.89 = (bf16[528,512]{1,0:T(8,128)(2,1)}, bf16[528,512]{1,0:T(8,128)(2,1)}, u32[]{:S(2)}, u32[]{:S(2)}) collective-permute-start(bf16[528,512]{1,0:T(8,128)(2,1)} %get-tuple-element.171), channel_id=1, source_target_pairs={{1,0},{2,1},{3,2},{5,4},{6,5},{7,6},{9,8},{10,9},{11,10},{13,12},{... | collective-permute-start | bytes 1622024 | tf_op jit(solution)/shard_map/ppermute | solution.py:755
  837.4 33.1 %collective-permute-start.105 = (bf16[512,512]{1,0:T(8,128)(2,1)}, bf16[512,512]{1,0:T(8,128)(2,1)}, u32[]{:S(2)}, u32[]{:S(2)}) collective-permute-start(bf16[512,512]{1,0:T(8,128)(2,1)} %get-tuple-element.125.own_ref), channel_id=1, source_target_pairs={{1,0},{2,1},{3,2},{5,4},{6,5},{7,6},{9,8},{10,9},{11,10},{13,12},{... | collective-permute-start | bytes 1572872 | tf_op jit(solution)/shard_map/ppermute | solution.py:730
  839.0 32.8 %collective-permute-start.102 = (bf16[512,512]{1,0:T(8,128)(2,1)}, bf16[512,512]{1,0:T(8,128)(2,1)}, u32[]{:S(2)}, u32[]{:S(2)}) collective-permute-start(bf16[512,512]{1,0:T(8,128)(2,1)} %get-tuple-element.125.own_ref), channel_id=1, source_target_pairs={{0,1},{1,2},{2,3},{4,5},{5,6},{6,7},{8,9},{9,10},{10,11},{12,13},{... | collective-permute-start | bytes 1572872 | tf_op jit(solution)/shard_map/ppermute | solution.py:728
  852.9 203.9 %all-reduce.20.cloned.1.call-start = ((), (), s32[]{:S(2)}) async-start(), calls=%async_computation.7 | async-start | bytes 16777216 | tf_op jit(solution)/shard_map/psum | solution.py:777
  877.0 225.7 %all-reduce.22.cloned.1.call-start = ((), (), s32[]{:S(2)}) async-start(), calls=%async_computation.8 | async-start | bytes 9437184 | tf_op jit(solution)/shard_map/psum | solution.py:777
  940.5 46.8 %collective-permute-start.117 = (bf16[528,512]{1,0:T(8,128)(2,1)}, bf16[528,512]{1,0:T(8,128)(2,1)}, u32[]{:S(2)}, u32[]{:S(2)}) collective-permute-start(bf16[528,512]{1,0:T(8,128)(2,1)} %get-tuple-element.181), channel_id=1, source_target_pairs={{3,2},{7,6},{11,10},{15,14},{19,18},{23,22},{27,26},{31,30}} | collective-permute-start | bytes 1622024 | tf_op jit(solution)/shard_map/ppermute | solution.py:755
  942.0 56.0 %collective-permute-start.114 = (bf16[528,512]{1,0:T(8,128)(2,1)}, bf16[528,512]{1,0:T(8,128)(2,1)}, u32[]{:S(2)}, u32[]{:S(2)}) collective-permute-start(bf16[528,512]{1,0:T(8,128)(2,1)} %get-tuple-element.182), channel_id=1, source_target_pairs={{0,1},{4,5},{8,9},{12,13},{16,17},{20,21},{24,25},{28,29}} | collective-permute-start | bytes 1622024 | tf_op jit(solution)/shard_map/ppermute | solution.py:754
  (337 other events, 4130.9 us)
Sparse Core Ops, SparseCore 0:
  88.7 136.6 all-gather.1
  423.2 57.1 reduce-scatter.2
  502.9 47.6 reduce-scatter.4
  598.4 102.7 all-reduce.15
  713.3 163.9 all-reduce.17
  882.2 127.6 all-reduce.19
  1016.2 86.4 all-reduce.21

commit v6 on v5

--- a/solution.py
+++ b/solution.py
@@ -444,7 +444,7 @@
 
 def hidden_forward(gate, upper, after):
     rows, width = gate.shape
-    tile = row_tiles(rows, 128)
+    tile = row_tiles(rows, 256)
     spec = pl.BlockSpec((tile, width), lambda t: (t, 0))
     return pl.pallas_call(
         hidden_kernel,
@@ -460,7 +460,7 @@
 
 def hidden_backward(gate, upper, grad):
     rows, width = gate.shape
-    tile = row_tiles(rows, 128)
+    tile = row_tiles(rows, 256)
     spec = pl.BlockSpec((tile, width), lambda t: (t, 0))
     return pl.pallas_call(
         hidden_backward_kernel,
@@ -500,7 +500,7 @@
 
 def pack_rows(grad, normed, extra, count):
     rows, width = grad.shape
-    tile = row_tiles(rows, 128)
+    tile = row_tiles(rows, 256)
     shape = (count, rows + PAD_ROWS, width // count)
     return pl.pallas_call(
         functools.partial(pack_kernel, count, tile),
@@ -1065,7 +1065,7 @@
     ]
     rms_values = jnp.sqrt(small[3 * width : -1] / (small[-1] * model_width))
     down_sums = [tie(v.astype(F32), wdq[0]) for v in down_sums]
-    ffn_sums = [tie(v.astype(F32), ldq[0]) for v in ffn_sums]
+    ffn_sums = [tie(v.astype(F32), ldq[1]) for v in ffn_sums]
     win_sums = [tie(v.astype(F32), tokens_grad[0]) for v in win_sums]
     lin_sums = [v.astype(F32) for v in lin_sums]
     return (

time: 1130 us -> 1130 us (level)
  no operation moved by 1% of the time
where the time goes in v6:
time: 1130 us; the launch traced here: 1120 us
  starting transfers between devices  344 us (30%)
  waiting for transfers between devices  247 us (22%)
  matrix products  182 us (16%)
  Pallas kernels  103 us (9%)
  local copies, waits for them, and re-layouts  101 us (9%)
  other arithmetic  94.8 us (8%)
  between operations  34.9 us (3%)
  blocking collectives  13.6 us (1%)
    ppermute x30, starting transfers between devices, scatter_sum(): right = lax.ppermute(to_right, 'mp', [(j, j + 1) for j in range(k)])  191 us
    ppermute x30, waiting for transfers between devices, line_gather(): lax.ppermute(left[-1], 'mp', [(j, j - 1) for j in range(1, count - k + 1)])  106 us
    ppermute x30, starting transfers between devices, line_gather(): lax.ppermute(right[-1], 'mp', [(j, j + 1) for j in range(k - 1, count - 1)])  79.7 us
    dot_general x22, matrix products, nt(): lax.dot_general(left, right, (((1,), (1,)), ((), ())), preferred_element_...  73.6 us
    unnamed x483, local copies, waits for them, and re-layouts  68.8 us
    dot_general x11, matrix products, tn(): lax.dot_general(left, right, (((0,), (0,)), ((), ())), preferred_element_...  61 us
    ppermute x30, waiting for transfers between devices, scatter_sum(): right = lax.ppermute(to_right, 'mp', [(j, j + 1) for j in range(k)])  54.5 us
    dot_general x18, matrix products, nn(): lax.dot_general(left, right, (((1,), (0,)), ((), ())), preferred_element_...  47.7 us
  transfers between devices with their start and end apart: 127, of which 29 were waited for; matrix products, arithmetic and copies ran while one was open for 27% of the time, Pallas kernels for 9%

profile of v6, /device:TPU:0, one launch (start us, length us, event | category | flops | bytes accessed | tf_op | source)
XLA Modules:
  0.0 1120.4 jit_solution(2724983694015623883)
XLA Ops:
  15.4 10.0 collective-permute-done.3.refs_3_
  28.9 11.5 %collective-permute-done.4.refs_4_ = bf16[512,512]{1,0:T(8,128)(2,1)} collective-permute-done((bf16[512,512]{1,0:T(8,128)(2,1)S(1)}, bf16[512,512]{1,0:T(8,128)(2,1)}, u32[]{:S(2)}, u32[]{:S(2)}) %collective-permute-start.4) | collective-permute-done | bytes 524320 | tf_op jit(solution)/shard_map/ppermute | solution.py:730
  100.1 11.0 collective-permute-start.7
  146.8 22.6 %collective-permute-done.11.left_ref = bf16[512,512]{1,0:T(8,128)(2,1)S(1)} collective-permute-done((bf16[512,512]{1,0:T(8,128)(2,1)}, bf16[512,512]{1,0:T(8,128)(2,1)S(1)}, u32[]{:S(2)}, u32[]{:S(2)}) %collective-permute-start.11) | collective-permute-done | bytes 524320 | tf_op jit(solution)/shard_map/ppermute | solution.py:755
  169.4 10.6 collective-permute-done.8.right_ref
  187.9 8.4 collective-permute-start.37
  198.7 12.2 %collective-permute-done.12.refs_0_ = bf16[512,512]{1,0:T(8,128)(2,1)S(1)} collective-permute-done((bf16[512,512]{1,0:T(8,128)(2,1)S(1)}, bf16[512,512]{1,0:T(8,128)(2,1)S(1)}, u32[]{:S(2)}, u32[]{:S(2)}) %collective-permute-start.12) | collective-permute-done | bytes 524320 | tf_op jit(solution)/shard_map/ppermute | solution.py:728
  212.9 14.7 %collective-permute-done.37 = bf16[512,512]{1,0:T(8,128)(2,1)S(1)} collective-permute-done((bf16[512,512]{1,0:T(8,128)(2,1)S(1)}, bf16[512,512]{1,0:T(8,128)(2,1)S(1)}, u32[]{:S(2)}, u32[]{:S(2)}) %collective-permute-start.37) | collective-permute-done | bytes 524320 | tf_op jit(solution)/shard_map/ppermute | solution.py:754
  302.4 17.0 %collective-permute-start.19 = (bf16[512,512]{1,0:T(8,128)(2,1)S(1)}, bf16[512,512]{1,0:T(8,128)(2,1)S(1)}, u32[]{:S(2)}, u32[]{:S(2)}) collective-permute-start(bf16[512,512]{1,0:T(8,128)(2,1)S(1)} %get-tuple-element.192), channel_id=1, source_target_pairs={{0,1},{1,2},{4,5},{5,6},{8,9},{9,10},{12,13},{13,14},{16,17},{17,1... | collective-permute-start | bytes 1572872 | tf_op jit(solution)/shard_map/ppermute | solution.py:754
  374.0 9.1 collective-permute-start.50
  430.7 14.4 %collective-permute-done.58.refs_4_ = bf16[512,512]{1,0:T(8,128)(2,1)} collective-permute-done((bf16[512,512]{1,0:T(8,128)(2,1)}, bf16[512,512]{1,0:T(8,128)(2,1)}, u32[]{:S(2)}, u32[]{:S(2)}) %collective-permute-start.58) | collective-permute-done | bytes 524320 | tf_op jit(solution)/shard_map/ppermute | solution.py:730
  455.5 23.4 %collective-permute-done.59.refs_5_ = bf16[512,512]{1,0:T(8,128)(2,1)S(1)} collective-permute-done((bf16[512,512]{1,0:T(8,128)(2,1)}, bf16[512,512]{1,0:T(8,128)(2,1)S(1)}, u32[]{:S(2)}, u32[]{:S(2)}) %collective-permute-start.59) | collective-permute-done | bytes 524320 | tf_op jit(solution)/shard_map/ppermute | solution.py:730
  525.5 8.7 fusion.96
  610.1 12.1 %collective-permute-start.61 = (bf16[528,512]{1,0:T(8,128)(2,1)S(1)}, bf16[528,512]{1,0:T(8,128)(2,1)S(1)}, u32[]{:S(2)}, u32[]{:S(2)}) collective-permute-start(bf16[528,512]{1,0:T(8,128)(2,1)S(1)} %get-tuple-element.176), channel_id=1, source_target_pairs={{0,1},{1,2},{4,5},{5,6},{8,9},{9,10},{12,13},{13,14},{16,17},{17,1... | collective-permute-start | bytes 1622024 | tf_op jit(solution)/shard_map/ppermute | solution.py:754
  630.5 11.3 %convolution_convert_fusion.1 = bf16[2048,1408]{1,0:T(8,128)(2,1)} fusion(bf16[1024,2048]{1,0:T(8,128)(2,1)} %constant_dynamic-update-slice_fusion, bf16[512,1408]{1,0:T(8,128)(2,1)S(1)} %copy-done.176, bf16[512,1408]{1,0:T(8,128)(2,1)S(1)} %copy-done.173), kind=kOutput, calls=%fused_computation.4 | convolution fusion | flops 5914230784 | bytes 12845056 | tf_op jit(solution)/shard_map/dot_general | solution.py:33
  660.4 8.6 convolution_convert_fusion.2
  781.3 10.7 collective-permute-start.97
  792.9 11.4 %collective-permute-start.85 = (bf16[528,512]{1,0:T(8,128)(2,1)S(1)}, bf16[528,512]{1,0:T(8,128)(2,1)S(1)}, u32[]{:S(2)}, u32[]{:S(2)}) collective-permute-start(bf16[528,512]{1,0:T(8,128)(2,1)S(1)} %get-tuple-element.172), channel_id=1, source_target_pairs={{0,1},{1,2},{4,5},{5,6},{8,9},{9,10},{12,13},{13,14},{16,17},{17,1... | collective-permute-start | bytes 1622024 | tf_op jit(solution)/shard_map/ppermute | solution.py:754
  813.3 9.8 collective-permute-start.98
  886.2 9.5 convert_add_fusion
  906.7 10.0 linear_backward.2
  942.4 11.5 %collective-permute-start.114 = (bf16[528,512]{1,0:T(8,128)(2,1)}, bf16[528,512]{1,0:T(8,128)(2,1)}, u32[]{:S(2)}, u32[]{:S(2)}) collective-permute-start(bf16[528,512]{1,0:T(8,128)(2,1)} %get-tuple-element.182), channel_id=1, source_target_pairs={{0,1},{4,5},{8,9},{12,13},{16,17},{20,21},{24,25},{28,29}} | collective-permute-start | bytes 1622024 | tf_op jit(solution)/shard_map/ppermute | solution.py:754
  1027.1 13.6 %psum.84 = f32[1542]{0:T(1024)S(1)} all-reduce(f32[1542]{0:T(1024)S(1)} %concatenate.85), channel_id=1, replica_groups=mesh['dp'=8,'mp'=4] {'dp'}, use_global_device_ids=true, to_apply=%region_31.32 | all-reduce | flops 1542 | bytes 12336 | tf_op jit(solution)/shard_map/psum | solution.py:1055
  1067.9 34.8 %all-reduce.22.cloned.1.call-done = (bf16[2048,64]{0,1:T(8,128)(2,1)}, bf16[2048,64]{0,1:T(8,128)(2,1)}, bf16[2048,512]{1,0:T(8,128)(2,1)}, bf16[512,2048]{1,0:T(8,128)(2,1)}) async-done(((bf16[2048,64]{0,1:T(8,128)(2,1)}, bf16[2048,64]{0,1:T(8,128)(2,1)}, bf16[2048,512]{1,0:T(8,128)(2,1)}, bf16[512,2048]{1,0:T(8,128)(2,1)}), (bf16[2048,64]{0,1:T(8,128)(2,1)}, bf16[2048,64]{0,1:T(8,128)(2,1)}, ...) | async-done | bytes 4718608 | tf_op jit(solution)/shard_map/psum | solution.py:777
  (959 shorter events, 768.4 us)
Async XLA Ops:
  7.2 269.0 %all-gather.2.cloned.1.call-start = ((), (), s32[]{:S(2)}) async-start(), calls=%async_computation.2 | async-start | bytes 5242880 | tf_op jit(solution)/shard_map/all_gather | solution.py:903
  88.6 464.5 %reduce-scatter.3.cloned.1.call-start = ((), (), s32[]{:S(2)}) async-start(), calls=%async_computation.3 | async-start | bytes 2621440 | tf_op jit(solution)/shard_map/reduce_scatter | solution.py:968
  100.1 35.1 %collective-permute-start.7 = (bf16[512,512]{1,0:T(8,128)(2,1)}, bf16[512,512]{1,0:T(8,128)(2,1)}, u32[]{:S(2)}, u32[]{:S(2)}) collective-permute-start(bf16[512,512]{1,0:T(8,128)(2,1)} %get-tuple-element.200), channel_id=1, source_target_pairs={{0,1},{1,2},{4,5},{5,6},{8,9},{9,10},{12,13},{13,14},{16,17},{17,1... | collective-permute-start | bytes 1572872 | tf_op jit(solution)/shard_map/ppermute | solution.py:754
  129.1 40.3 %collective-permute-start.11 = (bf16[512,512]{1,0:T(8,128)(2,1)}, bf16[512,512]{1,0:T(8,128)(2,1)S(1)}, u32[]{:S(2)}, u32[]{:S(2)}) collective-permute-start(bf16[512,512]{1,0:T(8,128)(2,1)} %get-tuple-element.199), channel_id=1, source_target_pairs={{1,0},{2,1},{3,2},{5,4},{6,5},{7,6},{9,8},{10,9},{11,10},{13,12},{... | collective-permute-start | bytes 1572872 | tf_op jit(solution)/shard_map/ppermute | solution.py:755
  130.6 57.1 %collective-permute-start.36 = (bf16[512,512]{1,0:T(8,128)(2,1)}, bf16[512,512]{1,0:T(8,128)(2,1)S(1)}, u32[]{:S(2)}, u32[]{:S(2)}) collective-permute-start(bf16[512,512]{1,0:T(8,128)(2,1)} %get-tuple-element.206), channel_id=1, source_target_pairs={{0,1},{4,5},{8,9},{12,13},{16,17},{20,21},{24,25},{28,29}} | collective-permute-start | bytes 1572872 | tf_op jit(solution)/shard_map/ppermute | solution.py:754
  136.5 43.5 %collective-permute-start.8 = (bf16[512,512]{1,0:T(8,128)(2,1)S(1)}, bf16[512,512]{1,0:T(8,128)(2,1)S(1)}, u32[]{:S(2)}, u32[]{:S(2)}) collective-permute-start(bf16[512,512]{1,0:T(8,128)(2,1)S(1)} %bitcast_add_fusion.39), channel_id=1, source_target_pairs={{0,1},{1,2},{2,3},{4,5},{5,6},{6,7},{8,9},{9,10},{10,11},{12,13},{... | collective-permute-start | bytes 1572872 | tf_op jit(solution)/shard_map/ppermute | solution.py:754
  146.0 41.8 %collective-permute-start.40 = (bf16[512,512]{1,0:T(8,128)(2,1)S(1)}, bf16[512,512]{1,0:T(8,128)(2,1)S(1)}, u32[]{:S(2)}, u32[]{:S(2)}) collective-permute-start(bf16[512,512]{1,0:T(8,128)(2,1)S(1)} %bitcast_add_fusion.28), channel_id=1, source_target_pairs={{2,1},{3,2},{6,5},{7,6},{10,9},{11,10},{14,13},{15,14},{18,17},{19... | collective-permute-start | bytes 1572872 | tf_op jit(solution)/shard_map/ppermute | solution.py:755
  187.9 39.8 %collective-permute-start.37 = (bf16[512,512]{1,0:T(8,128)(2,1)S(1)}, bf16[512,512]{1,0:T(8,128)(2,1)S(1)}, u32[]{:S(2)}, u32[]{:S(2)}) collective-permute-start(bf16[512,512]{1,0:T(8,128)(2,1)S(1)} %get-tuple-element.204), channel_id=1, source_target_pairs={{0,1},{1,2},{4,5},{5,6},{8,9},{9,10},{12,13},{13,14},{16,17},{17,1... | collective-permute-start | bytes 1572872 | tf_op jit(solution)/shard_map/ppermute | solution.py:754
  197.4 34.8 %collective-permute-start.16 = (bf16[512,512]{1,0:T(8,128)(2,1)S(1)}, bf16[512,512]{1,0:T(8,128)(2,1)S(1)}, u32[]{:S(2)}, u32[]{:S(2)}) collective-permute-start(bf16[512,512]{1,0:T(8,128)(2,1)S(1)} %collective-permute-done.15.refs_3_), channel_id=1, source_target_pairs={{1,0},{2,1},{5,4},{6,5},{9,8},{10,9},{13,12},{14,13},{17,16},{18,1... | collective-permute-start | bytes 1572872 | tf_op jit(solution)/shard_map/ppermute | solution.py:730
  423.1 132.4 %reduce-scatter.5.cloned.1.call-start = ((), (), s32[]{:S(2)}) async-start(), calls=%async_computation.4 | async-start | bytes 2621440 | tf_op jit(solution)/shard_map/reduce_scatter | solution.py:968
  445.1 33.8 %collective-permute-start.59 = (bf16[512,512]{1,0:T(8,128)(2,1)}, bf16[512,512]{1,0:T(8,128)(2,1)S(1)}, u32[]{:S(2)}, u32[]{:S(2)}) collective-permute-start(bf16[512,512]{1,0:T(8,128)(2,1)} %collective-permute-done.58.refs_4_), channel_id=1, source_target_pairs={{1,0},{5,4},{9,8},{13,12},{17,16},{21,20},{25,24},{29,28}} | collective-permute-start | bytes 1572872 | tf_op jit(solution)/shard_map/ppermute | solution.py:730
  446.4 32.5 %collective-permute-start.56 = (bf16[512,512]{1,0:T(8,128)(2,1)}, bf16[512,512]{1,0:T(8,128)(2,1)S(1)}, u32[]{:S(2)}, u32[]{:S(2)}) collective-permute-start(bf16[512,512]{1,0:T(8,128)(2,1)} %collective-permute-done.55.refs_1_), channel_id=1, source_target_pairs={{2,3},{6,7},{10,11},{14,15},{18,19},{22,23},{26,27},{30,31}} | collective-permute-start | bytes 1572872 | tf_op jit(solution)/shard_map/ppermute | solution.py:728
  594.1 292.1 %all-reduce.16.cloned.1.call-start = ((), (), s32[]{:S(2)}) async-start(), calls=%async_computation.5 | async-start | bytes 11534336 | tf_op jit(solution)/shard_map/psum | solution.py:777
  602.7 48.0 %collective-permute-start.77 = (bf16[528,512]{1,0:T(8,128)(2,1)S(1)}, bf16[528,512]{1,0:T(8,128)(2,1)S(1)}, u32[]{:S(2)}, u32[]{:S(2)}) collective-permute-start(bf16[528,512]{1,0:T(8,128)(2,1)S(1)} %get-tuple-element.187), channel_id=1, source_target_pairs={{1,0},{2,1},{3,2},{5,4},{6,5},{7,6},{9,8},{10,9},{11,10},{13,12},{... | collective-permute-start | bytes 1622024 | tf_op jit(solution)/shard_map/ppermute | solution.py:755
  610.1 33.8 %collective-permute-start.61 = (bf16[528,512]{1,0:T(8,128)(2,1)S(1)}, bf16[528,512]{1,0:T(8,128)(2,1)S(1)}, u32[]{:S(2)}, u32[]{:S(2)}) collective-permute-start(bf16[528,512]{1,0:T(8,128)(2,1)S(1)} %get-tuple-element.176), channel_id=1, source_target_pairs={{0,1},{1,2},{4,5},{5,6},{8,9},{9,10},{12,13},{13,14},{16,17},{17,1... | collective-permute-start | bytes 1622024 | tf_op jit(solution)/shard_map/ppermute | solution.py:754
  653.6 32.7 %collective-permute-start.81 = (bf16[512,512]{1,0:T(8,128)(2,1)}, bf16[512,512]{1,0:T(8,128)(2,1)}, u32[]{:S(2)}, u32[]{:S(2)}) collective-permute-start(bf16[512,512]{1,0:T(8,128)(2,1)} %broadcast_add_fusion.1.own_ref), channel_id=1, source_target_pairs={{1,0},{2,1},{3,2},{5,4},{6,5},{7,6},{9,8},{10,9},{11,10},{13,12},{... | collective-permute-start | bytes 1572872 | tf_op jit(solution)/shard_map/ppermute | solution.py:730
  655.0 32.5 %collective-permute-start.78 = (bf16[512,512]{1,0:T(8,128)(2,1)}, bf16[512,512]{1,0:T(8,128)(2,1)}, u32[]{:S(2)}, u32[]{:S(2)}) collective-permute-start(bf16[512,512]{1,0:T(8,128)(2,1)} %broadcast_add_fusion.1.own_ref), channel_id=1, source_target_pairs={{0,1},{1,2},{2,3},{4,5},{5,6},{6,7},{8,9},{9,10},{10,11},{12,13},{... | collective-permute-start | bytes 1572872 | tf_op jit(solution)/shard_map/ppermute | solution.py:728
  671.4 291.6 %all-reduce.18.cloned.1.call-start = ((), (), s32[]{:S(2)}) async-start(), calls=%async_computation.6 | async-start | bytes 23068672 | tf_op jit(solution)/shard_map/psum | solution.py:777
  811.9 43.9 %collective-permute-start.89 = (bf16[528,512]{1,0:T(8,128)(2,1)}, bf16[528,512]{1,0:T(8,128)(2,1)}, u32[]{:S(2)}, u32[]{:S(2)}) collective-permute-start(bf16[528,512]{1,0:T(8,128)(2,1)} %get-tuple-element.171), channel_id=1, source_target_pairs={{1,0},{2,1},{3,2},{5,4},{6,5},{7,6},{9,8},{10,9},{11,10},{13,12},{... | collective-permute-start | bytes 1622024 | tf_op jit(solution)/shard_map/ppermute | solution.py:755
  837.8 32.6 %collective-permute-start.105 = (bf16[512,512]{1,0:T(8,128)(2,1)}, bf16[512,512]{1,0:T(8,128)(2,1)}, u32[]{:S(2)}, u32[]{:S(2)}) collective-permute-start(bf16[512,512]{1,0:T(8,128)(2,1)} %get-tuple-element.125.own_ref), channel_id=1, source_target_pairs={{1,0},{2,1},{3,2},{5,4},{6,5},{7,6},{9,8},{10,9},{11,10},{13,12},{... | collective-permute-start | bytes 1572872 | tf_op jit(solution)/shard_map/ppermute | solution.py:730
  853.2 202.5 %all-reduce.20.cloned.1.call-start = ((), (), s32[]{:S(2)}) async-start(), calls=%async_computation.7 | async-start | bytes 16777216 | tf_op jit(solution)/shard_map/psum | solution.py:777
  876.9 225.8 %all-reduce.22.cloned.1.call-start = ((), (), s32[]{:S(2)}) async-start(), calls=%async_computation.8 | async-start | bytes 9437184 | tf_op jit(solution)/shard_map/psum | solution.py:777
  940.9 45.8 %collective-permute-start.117 = (bf16[528,512]{1,0:T(8,128)(2,1)}, bf16[528,512]{1,0:T(8,128)(2,1)}, u32[]{:S(2)}, u32[]{:S(2)}) collective-permute-start(bf16[528,512]{1,0:T(8,128)(2,1)} %get-tuple-element.181), channel_id=1, source_target_pairs={{3,2},{7,6},{11,10},{15,14},{19,18},{23,22},{27,26},{31,30}} | collective-permute-start | bytes 1622024 | tf_op jit(solution)/shard_map/ppermute | solution.py:755
  942.4 54.8 %collective-permute-start.114 = (bf16[528,512]{1,0:T(8,128)(2,1)}, bf16[528,512]{1,0:T(8,128)(2,1)}, u32[]{:S(2)}, u32[]{:S(2)}) collective-permute-start(bf16[528,512]{1,0:T(8,128)(2,1)} %get-tuple-element.182), channel_id=1, source_target_pairs={{0,1},{4,5},{8,9},{12,13},{16,17},{20,21},{24,25},{28,29}} | collective-permute-start | bytes 1622024 | tf_op jit(solution)/shard_map/ppermute | solution.py:754
  (337 other events, 4130.2 us)
Sparse Core Ops, SparseCore 0:
  88.7 136.6 all-gather.1
  423.2 57.1 reduce-scatter.2
  502.9 47.6 reduce-scatter.4
  598.5 102.7 all-reduce.15
  713.3 163.9 all-reduce.17
  882.3 127.6 all-reduce.19
  1015.3 87.3 all-reduce.21
